TPU v7x, 256 devices: a whole 4x4x8 slice. The times are simulated.
256 devices in a mesh: dp: 64 (over z, x, core), mp: 4 (over y).
Axes of the slice: x: 4, y: 4, z: 8, core: 2. Of those that a mesh axis runs over, the one named last changes fastest.
Arguments:
- tokens: bfloat16 [32768, 8192], P('dp', 'mp'), may hold values from -6 to 6
- out_grads: bfloat16 [32768, 28672], P('dp', 'mp'), may hold values from -6 to 6
- test_matrix: bfloat16 [28672, 80], P('mp'), may hold values from -0.03125 to 0.03125
- slot_counts: int32 [64], P('dp'), may hold values from 1 to 512, 16384 in all
Outputs:
- adapter_down: float32 [8192, 80], P(('mp', 'dp'))
- adapter_up: float32 [28672, 80], P(('mp', 'dp'))
Inputs may be any that keep to these rules, and one draw needn't show every extreme that they name: `slot_counts`: live slots of each block of 512 rows come first; some block is full.
All inputs are finite; a program needn't handle non-finite values.
Results may differ from a plain program's by a relative error of at most 0.009.
Values may be sent and summed in bfloat16 or wider, within the bound.
No kernel may reach another device: no remote copies, remote signals or barrier semaphores. Data moves between devices by JAX's collectives and lax.ppermute only.
A program may use at most 64 MiB of HBM per device.

v0:
```python
import jax
import jax.numpy as jnp
from jax import lax
from jax.sharding import PartitionSpec as P

D = 8192
FF = 28672


def token_contract(left, right):
    return lax.dot_general(
        left, right, (((0,), (0,)), ((), ())), preferred_element_type=jnp.float32
    )


def orthonormal(ranged_rows, gram):
    lower = jnp.linalg.cholesky(gram)
    return lax.linalg.triangular_solve(
        lower, ranged_rows, left_side=False, lower=True, transpose_a=True
    )


def local(tokens, out_grads, test_matrix, slot_counts):
    tok_rows = tokens.shape[0]
    live_rows = slot_counts[0]
    kept_mask = jnp.arange(tok_rows, dtype=jnp.int32) < live_rows
    masked = jnp.where(kept_mask[:, None], tokens, jnp.zeros_like(tokens))
    sketch_part = jnp.dot(out_grads, test_matrix, preferred_element_type=jnp.float32)
    sketch = lax.psum(sketch_part, "mp").astype(jnp.bfloat16)
    first_part = token_contract(masked, sketch)
    first_sum, live_total = lax.psum((first_part, slot_counts.astype(jnp.float32)), "dp")
    inv_root = lax.rsqrt(live_total[0])
    ranged = (inv_root * first_sum).astype(jnp.bfloat16)
    back_part = jnp.dot(masked, ranged, preferred_element_type=jnp.float32)
    back = (lax.psum(back_part, "mp") * D ** (-0.5)).astype(jnp.bfloat16)
    trans_part = token_contract(out_grads, back)
    transposed = (inv_root * lax.psum(trans_part, "dp")).astype(jnp.bfloat16)
    again_part = jnp.dot(out_grads, transposed, preferred_element_type=jnp.float32)
    again = (lax.psum(again_part, "mp") * FF ** (-0.5)).astype(jnp.bfloat16)
    columns = masked
    own_range = inv_root * lax.psum_scatter(
        token_contract(columns, again), "dp", scatter_dimension=0, tiled=True
    )
    local_gram = jnp.dot(own_range.T, own_range, precision=lax.Precision.HIGHEST)
    gram = lax.psum(local_gram, ("dp", "mp"))
    own_basis = orthonormal(own_range, gram)
    columns = masked
    basis_part = jnp.dot(
        columns,
        lax.all_gather(own_basis.astype(jnp.bfloat16), "dp", axis=0, tiled=True),
        preferred_element_type=jnp.float32,
    )
    projected = lax.psum(basis_part, "mp").astype(jnp.bfloat16)
    columns = out_grads
    adapter_up = inv_root * lax.psum_scatter(
        token_contract(columns, projected), "dp", scatter_dimension=0, tiled=True
    )
    adapter_down = own_basis * D**0.5
    return (adapter_down, adapter_up)


def solution(mesh):
    placed = (P("dp", "mp"), P("dp", "mp"), P("mp", None), P("dp"))
    return jax.shard_map(
        local,
        mesh=mesh,
        in_specs=placed,
        out_specs=(P(("mp", "dp"), None), P(("mp", "dp"), None)),
        check_vma=False,
    )
```

profile of v0, /device:TPU:1, one launch (start us, length us, event | category | flops | bytes accessed | tf_op | source)
XLA Modules:
  0.0 1018.7 jit_solution(17242075960471718213)
XLA Ops:
  7.2 1.2 copy-done
  8.4 5.5 fusion.24
  13.9 15.9 %all-reduce.18 = bf16[512,80]{0,1:T(8,128)(2,1)S(1)} all-reduce(f32[512,80]{0,1:T(8,128)S(1)} %fusion.24), channel_id=1, replica_groups=mesh['dp'=64,'mp'=4] {'mp'}, use_global_device_ids=true, to_apply=%region_1.2 | all-reduce | flops 40960 | bytes 245760 | tf_op jit(solution)/shard_map/psum | solution.py:29
  30.5 1.4 fusion.9
  32.0 131.5 %psum.56 = f32[1]{0:T(128)} all-reduce(f32[1]{0:T(128)S(6)} %convert_element_type.24), channel_id=1, replica_groups=mesh['dp'=64,'mp'=4] {'dp'}, use_global_device_ids=true, to_apply=%region_0.1 | all-reduce | flops 1 | bytes 8 | tf_op jit(solution)/shard_map/psum | solution.py:31
  164.2 54.4 %all-reduce.9.cloned.1.call-done = f32[2048,80]{0,1:T(8,128)} async-done(((f32[2048,80]{0,1:T(8,128)}), f32[2048,80]{0,1:T(8,128)}) %all-reduce.9.cloned.1.call-update) | async-done | bytes 655376 | tf_op jit(solution)/shard_map/psum | solution.py:31
  218.5 2.6 fusion.3
  221.2 43.1 %all-reduce.11.cloned.1.call-done = f32[512,80]{0,1:T(8,128)} async-done(((f32[512,80]{0,1:T(8,128)}), f32[512,80]{0,1:T(8,128)}) %all-reduce.11.cloned.1.call-update) | async-done | bytes 163856 | tf_op jit(solution)/shard_map/psum | solution.py:35
  264.3 5.9 convolution_bitcast_fusion.1
  270.3 191.3 %all-reduce.13.cloned.1.call-done = f32[7168,80]{0,1:T(8,128)} async-done(((f32[7168,80]{0,1:T(8,128)}), f32[7168,80]{0,1:T(8,128)}) %all-reduce.13.cloned.1.call-update) | async-done | bytes 2293776 | tf_op jit(solution)/shard_map/psum | solution.py:37
  461.7 6.8 fusion.2
  468.5 44.9 %all-reduce.15.cloned.1.call-done = f32[512,80]{0,1:T(8,128)} async-done(((f32[512,80]{0,1:T(8,128)}), f32[512,80]{0,1:T(8,128)}) %all-reduce.15.cloned.1.call-update) | async-done | bytes 163856 | tf_op jit(solution)/shard_map/psum | solution.py:39
  513.4 2.8 fusion.5
  516.3 138.0 %reduce-scatter.3.cloned.1.call-done = f32[32,80]{1,0:T(8,128)} async-done(((f32[2048,80]{1,0:T(8,128)}), f32[32,80]{1,0:T(8,128)}) %reduce-scatter.3.cloned.1.call-update) | async-done | bytes 10256 | tf_op jit(solution)/shard_map/reduce_scatter | solution.py:41
  654.3 1.0 fusion.16
  655.3 80.2 %psum.62 = f32[80,80]{0,1:T(8,128)S(1)} all-reduce(f32[80,80]{0,1:T(8,128)S(1)} %fusion.16), channel_id=1, replica_groups=mesh['dp'=64,'mp'=4] {'dp','mp'}, use_global_device_ids=true, to_apply=%region_7.8 | all-reduce | flops 6400 | bytes 51200 | tf_op jit(solution)/shard_map/psum | solution.py:45
  735.6 7.3 cholesky.16
  744.2 6.1 custom-call.6
  750.4 1.5 fusion.23
  751.9 50.2 %all_gather.3 = bf16[2048,80]{1,0:T(8,128)(2,1)S(1)} all-gather(bf16[32,80]{1,0:T(8,128)(2,1)S(1)} %get-tuple-element.2), channel_id=1, replica_groups=mesh['dp'=64,'mp'=4] {'dp'}, dimensions={0}, use_global_device_ids=true | all-gather | bytes 332800 | tf_op jit(solution)/shard_map/all_gather | solution.py:50
  802.9 13.0 %all-reduce.19 = bf16[512,80]{0,1:T(8,128)(2,1)S(1)} all-reduce(f32[512,80]{0,1:T(8,128)S(1)} %fusion.22), channel_id=1, replica_groups=mesh['dp'=64,'mp'=4] {'mp'}, use_global_device_ids=true, to_apply=%region_10.11 | all-reduce | flops 40960 | bytes 245760 | tf_op jit(solution)/shard_map/psum | solution.py:53
  815.9 5.9 convolution_bitcast_fusion
  823.7 186.6 %all-reduce.17.cloned.1.call-done = f32[7168,80]{0,1:T(8,128)} async-done(((f32[7168,80]{0,1:T(8,128)}), f32[7168,80]{0,1:T(8,128)}) %all-reduce.17.cloned.1.call-update) | async-done | bytes 2293776
  1010.3 1.6 dynamic-slice_multiply_fusion
  (25 shorter events, 3.9 us)
Async XLA Ops:
  7.2 1.3 copy-start
  7.2 23.3 %copy-start.1 = (bf16[512,2048]{1,0:T(8,128)(2,1)S(1)}, bf16[512,2048]{1,0:T(8,128)(2,1)}, u32[]{:S(2)}) copy-start(bf16[512,2048]{1,0:T(8,128)(2,1)} %param.4) | copy-start | bytes 6291460
  7.2 211.4 %all-reduce.9.cloned.1.call-start = ((), (), s32[]{:S(2)}) async-start(), calls=%async_computation.1 | async-start | bytes 1310720 | tf_op jit(solution)/shard_map/psum | solution.py:31
  31.9 232.4 %all-reduce.11.cloned.1.call-start = ((), (), s32[]{:S(2)}) async-start(), calls=%async_computation.2 | async-start | bytes 327680 | tf_op jit(solution)/shard_map/psum | solution.py:35
  221.2 240.5 %all-reduce.13.cloned.1.call-start = ((), (), s32[]{:S(2)}) async-start(), calls=%async_computation.3 | async-start | bytes 4587520 | tf_op jit(solution)/shard_map/psum | solution.py:37
  270.3 243.1 %all-reduce.15.cloned.1.call-start = ((), (), s32[]{:S(2)}) async-start(), calls=%async_computation.4 | async-start | bytes 327680 | tf_op jit(solution)/shard_map/psum | solution.py:39
  468.5 185.8 %reduce-scatter.3.cloned.1.call-start = ((), (), s32[]{:S(2)}) async-start(), calls=%async_computation.5 | async-start | bytes 1064960 | tf_op jit(solution)/shard_map/reduce_scatter | solution.py:41
  516.2 494.1 %all-reduce.17.cloned.1.call-start = ((), (), s32[]{:S(2)}) async-start(), calls=%async_computation.6 | async-start | bytes 4587520
  821.7 0.7 copy-start.2
Sparse Core Ops, SparseCore 0:
  32.1 186.4 all-reduce.8
  221.3 42.9 all-reduce.10
  270.4 191.2 all-reduce.12
  468.6 44.7 all-reduce.14
  517.7 136.5 reduce-scatter.2
  821.9 188.3 all-reduce.16
where the time goes:
time: 1020 us
  waiting for transfers between devices  658 us (65%)
  blocking collectives  291 us (29%)
  matrix products  34.2 us (3%)
  other arithmetic  16.4 us (2%)
  between operations  16.2 us (2%)
    psum x1, waiting for transfers between devices, local(): transposed = (inv_root * lax.psum(trans_part, 'dp')).astype(jnp.bfloat16)  191 us
    unnamed x7, waiting for transfers between devices  187 us
    reduce_scatter x1, waiting for transfers between devices, local(): lax.psum_scatter(token_contract(columns, again), 'dp', scatter_dimension=...  138 us
    psum x1, blocking collectives, local(): lax.psum((first_part, slot_counts.astype(jnp.float32)), 'dp')  131 us
    psum x1, blocking collectives, local(): gram = lax.psum(local_gram, ('dp', 'mp'))  80.2 us
    psum x1, waiting for transfers between devices, local(): lax.psum((first_part, slot_counts.astype(jnp.float32)), 'dp')  54.4 us
    all_gather x1, blocking collectives, local(): lax.all_gather(own_basis.astype(jnp.bfloat16), 'dp', axis=0, tiled=True)  50.2 us
    psum x1, waiting for transfers between devices, local(): again = (lax.psum(again_part, 'mp') * FF ** (-0.5)).astype(jnp.bfloat16)  44.9 us
  transfers between devices with their start and end apart: 6, of which 6 were waited for; matrix products, arithmetic and copies ran while one was open for 0% of the time, Pallas kernels for 0%

commit v1 on v0

v1 whole, which is shorter than its diff:
```python
import jax
import jax.numpy as jnp
from jax import lax
from jax.sharding import Mesh, PartitionSpec as P

D = 8192
FF = 28672
K = 80
LIVE = 16384
F32 = jnp.float32
BF16 = jnp.bfloat16


def dot(left, right, contract):
    return lax.dot_general(left, right, (contract, ((), ())), preferred_element_type=F32)


def along_features(small, big):
    return dot(small, big, ((1,), (1,)))


def along_tokens(small, big):
    return dot(small, big, ((1,), (0,)))


def shifted(value, axis, size, step):
    return lax.ppermute(value, axis, [(i, (i + step) % size) for i in range(size)])


def y_sum(part):
    sent = part.astype(BF16)
    came = [shifted(sent, "y", 4, step) for step in (1, 2, 3)]
    total = sent.astype(F32)
    for piece in came:
        total = total + piece.astype(F32)
    return total


def to_tiles(array):
    rows, cols = array.shape
    tiles = array.reshape(rows // 8, 8, cols // 128, 128).transpose(0, 2, 1, 3)
    return tiles.reshape(-1, 8, 128)


def from_tiles(tiles, rows, cols):
    split = tiles.reshape(rows // 8, cols // 128, 8, 128).transpose(0, 2, 1, 3)
    return split.reshape(rows, cols)


def exchange(pieces, axes):
    return lax.all_to_all(pieces, axes, 0, 0, tiled=True)


def spread(piece, axes, count):
    return exchange(jnp.broadcast_to(piece[None], (count,) + piece.shape), axes)


def dp_sum_small(part, scale):
    rows, cols = part.shape
    pieces = to_tiles(part.astype(BF16)).reshape(8, -1, 8, 128)
    mine = exchange(pieces, ("x", "c")).astype(F32).sum(0).astype(BF16)
    mine = (spread(mine, "z", 8).astype(F32).sum(0) * scale).astype(BF16)
    whole = spread(mine, ("x", "c"), 8)
    return from_tiles(whole, rows, cols)


def core_scatter(halves):
    core = lax.axis_index("c")
    kept = lax.dynamic_index_in_dim(halves, core, 0, keepdims=False)
    sent = lax.dynamic_index_in_dim(halves, 1 - core, 0, keepdims=False)
    came = shifted(sent, "c", 2, 1)
    return (kept.astype(F32) + came.astype(F32)).astype(BF16)


def core_gather(half):
    other = shifted(half, "c", 2, 1)
    first = lax.axis_index("c") == 0
    return jnp.stack([jnp.where(first, half, other), jnp.where(first, other, half)])


def dp_sum_big(part, scale):
    rows, cols = part.shape
    tiles = to_tiles(part.astype(BF16))
    count = tiles.shape[0]
    per = -(-count // 64)
    tiles = jnp.pad(tiles, ((0, 64 * per - count), (0, 0), (0, 0)))
    half = core_scatter(tiles.reshape(2, 32, per, 8, 128))
    mine = (exchange(half, ("z", "x")).astype(F32).sum(0) * scale).astype(BF16)
    whole = core_gather(spread(mine, ("z", "x"), 32))
    return from_tiles(whole.reshape(64 * per, 8, 128)[:count], rows, cols)


def local(tokens, out_grads, test_matrix, slot_counts):
    rows = tokens.shape[0]
    live_rows = slot_counts[0]
    kept = (jnp.arange(rows, dtype=jnp.int32) < live_rows)[None, :]
    scale = LIVE ** -0.5

    def masked(value):
        return jnp.where(kept, value, 0.0).astype(BF16)

    sketch = masked(y_sum(dot(test_matrix, out_grads, ((0,), (1,)))))
    ranged = dp_sum_small(along_tokens(sketch, tokens), scale)
    back = masked(y_sum(along_features(ranged, tokens)) * D ** -0.5)
    transposed = dp_sum_big(along_tokens(back, out_grads), scale)
    again = masked(y_sum(along_features(transposed, out_grads)) * FF ** -0.5)
    whole_range = dp_sum_small(along_tokens(again, tokens), scale)

    gram_part = along_features(whole_range, whole_range)
    gram = gram_part
    for step in (1, 2, 3):
        gram = gram + shifted(gram_part, "y", 4, step)
    lower = jnp.linalg.cholesky(gram)
    inverse = lax.linalg.triangular_solve(
        lower, jnp.eye(K, dtype=F32), left_side=True, lower=True
    )

    projected = masked(y_sum(along_features(whole_range, tokens)))
    up_part = along_tokens(projected, out_grads).astype(BF16)
    owned = up_part.shape[1] // 64
    up_part = up_part.reshape(K, 32, 2, owned).transpose(2, 1, 0, 3)
    digits = jnp.stack([live_rows // 32, live_rows % 32]).astype(BF16)
    digits = jnp.broadcast_to(digits, (2, 32, K, 2))
    up_part = jnp.concatenate([up_part, digits], axis=3)
    up_sum = exchange(core_scatter(up_part), ("z", "x")).astype(F32).sum(0)
    live_total = 32.0 * up_sum[0, owned] + up_sum[0, owned + 1]
    inv_root = lax.rsqrt(live_total)
    adapter_up = inv_root * jnp.dot(
        inverse, up_sum[:, :owned], precision=lax.Precision.HIGHEST
    ).T

    place = lax.axis_index(("z", "x", "c"))
    width = whole_range.shape[1] // 64
    own = lax.dynamic_slice_in_dim(whole_range, place * width, width, 1).astype(F32)
    adapter_down = jnp.dot(inverse, own, precision=lax.Precision.HIGHEST).T * D ** 0.5
    return adapter_down, adapter_up


def solution(mesh):
    split = Mesh(mesh.devices.reshape(8, 4, 2, 4), ("z", "x", "c", "y"))
    dp = ("z", "x", "c")
    placed = (P(dp, "y"), P(dp, "y"), P("y", None), P(dp))
    return jax.shard_map(
        local,
        mesh=split,
        in_specs=placed,
        out_specs=(P(("y",) + dp, None), P(("y",) + dp, None)),
        check_vma=False,
    )
```

time: 1020 us -> 242 us (0.24)
  waiting for transfers between devices: 658 us -> 37.8 us
  blocking collectives: 291 us -> 114 us
  starting transfers between devices: 0.25 us -> 29.8 us
  between operations: 16.2 us -> 2.84 us
    psum x4 -> x0, waiting for transfers between devices: 334 us -> none  [the longest x1 191 us: local(): transposed = (inv_root * lax.psum(trans_part, 'dp')).astype(jnp.bfloat16)]
    psum x4 -> x0, blocking collectives: 241 us -> none  [the longest x1 131 us: local(): lax.psum((first_part, slot_counts.astype(jnp.float32)), 'dp')]
    unnamed x7 -> x0, waiting for transfers between devices: 187 us -> none
    reduce_scatter x1 -> x0, waiting for transfers between devices: 138 us -> none  [local(): lax.psum_scatter(token_contract(columns, again), 'dp', scatter_dimension=...]
    all_to_all x0 -> x7, blocking collectives: none -> 114 us  [exchange(): return lax.all_to_all(pieces, axes, 0, 0, tiled=True)]
    all_gather x1 -> x0, blocking collectives: 50.2 us -> none  [local(): lax.all_gather(own_basis.astype(jnp.bfloat16), 'dp', axis=0, tiled=True)]
    ppermute x0 -> x18, waiting for transfers between devices: none -> 27.6 us  [shifted(): lax.ppermute(value, axis, [(i, (i + step) % size) for i in range(size)])]
    ppermute x0 -> x18, starting transfers between devices: none -> 20.9 us  [shifted(): lax.ppermute(value, axis, [(i, (i + step) % size) for i in range(size)])]
  transfers between devices with their start and end apart: 6 -> 20, of which waited for: 6 -> 17; matrix products, arithmetic and copies ran while one was open for 0% -> 7% of each run, Pallas kernels for 0% -> 0%
where the time goes in v1:
time: 242 us; the launch traced here: 240 us
  blocking collectives  114 us (47%)
  waiting for transfers between devices  37.8 us (16%)
  starting transfers between devices  29.8 us (12%)
  matrix products  26 us (11%)
  other arithmetic  19.2 us (8%)
  local copies, waits for them, and re-layouts  10.5 us (4%)
  between operations  2.84 us (1%)
    all_to_all x7, blocking collectives, exchange(): return lax.all_to_all(pieces, axes, 0, 0, tiled=True)  114 us
    ppermute x18, waiting for transfers between devices, shifted(): lax.ppermute(value, axis, [(i, (i + step) % size) for i in range(size)])  27.6 us
    dot_general x9, matrix products, dot(): lax.dot_general(left, right, (contract, ((), ())), preferred_element_type...  24.1 us
    ppermute x18, starting transfers between devices, shifted(): lax.ppermute(value, axis, [(i, (i + step) % size) for i in range(size)])  20.9 us
    all_to_all x2, waiting for transfers between devices, exchange(): return lax.all_to_all(pieces, axes, 0, 0, tiled=True)  10.2 us
    all_to_all x2, starting transfers between devices, exchange(): return lax.all_to_all(pieces, axes, 0, 0, tiled=True)  8.83 us
    another operation x3, other arithmetic, local(): lower = jnp.linalg.cholesky(gram)  7.98 us
    another operation x2, other arithmetic, local(): lax.linalg.triangular_solve(lower, jnp.eye(K, dtype=F32), left_side=True,...  6.78 us
  transfers between devices with their start and end apart: 20, of which 17 were waited for; matrix products, arithmetic and copies ran while one was open for 7% of the time, Pallas kernels for 0%

profile of v1, /device:TPU:1, one launch (start us, length us, event | category | flops | bytes accessed | tf_op | source)
XLA Modules:
  0.0 240.5 jit_solution(11479179408382911519)
XLA Ops:
  0.6 5.9 %convolution_convert_fusion.7 = bf16[80,512]{1,0:T(8,128)(2,1)S(1)} fusion(bf16[7168,80]{0,1:T(8,128)(2,1)} %param.6, bf16[512,7168]{1,0:T(8,128)(2,1)} %param.5), kind=kOutput, calls=%fused_computation.16 | convolution fusion | flops 587243520 | bytes 8568832 | tf_op jit(solution)/shard_map/dot_general | solution.py:15
  6.6 3.6 %collective-permute-start.2 = (bf16[80,512]{1,0:T(8,128)(2,1)S(1)}, bf16[80,512]{1,0:T(8,128)(2,1)S(1)}, u32[]{:S(2)}, u32[]{:S(2)}) collective-permute-start(bf16[80,512]{1,0:T(8,128)(2,1)S(1)} %convolution_convert_fusion.7), channel_id=1, source_target_pairs={{0,3},{1,0},{2,1},{3,2},{4,7},{5,4},{6,5},{7,6},{8,11},{9,8},{10,9... | collective-permute-start | bytes 245768 | tf_op jit(solution)/shard_map/ppermute | solution.py:27
  11.9 3.2 %collective-permute-done.1 = bf16[80,512]{1,0:T(8,128)(2,1)S(1)} collective-permute-done((bf16[80,512]{1,0:T(8,128)(2,1)S(1)}, bf16[80,512]{1,0:T(8,128)(2,1)S(1)}, u32[]{:S(2)}, u32[]{:S(2)}) %collective-permute-start.1) | collective-permute-done | bytes 81952 | tf_op jit(solution)/shard_map/ppermute | solution.py:27
  17.6 12.8 %all_to_all.45 = bf16[8,20,8,128]{3,2,1,0:T(8,128)(2,1)S(1)} all-to-all(bf16[8,20,8,128]{3,2,1,0:T(8,128)(2,1)S(1)} %bitcast.92), channel_id=1, replica_groups=mesh['z'=8,'x'=4,'c'=2,'y'=4] {'x','c'}, dimensions={0} | all-to-all | bytes 655360 | tf_op jit(solution)/shard_map/all_to_all | solution.py:51
  30.5 19.3 %all_to_all.46 = bf16[8,20,8,128]{3,2,1,0:T(8,128)(2,1)S(1)} all-to-all(bf16[8,20,8,128]{3,2,1,0:T(8,128)(2,1)S(1)} %broadcast_in_dim.62), channel_id=1, replica_groups=mesh['z'=8,'x'=4,'c'=2,'y'=4] {'z'}, dimensions={0} | all-to-all | bytes 655360 | tf_op jit(solution)/shard_map/all_to_all | solution.py:51
  50.0 12.8 %all_to_all.47 = bf16[8,20,8,128]{3,2,1,0:T(8,128)(2,1)S(1)} all-to-all(bf16[8,20,8,128]{3,2,1,0:T(8,128)(2,1)S(1)} %broadcast_in_dim.63), channel_id=1, replica_groups=mesh['z'=8,'x'=4,'c'=2,'y'=4] {'x','c'}, dimensions={0} | all-to-all | bytes 655360 | tf_op jit(solution)/shard_map/all_to_all | solution.py:51
  70.5 4.5 %convolution_convert_fusion.1 = bf16[80,7168]{1,0:T(8,128)(2,1)S(1)} fusion(bf16[512,7168]{1,0:T(8,128)(2,1)} %param.5, bf16[80,512]{1,0:T(8,128)(2,1)S(1)} %collective-permute-done.5, bf16[80,512]{1,0:T(8,128)(2,1)S(1)} %collective-permute-done.4, bf16[80,512]{1,0:T(8,128)(2,1)S(1)} %collective-permute-done.3, ...), kind=kOutput, calls=%fused_computation.1 | convolution fusion | flops 588185600 | bytes 8815104 | tf_op jit(solution)/shard_map/dot_general | solution.py:15
  80.6 20.8 %all_to_all.48 = bf16[32,9,8,128]{3,2,1,0:T(8,128)(2,1)S(1)} all-to-all(bf16[32,9,8,128]{3,2,1,0:T(8,128)(2,1)S(1)} %fusion.1), channel_id=1, replica_groups=mesh['z'=8,'x'=4,'c'=2,'y'=4] {'z','x'}, dimensions={0} | all-to-all | bytes 1179648 | tf_op jit(solution)/shard_map/all_to_all | solution.py:51
  101.6 21.6 %all_to_all.49 = bf16[32,9,8,128]{3,2,1,0:T(8,128)(2,1)S(1)} all-to-all(bf16[32,9,8,128]{3,2,1,0:T(8,128)(2,1)S(1)} %broadcast_in_dim.64), channel_id=1, replica_groups=mesh['z'=8,'x'=4,'c'=2,'y'=4] {'z','x'}, dimensions={0} | all-to-all | bytes 1179648 | tf_op jit(solution)/shard_map/all_to_all | solution.py:51
  123.2 3.5 %collective-permute-start.7 = (bf16[32,9,8,128]{3,2,1,0:T(8,128)(2,1)S(1)}, bf16[32,9,8,128]{3,2,1,0:T(8,128)(2,1)S(1)}, u32[]{:S(2)}, u32[]{:S(2)}) collective-permute-start(bf16[32,9,8,128]{3,2,1,0:T(8,128)(2,1)S(1)} %all_to_all.49), channel_id=1, source_target_pairs={{0,4},{4,0},{1,5},{5,1},{2,6},{6,2},{3,7},{7,3},{8,12},{12,8},{9,1... | collective-permute-start | bytes 1769480 | tf_op jit(solution)/shard_map/ppermute | solution.py:27
  128.6 5.4 %convolution_convert_fusion.5 = bf16[80,512]{1,0:T(8,128)(2,1)S(1)} fusion(bf16[80,7168]{1,0:T(8,128)(2,1)S(1)} %bitcast.91, bf16[512,7168]{1,0:T(8,128)(2,1)} %param.5), kind=kOutput, calls=%fused_computation.14 | convolution fusion | flops 587243520 | bytes 8568832 | tf_op jit(solution)/shard_map/dot_general | solution.py:15
  137.8 2.4 collective-permute-done.9
  140.2 2.3 collective-permute-done.8
  142.9 12.1 %all_to_all.50 = bf16[8,20,8,128]{3,2,1,0:T(8,128)(2,1)S(1)} all-to-all(bf16[8,20,8,128]{3,2,1,0:T(8,128)(2,1)S(1)} %bitcast.93), channel_id=1, replica_groups=mesh['z'=8,'x'=4,'c'=2,'y'=4] {'x','c'}, dimensions={0} | all-to-all | bytes 655360 | tf_op jit(solution)/shard_map/all_to_all | solution.py:51
  155.1 15.0 %all_to_all.51 = bf16[8,20,8,128]{3,2,1,0:T(8,128)(2,1)S(1)} all-to-all(bf16[8,20,8,128]{3,2,1,0:T(8,128)(2,1)S(1)} %broadcast_in_dim.65), channel_id=1, replica_groups=mesh['z'=8,'x'=4,'c'=2,'y'=4] {'z'}, dimensions={0} | all-to-all | bytes 655360 | tf_op jit(solution)/shard_map/all_to_all | solution.py:51
  170.9 4.9 %all-to-all-start.7 = ((bf16[8,20,8,128]{3,2,1,0:T(8,128)(2,1)}), bf16[8,20,8,128]{3,2,1,0:T(8,128)(2,1)S(1)}, u32[]{:S(2)}, u32[]{:S(2)}) async-start(bf16[8,20,8,128]{3,2,1,0:T(8,128)(2,1)} %broadcast_in_dim.66), calls=%async_computation.7 | async-start | bytes 655360 | tf_op jit(solution)/shard_map/all_to_all | solution.py:51
  175.9 7.1 %all-to-all-done.7 = bf16[8,20,8,128]{3,2,1,0:T(8,128)(2,1)S(1)} async-done(((bf16[8,20,8,128]{3,2,1,0:T(8,128)(2,1)}), bf16[8,20,8,128]{3,2,1,0:T(8,128)(2,1)S(1)}, u32[]{:S(2)}, u32[]{:S(2)}) %all-to-all-start.7) | async-done | bytes 327712 | tf_op jit(solution)/shard_map/all_to_all | solution.py:51
  189.8 5.5 %convolution_convert_fusion = bf16[80,7168]{1,0:T(8,128)(2,1)} fusion(bf16[512,7168]{1,0:T(8,128)(2,1)} %param.5, bf16[80,512]{1,0:T(8,128)(2,1)S(1)} %collective-permute-done.16, bf16[80,512]{1,0:T(8,128)(2,1)S(1)} %collective-permute-done.15, bf16[80,512]{1,0:T(8,128)(2,1)S(1)} %collective-permute-done.14, ...), kind=kOutput, calls=%fused_computation | convolution fusion | flops 588144640 | bytes 8815104 | tf_op jit(solution)/shard_map/dot_general | solution.py:15
  195.3 3.6 %reshape.90 = bf16[80,32,2,112]{3,2,1,0:T(2,128)(2,1)} reshape(bf16[80,7168]{1,0:T(8,128)(2,1)} %convolution_convert_fusion) | data formatting | bytes 2293760 | tf_op jit(solution)/shard_map/reshape | solution.py:121
  203.5 2.9 %collective-permute-start.17 = (bf16[32,80,114]{2,1,0:T(8,128)(2,1)}, bf16[32,80,114]{2,1,0:T(8,128)(2,1)S(1)}, u32[]{:S(2)}, u32[]{:S(2)}) collective-permute-start(bf16[32,80,114]{2,1,0:T(8,128)(2,1)} %dynamic-slice_bitcast_fusion), channel_id=1, source_target_pairs={{0,4},{4,0},{1,5},{5,1},{2,6},{6,2},{3,7},{7,3},{8,12},{12,8},{9,1... | collective-permute-start | bytes 1751048 | tf_op jit(solution)/shard_map/ppermute | solution.py:27
  214.7 3.9 %all-to-all-start.8 = ((bf16[32,80,114]{2,1,0:T(8,128)(2,1)}), bf16[32,80,114]{2,1,0:T(8,128)(2,1)S(1)}, u32[]{:S(2)}, u32[]{:S(2)}) async-start(bf16[32,80,114]{2,1,0:T(8,128)(2,1)} %fusion), calls=%async_computation.8 | async-start | bytes 1310720 | tf_op jit(solution)/shard_map/all_to_all | solution.py:51
  218.6 7.3 %cholesky.17 = f32[80,80]{1,0:T(8,128)S(1)} custom-call(f32[80,80]{1,0:T(8,128)S(1)} %fusion.16), custom_call_target="Cholesky" | custom-call | tf_op jit(solution)/shard_map/jit(cholesky)/cholesky | solution.py:113
  227.3 6.1 %custom-call.6 = f32[1,80,80]{1,2,0:T(8,128)S(1)} custom-call(f32[1,80,80]{2,1,0:T(8,128)S(1)} %fusion.12), custom_call_target="InvertDiagBlocksLowerTriangular" | custom-call | tf_op jit(solution)/shard_map/triangular_solve | solution.py:114
  234.5 3.1 %all-to-all-done.8 = bf16[32,80,114]{2,1,0:T(8,128)(2,1)S(1)} async-done(((bf16[32,80,114]{2,1,0:T(8,128)(2,1)}), bf16[32,80,114]{2,1,0:T(8,128)(2,1)S(1)}, u32[]{:S(2)}, u32[]{:S(2)}) %all-to-all-start.8) | async-done | bytes 583712 | tf_op jit(solution)/shard_map/all_to_all | solution.py:51
  (75 shorter events, 48.0 us)
Async XLA Ops:
  0.6 16.5 %copy-start = (bf16[512,2048]{1,0:T(8,128)(2,1)S(1)}, bf16[512,2048]{1,0:T(8,128)(2,1)}, u32[]{:S(2)}) copy-start(bf16[512,2048]{1,0:T(8,128)(2,1)} %param.4) | copy-start | bytes 6291460
  6.6 5.3 %collective-permute-start.2 = (bf16[80,512]{1,0:T(8,128)(2,1)S(1)}, bf16[80,512]{1,0:T(8,128)(2,1)S(1)}, u32[]{:S(2)}, u32[]{:S(2)}) collective-permute-start(bf16[80,512]{1,0:T(8,128)(2,1)S(1)} %convolution_convert_fusion.7), channel_id=1, source_target_pairs={{0,3},{1,0},{2,1},{3,2},{4,7},{5,4},{6,5},{7,6},{8,11},{9,8},{10,9... | collective-permute-start | bytes 245768 | tf_op jit(solution)/shard_map/ppermute | solution.py:27
  10.2 4.9 %collective-permute-start.1 = (bf16[80,512]{1,0:T(8,128)(2,1)S(1)}, bf16[80,512]{1,0:T(8,128)(2,1)S(1)}, u32[]{:S(2)}, u32[]{:S(2)}) collective-permute-start(bf16[80,512]{1,0:T(8,128)(2,1)S(1)} %convolution_convert_fusion.7), channel_id=1, source_target_pairs={{0,2},{1,3},{2,0},{3,1},{4,6},{5,7},{6,4},{7,5},{8,10},{9,11},{10,... | collective-permute-start | bytes 245768 | tf_op jit(solution)/shard_map/ppermute | solution.py:27
  10.6 6.6 %collective-permute-start = (bf16[80,512]{1,0:T(8,128)(2,1)S(1)}, bf16[80,512]{1,0:T(8,128)(2,1)S(1)}, u32[]{:S(2)}, u32[]{:S(2)}) collective-permute-start(bf16[80,512]{1,0:T(8,128)(2,1)S(1)} %convolution_convert_fusion.7), channel_id=1, source_target_pairs={{0,1},{1,2},{2,3},{3,0},{4,5},{5,6},{6,7},{7,4},{8,9},{9,10},{10,1... | collective-permute-start | bytes 245768 | tf_op jit(solution)/shard_map/ppermute | solution.py:27
  63.5 3.4 %collective-permute-start.5 = (bf16[80,512]{1,0:T(8,128)(2,1)S(1)}, bf16[80,512]{1,0:T(8,128)(2,1)S(1)}, u32[]{:S(2)}, u32[]{:S(2)}) collective-permute-start(bf16[80,512]{1,0:T(8,128)(2,1)S(1)} %convolution_convert_fusion.6), channel_id=1, source_target_pairs={{0,3},{1,0},{2,1},{3,2},{4,7},{5,4},{6,5},{7,6},{8,11},{9,8},{10,9... | collective-permute-start | bytes 245768 | tf_op jit(solution)/shard_map/ppermute | solution.py:27
  63.8 4.8 %collective-permute-start.4 = (bf16[80,512]{1,0:T(8,128)(2,1)S(1)}, bf16[80,512]{1,0:T(8,128)(2,1)S(1)}, u32[]{:S(2)}, u32[]{:S(2)}) collective-permute-start(bf16[80,512]{1,0:T(8,128)(2,1)S(1)} %convolution_convert_fusion.6), channel_id=1, source_target_pairs={{0,2},{1,3},{2,0},{3,1},{4,6},{5,7},{6,4},{7,5},{8,10},{9,11},{10,... | collective-permute-start | bytes 245768 | tf_op jit(solution)/shard_map/ppermute | solution.py:27
  64.3 6.2 %collective-permute-start.3 = (bf16[80,512]{1,0:T(8,128)(2,1)S(1)}, bf16[80,512]{1,0:T(8,128)(2,1)S(1)}, u32[]{:S(2)}, u32[]{:S(2)}) collective-permute-start(bf16[80,512]{1,0:T(8,128)(2,1)S(1)} %convolution_convert_fusion.6), channel_id=1, source_target_pairs={{0,1},{1,2},{2,3},{3,0},{4,5},{5,6},{6,7},{7,4},{8,9},{9,10},{10,1... | collective-permute-start | bytes 245768 | tf_op jit(solution)/shard_map/ppermute | solution.py:27
  75.9 3.5 %collective-permute-start.6 = (bf16[32,9,8,128]{3,2,1,0:T(8,128)(2,1)}, bf16[32,9,8,128]{3,2,1,0:T(8,128)(2,1)}, u32[]{:S(2)}, u32[]{:S(2)}) collective-permute-start(bf16[32,9,8,128]{3,2,1,0:T(8,128)(2,1)} %dynamic-slice_bitcast_fusion.1), channel_id=1, source_target_pairs={{0,4},{4,0},{1,5},{5,1},{2,6},{6,2},{3,7},{7,3},{8,12},{12,8},{9,1... | collective-permute-start | bytes 1769480 | tf_op jit(solution)/shard_map/ppermute | solution.py:27
  123.2 5.1 %collective-permute-start.7 = (bf16[32,9,8,128]{3,2,1,0:T(8,128)(2,1)S(1)}, bf16[32,9,8,128]{3,2,1,0:T(8,128)(2,1)S(1)}, u32[]{:S(2)}, u32[]{:S(2)}) collective-permute-start(bf16[32,9,8,128]{3,2,1,0:T(8,128)(2,1)S(1)} %all_to_all.49), channel_id=1, source_target_pairs={{0,4},{4,0},{1,5},{5,1},{2,6},{6,2},{3,7},{7,3},{8,12},{12,8},{9,1... | collective-permute-start | bytes 1769480 | tf_op jit(solution)/shard_map/ppermute | solution.py:27
  134.1 3.7 %collective-permute-start.10 = (bf16[80,512]{1,0:T(8,128)(2,1)S(1)}, bf16[80,512]{1,0:T(8,128)(2,1)S(1)}, u32[]{:S(2)}, u32[]{:S(2)}) collective-permute-start(bf16[80,512]{1,0:T(8,128)(2,1)S(1)} %convolution_convert_fusion.5), channel_id=1, source_target_pairs={{0,3},{1,0},{2,1},{3,2},{4,7},{5,4},{6,5},{7,6},{8,11},{9,8},{10,9... | collective-permute-start | bytes 245768 | tf_op jit(solution)/shard_map/ppermute | solution.py:27
  135.3 4.9 %collective-permute-start.9 = (bf16[80,512]{1,0:T(8,128)(2,1)S(1)}, bf16[80,512]{1,0:T(8,128)(2,1)S(1)}, u32[]{:S(2)}, u32[]{:S(2)}) collective-permute-start(bf16[80,512]{1,0:T(8,128)(2,1)S(1)} %convolution_convert_fusion.5), channel_id=1, source_target_pairs={{0,2},{1,3},{2,0},{3,1},{4,6},{5,7},{6,4},{7,5},{8,10},{9,11},{10,... | collective-permute-start | bytes 245768 | tf_op jit(solution)/shard_map/ppermute | solution.py:27
  136.0 6.5 %collective-permute-start.8 = (bf16[80,512]{1,0:T(8,128)(2,1)S(1)}, bf16[80,512]{1,0:T(8,128)(2,1)S(1)}, u32[]{:S(2)}, u32[]{:S(2)}) collective-permute-start(bf16[80,512]{1,0:T(8,128)(2,1)S(1)} %convolution_convert_fusion.5), channel_id=1, source_target_pairs={{0,1},{1,2},{2,3},{3,0},{4,5},{5,6},{6,7},{7,4},{8,9},{9,10},{10,1... | collective-permute-start | bytes 245768 | tf_op jit(solution)/shard_map/ppermute | solution.py:27
  170.9 12.1 %all-to-all-start.7 = ((bf16[8,20,8,128]{3,2,1,0:T(8,128)(2,1)}), bf16[8,20,8,128]{3,2,1,0:T(8,128)(2,1)S(1)}, u32[]{:S(2)}, u32[]{:S(2)}) async-start(bf16[8,20,8,128]{3,2,1,0:T(8,128)(2,1)} %broadcast_in_dim.66), calls=%async_computation.7 | async-start | bytes 655360 | tf_op jit(solution)/shard_map/all_to_all | solution.py:51
  183.8 3.4 %collective-permute-start.16 = (bf16[80,512]{1,0:T(8,128)(2,1)S(1)}, bf16[80,512]{1,0:T(8,128)(2,1)S(1)}, u32[]{:S(2)}, u32[]{:S(2)}) collective-permute-start(bf16[80,512]{1,0:T(8,128)(2,1)S(1)} %convolution_convert_fusion.4), channel_id=1, source_target_pairs={{0,3},{1,0},{2,1},{3,2},{4,7},{5,4},{6,5},{7,6},{8,11},{9,8},{10,9... | collective-permute-start | bytes 245768 | tf_op jit(solution)/shard_map/ppermute | solution.py:27
  184.1 4.8 %collective-permute-start.15 = (bf16[80,512]{1,0:T(8,128)(2,1)S(1)}, bf16[80,512]{1,0:T(8,128)(2,1)S(1)}, u32[]{:S(2)}, u32[]{:S(2)}) collective-permute-start(bf16[80,512]{1,0:T(8,128)(2,1)S(1)} %convolution_convert_fusion.4), channel_id=1, source_target_pairs={{0,2},{1,3},{2,0},{3,1},{4,6},{5,7},{6,4},{7,5},{8,10},{9,11},{10,... | collective-permute-start | bytes 245768 | tf_op jit(solution)/shard_map/ppermute | solution.py:27
  184.8 5.0 %collective-permute-start.14 = (bf16[80,512]{1,0:T(8,128)(2,1)S(1)}, bf16[80,512]{1,0:T(8,128)(2,1)S(1)}, u32[]{:S(2)}, u32[]{:S(2)}) collective-permute-start(bf16[80,512]{1,0:T(8,128)(2,1)S(1)} %convolution_convert_fusion.4), channel_id=1, source_target_pairs={{0,1},{1,2},{2,3},{3,0},{4,5},{5,6},{6,7},{7,4},{8,9},{9,10},{10,1... | collective-permute-start | bytes 245768 | tf_op jit(solution)/shard_map/ppermute | solution.py:27
  201.5 1.1 copy-start.1
  203.5 9.0 %collective-permute-start.17 = (bf16[32,80,114]{2,1,0:T(8,128)(2,1)}, bf16[32,80,114]{2,1,0:T(8,128)(2,1)S(1)}, u32[]{:S(2)}, u32[]{:S(2)}) collective-permute-start(bf16[32,80,114]{2,1,0:T(8,128)(2,1)} %dynamic-slice_bitcast_fusion), channel_id=1, source_target_pairs={{0,4},{4,0},{1,5},{5,1},{2,6},{6,2},{3,7},{7,3},{8,12},{12,8},{9,1... | collective-permute-start | bytes 1751048 | tf_op jit(solution)/shard_map/ppermute | solution.py:27
  206.6 4.5 %collective-permute-start.12 = (f32[80,80]{0,1:T(8,128)S(1)}, f32[80,80]{0,1:T(8,128)S(1)}, u32[]{:S(2)}, u32[]{:S(2)}) collective-permute-start(f32[80,80]{0,1:T(8,128)S(1)} %fusion.26), channel_id=1, source_target_pairs={{0,2},{1,3},{2,0},{3,1},{4,6},{5,7},{6,4},{7,5},{8,10},{9,11},{10,... | collective-permute-start | bytes 76808 | tf_op jit(solution)/shard_map/ppermute | solution.py:27
  207.2 5.2 %collective-permute-start.11 = (f32[80,80]{0,1:T(8,128)S(1)}, f32[80,80]{0,1:T(8,128)S(1)}, u32[]{:S(2)}, u32[]{:S(2)}) collective-permute-start(f32[80,80]{0,1:T(8,128)S(1)} %fusion.26), channel_id=1, source_target_pairs={{0,1},{1,2},{2,3},{3,0},{4,5},{5,6},{6,7},{7,4},{8,9},{9,10},{10,1... | collective-permute-start | bytes 76808 | tf_op jit(solution)/shard_map/ppermute | solution.py:27
  208.4 4.0 %collective-permute-start.13 = (f32[80,80]{0,1:T(8,128)S(1)}, f32[80,80]{0,1:T(8,128)S(1)}, u32[]{:S(2)}, u32[]{:S(2)}) collective-permute-start(f32[80,80]{0,1:T(8,128)S(1)} %fusion.26), channel_id=1, source_target_pairs={{0,3},{1,0},{2,1},{3,2},{4,7},{5,4},{6,5},{7,6},{8,11},{9,8},{10,9... | collective-permute-start | bytes 76808 | tf_op jit(solution)/shard_map/ppermute | solution.py:27
  214.7 22.9 %all-to-all-start.8 = ((bf16[32,80,114]{2,1,0:T(8,128)(2,1)}), bf16[32,80,114]{2,1,0:T(8,128)(2,1)S(1)}, u32[]{:S(2)}, u32[]{:S(2)}) async-start(bf16[32,80,114]{2,1,0:T(8,128)(2,1)} %fusion), calls=%async_computation.8 | async-start | bytes 1310720 | tf_op jit(solution)/shard_map/all_to_all | solution.py:51

commit v2 on v1

v2 whole, which is shorter than its diff:
```python
import functools

import jax
import jax.numpy as jnp
from jax import lax
from jax.experimental import pallas as pl
from jax.experimental.pallas import tpu as pltpu
from jax.sharding import Mesh, PartitionSpec as P

D = 8192
FF = 28672
K = 80
LIVE = 16384
F32 = jnp.float32
BF16 = jnp.bfloat16


def dot(left, right, contract):
    return lax.dot_general(left, right, (contract, ((), ())), preferred_element_type=F32)


def along_features(small, big):
    return dot(small, big, ((1,), (1,)))


def along_tokens(small, big):
    return dot(small, big, ((1,), (0,)))


def shifted(value, axis, size, step):
    return lax.ppermute(value, axis, [(i, (i + step) % size) for i in range(size)])


def y_pieces(part):
    sent = part.astype(BF16)
    return [sent] + [shifted(sent, "y", 4, step) for step in (1, 2, 3)]


def y_sum(part):
    pieces = y_pieces(part)
    total = pieces[0].astype(F32)
    for piece in pieces[1:]:
        total = total + piece.astype(F32)
    return total


def to_tiles(array):
    rows, cols = array.shape
    tiles = array.reshape(rows // 8, 8, cols // 128, 128).transpose(0, 2, 1, 3)
    return tiles.reshape(-1, 8, 128)


def from_tiles(tiles, rows, cols):
    split = tiles.reshape(rows // 8, cols // 128, 8, 128).transpose(0, 2, 1, 3)
    return split.reshape(rows, cols)


def aligned(square):
    return jnp.pad(square, ((0, 0), (0, 128 - square.shape[1])))


def exchange(pieces, axes):
    return lax.all_to_all(pieces, axes, 0, 0, tiled=True)


def spread(piece, axes, count):
    return exchange(jnp.broadcast_to(piece[None], (count,) + piece.shape), axes)


def core_add(kept, sent):
    came = shifted(sent, "c", 2, 1)
    return (kept.astype(F32) + came.astype(F32)).astype(BF16)


def chip_sum(half, scale):
    rows, cols = half.shape
    tiles = to_tiles(half)
    count = tiles.shape[0]
    per = -(-count // 32)
    tiles = jnp.pad(tiles, ((0, 32 * per - count), (0, 0), (0, 0)))
    pieces = tiles.reshape(32, per, 8, 128)
    mine = (exchange(pieces, ("z", "x")).astype(F32).sum(0) * scale).astype(BF16)
    whole = spread(mine, ("z", "x"), 32).reshape(32 * per, 8, 128)[:count]
    own = from_tiles(whole, rows, cols)
    return jnp.concatenate([own, shifted(own, "c", 2, 1)], 0)


CHUNKS = 14
BLOCK = 1024
VMEM = pl.BlockSpec(memory_space=pltpu.VMEM)
SMEM = pl.BlockSpec(memory_space=pltpu.SMEM)


def cost(grads):
    rows, cols = grads.shape
    return pl.CostEstimate(
        flops=2 * K * rows * cols, bytes_accessed=2 * rows * cols, transcendentals=0
    )


PARAMS = pltpu.CompilerParams(vmem_limit_bytes=16 << 20)


def load_kernel(
    place_ref, test_ref, grads_ref, part_ref, held_ref, test_held, sems, test_sems
):
    width = grads_ref.shape[1] // CHUNKS
    copies = []
    for k in range(CHUNKS):
        cols = pl.ds(k * width, width)
        first = pltpu.make_async_copy(
            test_ref.at[:, cols], test_held.at[:, cols], test_sems.at[k]
        )
        second = pltpu.make_async_copy(
            grads_ref.at[:, cols], held_ref.at[:, cols], sems.at[k]
        )
        first.start()
        second.start()
        copies.append((first, second))
    total = None
    for k in range(CHUNKS):
        cols = pl.ds(k * width, width)
        copies[k][0].wait()
        copies[k][1].wait()
        step = dot(test_held[:, cols], held_ref[:, cols], ((1,), (1,)))
        total = step if total is None else total + step
    swapped = jnp.concatenate([total[K // 2 :], total[: K // 2]], 0)
    part_ref[...] = jnp.where(place_ref[1] == 0, total, swapped).astype(BF16)


def load_and_sketch(place, test_t, grads):
    rows, cols = grads.shape
    test_t = pltpu.with_memory_space_constraint(test_t, pltpu.HBM)
    grads = pltpu.with_memory_space_constraint(grads, pltpu.HBM)
    return pl.pallas_call(
        load_kernel,
        out_shape=(
            jax.ShapeDtypeStruct((K, rows), BF16),
            pltpu.VMEM((rows, cols), BF16),
        ),
        in_specs=[SMEM] + [pl.BlockSpec(memory_space=pl.ANY)] * 2,
        out_specs=(VMEM, VMEM),
        scratch_shapes=[
            pltpu.VMEM((K, cols), BF16),
            pltpu.SemaphoreType.DMA((CHUNKS,)),
            pltpu.SemaphoreType.DMA((CHUNKS,)),
        ],
        compiler_params=PARAMS,
        cost_estimate=cost(grads),
        name="load_and_sketch",
    )(place, test_t, grads)


def summed_small(live_ref, refs, scale):
    total = refs[0][...].astype(F32)
    for ref in refs[1:]:
        total = total + ref[...].astype(F32)
    row = lax.broadcasted_iota(jnp.int32, total.shape, 1)
    return jnp.where(row < live_ref[0], total * scale, 0.0).astype(BF16)


def token_kernel(scale, live_ref, *refs):
    big_ref, kept_ref, sent_ref = refs[-3:]
    small = summed_small(live_ref, refs[:-3], scale)
    half = K // 2
    for k in range(big_ref.shape[1] // BLOCK):
        cols = slice(k * BLOCK, (k + 1) * BLOCK)
        out = dot(small, big_ref[:, cols], ((1,), (0,)))
        kept_ref[:, cols] = out[:half].astype(kept_ref.dtype)
        sent_ref[:, cols] = out[half:].astype(sent_ref.dtype)


def token_parts(live, pieces, big, scale, dtype):
    big = pltpu.with_memory_space_constraint(big, pltpu.VMEM)
    shape = jax.ShapeDtypeStruct((K // 2, big.shape[1]), dtype)
    return pl.pallas_call(
        functools.partial(token_kernel, scale),
        out_shape=(shape, shape),
        in_specs=[SMEM] + [VMEM] * (len(pieces) + 1),
        out_specs=(VMEM, VMEM),
        compiler_params=PARAMS,
        cost_estimate=cost(big),
        name="token_parts",
    )(live, *pieces, big)


def again_kernel(small_ref, big_ref, part_ref):
    total = None
    for k in range(big_ref.shape[1] // BLOCK):
        cols = slice(k * BLOCK, (k + 1) * BLOCK)
        step = dot(small_ref[:, cols], big_ref[:, cols], ((1,), (1,)))
        total = step if total is None else total + step
    part_ref[...] = total.astype(BF16)


def again_part(small, held):
    rows, cols = held.shape
    held = pltpu.with_memory_space_constraint(held, pltpu.VMEM)
    return pl.pallas_call(
        again_kernel,
        out_shape=jax.ShapeDtypeStruct((K, rows), BF16),
        in_specs=[VMEM, VMEM],
        out_specs=VMEM,
        compiler_params=PARAMS,
        cost_estimate=cost(held),
        name="again_part",
    )(small, held)


def up_kernel(place_ref, live_ref, small_ref, big_ref, kept_ref, sent_ref):
    owned = big_ref.shape[1] // 64
    lane = lax.broadcasted_iota(jnp.int32, (K, 128), 1)
    live = live_ref[0]
    high = (live // 32).astype(F32)
    low = (live % 32).astype(F32)
    digits = jnp.where(lane == owned, high, jnp.where(lane == owned + 1, low, 0.0))
    tail = digits.astype(BF16)[:, owned:]
    wide = small_ref[...].astype(F32)
    both = jnp.concatenate([wide, wide[: K // 2]], 0).astype(BF16)

    def fill(places):
        for z in range(8):
            block = big_ref[:, z * 8 * owned : (z + 1) * 8 * owned]
            out = dot(both, block, ((1,), (0,)))
            views = (out[:K].astype(BF16), out[K // 2 :].astype(BF16))
            for x in range(4):
                for c in range(2):
                    at = (2 * x + c) * owned
                    ref, turn = places[c]
                    piece = views[turn][:, at : at + owned]
                    ref[4 * z + x] = jnp.concatenate([piece, tail], 1)

    @pl.when(place_ref[1] == 0)
    def _():
        fill(((kept_ref, 0), (sent_ref, 1)))

    @pl.when(place_ref[1] != 0)
    def _():
        fill(((sent_ref, 1), (kept_ref, 0)))


def up_parts(place, live, small, held):
    held = pltpu.with_memory_space_constraint(held, pltpu.VMEM)
    shape = jax.ShapeDtypeStruct((32, K, 128), BF16)
    return pl.pallas_call(
        up_kernel,
        out_shape=(shape, shape),
        in_specs=[SMEM] * 2 + [VMEM] * 2,
        out_specs=(VMEM, VMEM),
        compiler_params=PARAMS,
        cost_estimate=cost(held),
        name="up_parts",
    )(place, live, small, held)


def unturned(rows, first):
    return jnp.where(first, rows, jnp.roll(rows, K // 2, 0))


def local(tokens, out_grads, test_matrix, slot_counts):
    rows = tokens.shape[0]
    live_rows = slot_counts[0]
    kept = (jnp.arange(rows, dtype=jnp.int32) < live_rows)[None, :]
    scale = LIVE ** -0.5
    place = jnp.stack([lax.axis_index(("z", "x", "c")), lax.axis_index("c")])
    width = tokens.shape[1] // 64

    def masked(value):
        return jnp.where(kept, value, 0.0).astype(BF16)

    sketch_part, held = load_and_sketch(place, test_matrix.T, out_grads)
    sketch_pieces = y_pieces(sketch_part)
    ranged = chip_sum(
        core_add(*token_parts(slot_counts, sketch_pieces, tokens, 1.0, F32)), scale
    )
    back_pieces = y_pieces(along_features(ranged, tokens))
    transposed = chip_sum(
        core_add(*token_parts(slot_counts, back_pieces, held, D ** -0.5, BF16)), scale
    )
    again_pieces = y_pieces(again_part(transposed, held))
    whole_range = chip_sum(
        core_add(*token_parts(slot_counts, again_pieces, tokens, FF ** -0.5, F32)), scale
    )

    gram_part = along_features(whole_range, whole_range)
    high = gram_part.astype(BF16)
    low = (gram_part - high.astype(F32)).astype(BF16)
    joined = jnp.concatenate(
        [along_features(whole_range, tokens).astype(BF16), aligned(high), aligned(low)], 1
    )
    summed = y_sum(joined)
    projected = masked(summed[:, :rows])
    gram = summed[:, rows : rows + K] + summed[:, rows + 128 : rows + 128 + K]
    kept_up, sent_up = up_parts(place, slot_counts, projected, held)
    gram, sent_up, place = lax.optimization_barrier((gram, sent_up, place))
    first = place[1] == 0
    gram = unturned(unturned(gram, first).T, first)
    lower = jnp.linalg.cholesky(gram)
    inverse = lax.linalg.triangular_solve(
        lower, jnp.eye(K, dtype=F32), left_side=True, lower=True
    )

    up_sum = exchange(core_add(kept_up, sent_up), ("z", "x")).astype(F32).sum(0)
    owned = out_grads.shape[1] // 64
    live_total = 32.0 * up_sum[0, owned] + up_sum[0, owned + 1]
    inv_root = lax.rsqrt(live_total)
    adapter_up = inv_root * jnp.dot(
        inverse, unturned(up_sum[:, :owned], first), precision=lax.Precision.HIGHEST
    ).T

    own = lax.dynamic_slice_in_dim(whole_range, place[0] * width, width, 1)
    own = unturned(own.astype(F32), first)
    adapter_down = jnp.dot(inverse, own, precision=lax.Precision.HIGHEST).T * D ** 0.5
    return adapter_down, adapter_up


def solution(mesh):
    split = Mesh(mesh.devices.reshape(8, 4, 2, 4), ("z", "x", "c", "y"))
    dp = ("z", "x", "c")
    placed = (P(dp, "y"), P(dp, "y"), P("y", None), P(dp))
    return jax.shard_map(
        local,
        mesh=split,
        in_specs=placed,
        out_specs=(P(("y",) + dp, None), P(("y",) + dp, None)),
        check_vma=False,
    )
```

time: 242 us -> 207 us (0.86)
  matrix products: 26 us -> 3.63 us
  waiting for transfers between devices: 37.8 us -> 25.6 us
  Pallas kernels: 0 us -> 11.4 us
  local copies, waits for them, and re-layouts: 10.5 us -> 1.64 us
  blocking collectives: 114 us -> 106 us
  starting transfers between devices: 29.8 us -> 37.3 us
  other arithmetic: 19.2 us -> 16.7 us
    dot_general x9 -> x3, matrix products: 24.1 us -> 1.76 us  [dot(): lax.dot_general(left, right, (contract, ((), ())), preferred_element_type...]
    ppermute x18 -> x19, starting transfers between devices: 20.9 us -> 33.4 us  [shifted(): lax.ppermute(value, axis, [(i, (i + step) % size) for i in range(size)])]
    pallas_call x0 -> x6, Pallas kernels: none -> 11.4 us  [the longest x1 4.75 us: load_and_sketch(): pl.pallas_call(load_kernel, out_shape=(jax.ShapeDtypeStruct((K, rows), BF...]
    all_to_all x7 -> x6, blocking collectives: 114 us -> 106 us  [exchange(): return lax.all_to_all(pieces, axes, 0, 0, tiled=True)]
    all_to_all x2 -> x1, waiting for transfers between devices: 10.2 us -> 2.37 us  [exchange(): return lax.all_to_all(pieces, axes, 0, 0, tiled=True)]
    reshape x2 -> x0, local copies, waits for them, and re-layouts: 5.81 us -> none  [local(): up_part = up_part.reshape(K, 32, 2, owned).transpose(2, 1, 0, 3)]
    all_to_all x2 -> x1, starting transfers between devices: 8.83 us -> 3.9 us  [exchange(): return lax.all_to_all(pieces, axes, 0, 0, tiled=True)]
    ppermute x18 -> x19, waiting for transfers between devices: 27.6 us -> 23.2 us  [shifted(): lax.ppermute(value, axis, [(i, (i + step) % size) for i in range(size)])]
  transfers between devices with their start and end apart: 20 -> 20, of which waited for: 17 -> 17; matrix products, arithmetic and copies ran while one was open for 7% -> 8% of each run, Pallas kernels for 0% -> 0%
where the time goes in v2:
time: 207 us; the launch traced here: 206 us
  blocking collectives  106 us (51%)
  starting transfers between devices  37.3 us (18%)
  waiting for transfers between devices  25.6 us (12%)
  other arithmetic  16.7 us (8%)
  Pallas kernels  11.4 us (6%)
  between operations  4.17 us (2%)
  matrix products  3.63 us (2%)
    all_to_all x6, blocking collectives, exchange(): return lax.all_to_all(pieces, axes, 0, 0, tiled=True)  106 us
    ppermute x19, starting transfers between devices, shifted(): lax.ppermute(value, axis, [(i, (i + step) % size) for i in range(size)])  33.4 us
    ppermute x19, waiting for transfers between devices, shifted(): lax.ppermute(value, axis, [(i, (i + step) % size) for i in range(size)])  23.2 us
    another operation x3, other arithmetic, local(): lower = jnp.linalg.cholesky(gram)  7.98 us
    another operation x2, other arithmetic, local(): lax.linalg.triangular_solve(lower, jnp.eye(K, dtype=F32), left_side=True,...  6.78 us
    pallas_call x1, Pallas kernels, load_and_sketch(): pl.pallas_call(load_kernel, out_shape=(jax.ShapeDtypeStruct((K, rows), BF...  4.75 us
  transfers between devices with their start and end apart: 20, of which 17 were waited for; matrix products, arithmetic and copies ran while one was open for 8% of the time, Pallas kernels for 0%

profile of v2, /device:TPU:1, one launch (start us, length us, event | category | flops | bytes accessed | tf_op | source)
XLA Modules:
  0.0 206.2 jit_solution(6358659143677515912)
XLA Ops:
  0.7 4.8 %load_and_sketch.1 = (bf16[80,512]{1,0:T(8,128)(2,1)S(1)}, bf16[512,7168]{1,0:T(8,128)(2,1)S(1)}) custom-call(s32[2]{0:T(128)S(1)} %pad_add_fusion.place_ref, bf16[80,7168]{1,0:T(8,128)(2,1)} %bitcast.68, bf16[512,7168]{1,0:T(8,128)(2,1)} %grads_ref.1), custom_call_target="tpu_custom_call" | custom-call | flops 587202560 | bytes 7340032 | tf_op jit(solution)/shard_map/load_and_sketch/pallas_call | solution.py:135
  7.7 2.6 %collective-permute-start.1 = (bf16[80,512]{1,0:T(8,128)(2,1)S(1)}, bf16[80,512]{1,0:T(8,128)(2,1)S(1)}, u32[]{:S(2)}, u32[]{:S(2)}) collective-permute-start(bf16[80,512]{1,0:T(8,128)(2,1)S(1)} %get-tuple-element.15.refs_0_), channel_id=1, source_target_pairs={{0,2},{1,3},{2,0},{3,1},{4,6},{5,7},{6,4},{7,5},{8,10},{9,11},{10,... | collective-permute-start | bytes 245768 | tf_op jit(solution)/shard_map/ppermute | solution.py:31
  14.4 2.4 %collective-permute-start.3 = (f32[40,2048]{1,0:T(8,128)S(1)}, f32[40,2048]{1,0:T(8,128)S(1)}, u32[]{:S(2)}, u32[]{:S(2)}) collective-permute-start(f32[40,2048]{1,0:T(8,128)S(1)} %get-tuple-element.17), channel_id=1, source_target_pairs={{0,4},{4,0},{1,5},{5,1},{2,6},{6,2},{3,7},{7,3},{8,12},{12,8},{9,1... | collective-permute-start | bytes 983048 | tf_op jit(solution)/shard_map/ppermute | solution.py:31
  18.1 21.2 %all_to_all.35 = bf16[32,3,8,128]{3,2,1,0:T(8,128)(2,1)S(1)} all-to-all(bf16[32,3,8,128]{3,2,1,0:T(8,128)(2,1)S(1)} %bitcast.70), channel_id=1, replica_groups=mesh['z'=8,'x'=4,'c'=2,'y'=4] {'z','x'}, dimensions={0} | all-to-all | bytes 393216 | tf_op jit(solution)/shard_map/all_to_all | solution.py:63
  39.4 13.8 %all_to_all.36 = bf16[32,3,8,128]{3,2,1,0:T(8,128)(2,1)S(1)} all-to-all(bf16[32,3,8,128]{3,2,1,0:T(8,128)(2,1)S(1)} %broadcast_in_dim.15), channel_id=1, replica_groups=mesh['z'=8,'x'=4,'c'=2,'y'=4] {'z','x'}, dimensions={0} | all-to-all | bytes 393216 | tf_op jit(solution)/shard_map/all_to_all | solution.py:63
  53.2 3.1 %collective-permute-start.4 = (bf16[40,2048]{1,0:T(8,128)(2,1)S(1)}, bf16[40,2048]{1,0:T(8,128)(2,1)S(1)}, u32[]{:S(2)}, u32[]{:S(2)}) collective-permute-start(bf16[40,2048]{1,0:T(8,128)(2,1)S(1)} %bitcast.73), channel_id=1, source_target_pairs={{0,4},{4,0},{1,5},{5,1},{2,6},{6,2},{3,7},{7,3},{8,12},{12,8},{9,1... | collective-permute-start | bytes 491528 | tf_op jit(solution)/shard_map/ppermute | solution.py:31
  58.6 3.0 %collective-permute-start.6 = (bf16[80,512]{1,0:T(8,128)(2,1)S(1)}, bf16[80,512]{1,0:T(8,128)(2,1)S(1)}, u32[]{:S(2)}, u32[]{:S(2)}) collective-permute-start(bf16[80,512]{1,0:T(8,128)(2,1)S(1)} %convolution_convert_fusion.1.refs_0_), channel_id=1, source_target_pairs={{0,2},{1,3},{2,0},{3,1},{4,6},{5,7},{6,4},{7,5},{8,10},{9,11},{10,... | collective-permute-start | bytes 245768 | tf_op jit(solution)/shard_map/ppermute | solution.py:31
  63.0 2.5 %collective-permute-done.6.refs_2_ = bf16[80,512]{1,0:T(8,128)(2,1)S(1)} collective-permute-done((bf16[80,512]{1,0:T(8,128)(2,1)S(1)}, bf16[80,512]{1,0:T(8,128)(2,1)S(1)}, u32[]{:S(2)}, u32[]{:S(2)}) %collective-permute-start.6) | collective-permute-done | bytes 81952 | tf_op jit(solution)/shard_map/ppermute | solution.py:31
  70.3 20.6 %all_to_all.37 = bf16[32,9,8,128]{3,2,1,0:T(8,128)(2,1)S(1)} all-to-all(bf16[32,9,8,128]{3,2,1,0:T(8,128)(2,1)S(1)} %bitcast.59), channel_id=1, replica_groups=mesh['z'=8,'x'=4,'c'=2,'y'=4] {'z','x'}, dimensions={0} | all-to-all | bytes 1179648 | tf_op jit(solution)/shard_map/all_to_all | solution.py:63
  91.1 21.5 %all_to_all.38 = bf16[32,9,8,128]{3,2,1,0:T(8,128)(2,1)S(1)} all-to-all(bf16[32,9,8,128]{3,2,1,0:T(8,128)(2,1)S(1)} %broadcast_in_dim.16), channel_id=1, replica_groups=mesh['z'=8,'x'=4,'c'=2,'y'=4] {'z','x'}, dimensions={0} | all-to-all | bytes 1179648 | tf_op jit(solution)/shard_map/all_to_all | solution.py:63
  112.7 3.9 %collective-permute-start.9 = (bf16[40,7168]{1,0:T(8,128)(2,1)S(1)}, bf16[40,7168]{1,0:T(8,128)(2,1)S(1)}, u32[]{:S(2)}, u32[]{:S(2)}) collective-permute-start(bf16[40,7168]{1,0:T(8,128)(2,1)S(1)} %bitcast.61), channel_id=1, source_target_pairs={{0,4},{4,0},{1,5},{5,1},{2,6},{6,2},{3,7},{7,3},{8,12},{12,8},{9,1... | collective-permute-start | bytes 1720328 | tf_op jit(solution)/shard_map/ppermute | solution.py:31
  118.3 2.3 %again_part.1.refs_0_ = bf16[80,512]{1,0:T(8,128)(2,1)S(1)} custom-call(bf16[80,7168]{1,0:T(8,128)(2,1)S(1)} %pad_maximum_fusion.small_ref, bf16[512,7168]{1,0:T(8,128)(2,1)S(1)} %get-tuple-element.18.refs_4_.big_ref), custom_call_target="tpu_custom_call" | custom-call | flops 587202560 | bytes 7340032 | tf_op jit(solution)/shard_map/again_part/pallas_call | solution.py:199
  121.4 2.5 %collective-permute-start.11 = (bf16[80,512]{1,0:T(8,128)(2,1)S(1)}, bf16[80,512]{1,0:T(8,128)(2,1)S(1)}, u32[]{:S(2)}, u32[]{:S(2)}) collective-permute-start(bf16[80,512]{1,0:T(8,128)(2,1)S(1)} %again_part.1.refs_0_), channel_id=1, source_target_pairs={{0,2},{1,3},{2,0},{3,1},{4,6},{5,7},{6,4},{7,5},{8,10},{9,11},{10,... | collective-permute-start | bytes 245768 | tf_op jit(solution)/shard_map/ppermute | solution.py:31
  125.5 2.2 %collective-permute-done.11.refs_2_ = bf16[80,512]{1,0:T(8,128)(2,1)S(1)} collective-permute-done((bf16[80,512]{1,0:T(8,128)(2,1)S(1)}, bf16[80,512]{1,0:T(8,128)(2,1)S(1)}, u32[]{:S(2)}, u32[]{:S(2)}) %collective-permute-start.11) | collective-permute-done | bytes 81952 | tf_op jit(solution)/shard_map/ppermute | solution.py:31
  131.2 14.8 %all_to_all.39 = bf16[32,3,8,128]{3,2,1,0:T(8,128)(2,1)S(1)} all-to-all(bf16[32,3,8,128]{3,2,1,0:T(8,128)(2,1)S(1)} %bitcast.69), channel_id=1, replica_groups=mesh['z'=8,'x'=4,'c'=2,'y'=4] {'z','x'}, dimensions={0} | all-to-all | bytes 393216 | tf_op jit(solution)/shard_map/all_to_all | solution.py:63
  146.1 13.8 %all_to_all.40 = bf16[32,3,8,128]{3,2,1,0:T(8,128)(2,1)S(1)} all-to-all(bf16[32,3,8,128]{3,2,1,0:T(8,128)(2,1)S(1)} %broadcast_in_dim.21), channel_id=1, replica_groups=mesh['z'=8,'x'=4,'c'=2,'y'=4] {'z','x'}, dimensions={0} | all-to-all | bytes 393216 | tf_op jit(solution)/shard_map/all_to_all | solution.py:63
  159.9 3.1 %collective-permute-start.14 = (bf16[40,2048]{1,0:T(8,128)(2,1)S(1)}, bf16[40,2048]{1,0:T(8,128)(2,1)S(1)}, u32[]{:S(2)}, u32[]{:S(2)}) collective-permute-start(bf16[40,2048]{1,0:T(8,128)(2,1)S(1)} %bitcast.64), channel_id=1, source_target_pairs={{0,4},{4,0},{1,5},{5,1},{2,6},{6,2},{3,7},{7,3},{8,12},{12,8},{9,1... | collective-permute-start | bytes 491528 | tf_op jit(solution)/shard_map/ppermute | solution.py:31
  165.6 2.9 %collective-permute-start.16 = (bf16[80,768]{1,0:T(8,128)(2,1)S(1)}, bf16[80,768]{1,0:T(8,128)(2,1)S(1)}, u32[]{:S(2)}, u32[]{:S(2)}) collective-permute-start(bf16[80,768]{1,0:T(8,128)(2,1)S(1)} %fusion.9), channel_id=1, source_target_pairs={{0,2},{1,3},{2,0},{3,1},{4,6},{5,7},{6,4},{7,5},{8,10},{9,11},{10,... | collective-permute-start | bytes 368648 | tf_op jit(solution)/shard_map/ppermute | solution.py:31
  168.5 2.4 %collective-permute-done.15 = bf16[80,768]{1,0:T(8,128)(2,1)S(1)} collective-permute-done((bf16[80,768]{1,0:T(8,128)(2,1)S(1)}, bf16[80,768]{1,0:T(8,128)(2,1)S(1)}, u32[]{:S(2)}, u32[]{:S(2)}) %collective-permute-start.15) | collective-permute-done | bytes 122912 | tf_op jit(solution)/shard_map/ppermute | solution.py:31
  170.9 3.3 %collective-permute-done.16 = bf16[80,768]{1,0:T(8,128)(2,1)S(1)} collective-permute-done((bf16[80,768]{1,0:T(8,128)(2,1)S(1)}, bf16[80,768]{1,0:T(8,128)(2,1)S(1)}, u32[]{:S(2)}, u32[]{:S(2)}) %collective-permute-start.16) | collective-permute-done | bytes 122912 | tf_op jit(solution)/shard_map/ppermute | solution.py:31
  180.5 3.9 %all-to-all-start.6 = ((bf16[32,80,128]{2,1,0:T(8,128)(2,1)}), bf16[32,80,128]{2,1,0:T(8,128)(2,1)S(1)}, u32[]{:S(2)}, u32[]{:S(2)}) async-start(bf16[32,80,128]{2,1,0:T(8,128)(2,1)} %add_convert_fusion), calls=%async_computation.6 | async-start | bytes 1310720 | tf_op jit(solution)/shard_map/all_to_all | solution.py:63
  184.4 7.3 %cholesky.17 = f32[80,80]{1,0:T(8,128)S(1)} custom-call(f32[80,80]{1,0:T(8,128)S(1)} %fusion.19), custom_call_target="Cholesky" | custom-call | tf_op jit(solution)/shard_map/jit(cholesky)/cholesky | solution.py:298
  193.0 6.1 %custom-call.6 = f32[1,80,80]{1,2,0:T(8,128)S(1)} custom-call(f32[1,80,80]{2,1,0:T(8,128)S(1)} %fusion.10), custom_call_target="InvertDiagBlocksLowerTriangular" | custom-call | tf_op jit(solution)/shard_map/triangular_solve | solution.py:299
  201.0 2.4 %all-to-all-done.6 = bf16[32,80,128]{2,1,0:T(8,128)(2,1)S(1)} async-done(((bf16[32,80,128]{2,1,0:T(8,128)(2,1)}), bf16[32,80,128]{2,1,0:T(8,128)(2,1)S(1)}, u32[]{:S(2)}, u32[]{:S(2)}) %all-to-all-start.6) | async-done | bytes 655392 | tf_op jit(solution)/shard_map/all_to_all | solution.py:63
  (79 shorter events, 35.5 us)
Async XLA Ops:
  0.7 13.2 %copy-start = (bf16[512,2048]{1,0:T(8,128)(2,1)S(1)}, bf16[512,2048]{1,0:T(8,128)(2,1)}, u32[]{:S(2)}) copy-start(bf16[512,2048]{1,0:T(8,128)(2,1)} %refs_4_.3) | copy-start | bytes 6291460
  5.5 6.5 %collective-permute-start = (bf16[80,512]{1,0:T(8,128)(2,1)S(1)}, bf16[80,512]{1,0:T(8,128)(2,1)S(1)}, u32[]{:S(2)}, u32[]{:S(2)}) collective-permute-start(bf16[80,512]{1,0:T(8,128)(2,1)S(1)} %get-tuple-element.15.refs_0_), channel_id=1, source_target_pairs={{0,1},{1,2},{2,3},{3,0},{4,5},{5,6},{6,7},{7,4},{8,9},{9,10},{10,1... | collective-permute-start | bytes 245768 | tf_op jit(solution)/shard_map/ppermute | solution.py:31
  7.7 5.9 %collective-permute-start.1 = (bf16[80,512]{1,0:T(8,128)(2,1)S(1)}, bf16[80,512]{1,0:T(8,128)(2,1)S(1)}, u32[]{:S(2)}, u32[]{:S(2)}) collective-permute-start(bf16[80,512]{1,0:T(8,128)(2,1)S(1)} %get-tuple-element.15.refs_0_), channel_id=1, source_target_pairs={{0,2},{1,3},{2,0},{3,1},{4,6},{5,7},{6,4},{7,5},{8,10},{9,11},{10,... | collective-permute-start | bytes 245768 | tf_op jit(solution)/shard_map/ppermute | solution.py:31
  10.3 3.6 %collective-permute-start.2 = (bf16[80,512]{1,0:T(8,128)(2,1)S(1)}, bf16[80,512]{1,0:T(8,128)(2,1)S(1)}, u32[]{:S(2)}, u32[]{:S(2)}) collective-permute-start(bf16[80,512]{1,0:T(8,128)(2,1)S(1)} %get-tuple-element.15.refs_0_), channel_id=1, source_target_pairs={{0,3},{1,0},{2,1},{3,2},{4,7},{5,4},{6,5},{7,6},{8,11},{9,8},{10,9... | collective-permute-start | bytes 245768 | tf_op jit(solution)/shard_map/ppermute | solution.py:31
  14.4 3.6 %collective-permute-start.3 = (f32[40,2048]{1,0:T(8,128)S(1)}, f32[40,2048]{1,0:T(8,128)S(1)}, u32[]{:S(2)}, u32[]{:S(2)}) collective-permute-start(f32[40,2048]{1,0:T(8,128)S(1)} %get-tuple-element.17), channel_id=1, source_target_pairs={{0,4},{4,0},{1,5},{5,1},{2,6},{6,2},{3,7},{7,3},{8,12},{12,8},{9,1... | collective-permute-start | bytes 983048 | tf_op jit(solution)/shard_map/ppermute | solution.py:31
  53.2 4.1 %collective-permute-start.4 = (bf16[40,2048]{1,0:T(8,128)(2,1)S(1)}, bf16[40,2048]{1,0:T(8,128)(2,1)S(1)}, u32[]{:S(2)}, u32[]{:S(2)}) collective-permute-start(bf16[40,2048]{1,0:T(8,128)(2,1)S(1)} %bitcast.73), channel_id=1, source_target_pairs={{0,4},{4,0},{1,5},{5,1},{2,6},{6,2},{3,7},{7,3},{8,12},{12,8},{9,1... | collective-permute-start | bytes 491528 | tf_op jit(solution)/shard_map/ppermute | solution.py:31
  58.1 4.9 %collective-permute-start.5 = (bf16[80,512]{1,0:T(8,128)(2,1)S(1)}, bf16[80,512]{1,0:T(8,128)(2,1)S(1)}, u32[]{:S(2)}, u32[]{:S(2)}) collective-permute-start(bf16[80,512]{1,0:T(8,128)(2,1)S(1)} %convolution_convert_fusion.1.refs_0_), channel_id=1, source_target_pairs={{0,1},{1,2},{2,3},{3,0},{4,5},{5,6},{6,7},{7,4},{8,9},{9,10},{10,1... | collective-permute-start | bytes 245768 | tf_op jit(solution)/shard_map/ppermute | solution.py:31
  58.6 7.0 %collective-permute-start.6 = (bf16[80,512]{1,0:T(8,128)(2,1)S(1)}, bf16[80,512]{1,0:T(8,128)(2,1)S(1)}, u32[]{:S(2)}, u32[]{:S(2)}) collective-permute-start(bf16[80,512]{1,0:T(8,128)(2,1)S(1)} %convolution_convert_fusion.1.refs_0_), channel_id=1, source_target_pairs={{0,2},{1,3},{2,0},{3,1},{4,6},{5,7},{6,4},{7,5},{8,10},{9,11},{10,... | collective-permute-start | bytes 245768 | tf_op jit(solution)/shard_map/ppermute | solution.py:31
  61.6 4.0 %collective-permute-start.7 = (bf16[80,512]{1,0:T(8,128)(2,1)S(1)}, bf16[80,512]{1,0:T(8,128)(2,1)S(1)}, u32[]{:S(2)}, u32[]{:S(2)}) collective-permute-start(bf16[80,512]{1,0:T(8,128)(2,1)S(1)} %convolution_convert_fusion.1.refs_0_), channel_id=1, source_target_pairs={{0,3},{1,0},{2,1},{3,2},{4,7},{5,4},{6,5},{7,6},{8,11},{9,8},{10,9... | collective-permute-start | bytes 245768 | tf_op jit(solution)/shard_map/ppermute | solution.py:31
  67.0 3.1 %collective-permute-start.8 = (bf16[40,7168]{1,0:T(8,128)(2,1)S(1)}, bf16[40,7168]{1,0:T(8,128)(2,1)S(1)}, u32[]{:S(2)}, u32[]{:S(2)}) collective-permute-start(bf16[40,7168]{1,0:T(8,128)(2,1)S(1)} %get-tuple-element.20), channel_id=1, source_target_pairs={{0,4},{4,0},{1,5},{5,1},{2,6},{6,2},{3,7},{7,3},{8,12},{12,8},{9,1... | collective-permute-start | bytes 1720328 | tf_op jit(solution)/shard_map/ppermute | solution.py:31
  112.7 5.5 %collective-permute-start.9 = (bf16[40,7168]{1,0:T(8,128)(2,1)S(1)}, bf16[40,7168]{1,0:T(8,128)(2,1)S(1)}, u32[]{:S(2)}, u32[]{:S(2)}) collective-permute-start(bf16[40,7168]{1,0:T(8,128)(2,1)S(1)} %bitcast.61), channel_id=1, source_target_pairs={{0,4},{4,0},{1,5},{5,1},{2,6},{6,2},{3,7},{7,3},{8,12},{12,8},{9,1... | collective-permute-start | bytes 1720328 | tf_op jit(solution)/shard_map/ppermute | solution.py:31
  120.6 4.9 %collective-permute-start.10 = (bf16[80,512]{1,0:T(8,128)(2,1)S(1)}, bf16[80,512]{1,0:T(8,128)(2,1)S(1)}, u32[]{:S(2)}, u32[]{:S(2)}) collective-permute-start(bf16[80,512]{1,0:T(8,128)(2,1)S(1)} %again_part.1.refs_0_), channel_id=1, source_target_pairs={{0,1},{1,2},{2,3},{3,0},{4,5},{5,6},{6,7},{7,4},{8,9},{9,10},{10,1... | collective-permute-start | bytes 245768 | tf_op jit(solution)/shard_map/ppermute | solution.py:31
  121.4 6.4 %collective-permute-start.11 = (bf16[80,512]{1,0:T(8,128)(2,1)S(1)}, bf16[80,512]{1,0:T(8,128)(2,1)S(1)}, u32[]{:S(2)}, u32[]{:S(2)}) collective-permute-start(bf16[80,512]{1,0:T(8,128)(2,1)S(1)} %again_part.1.refs_0_), channel_id=1, source_target_pairs={{0,2},{1,3},{2,0},{3,1},{4,6},{5,7},{6,4},{7,5},{8,10},{9,11},{10,... | collective-permute-start | bytes 245768 | tf_op jit(solution)/shard_map/ppermute | solution.py:31
  123.8 4.3 %collective-permute-start.12 = (bf16[80,512]{1,0:T(8,128)(2,1)S(1)}, bf16[80,512]{1,0:T(8,128)(2,1)S(1)}, u32[]{:S(2)}, u32[]{:S(2)}) collective-permute-start(bf16[80,512]{1,0:T(8,128)(2,1)S(1)} %again_part.1.refs_0_), channel_id=1, source_target_pairs={{0,3},{1,0},{2,1},{3,2},{4,7},{5,4},{6,5},{7,6},{8,11},{9,8},{10,9... | collective-permute-start | bytes 245768 | tf_op jit(solution)/shard_map/ppermute | solution.py:31
  128.6 2.6 %collective-permute-start.13 = (f32[40,2048]{1,0:T(8,128)S(1)}, f32[40,2048]{1,0:T(8,128)S(1)}, u32[]{:S(2)}, u32[]{:S(2)}) collective-permute-start(f32[40,2048]{1,0:T(8,128)S(1)} %get-tuple-element.22), channel_id=1, source_target_pairs={{0,4},{4,0},{1,5},{5,1},{2,6},{6,2},{3,7},{7,3},{8,12},{12,8},{9,1... | collective-permute-start | bytes 983048 | tf_op jit(solution)/shard_map/ppermute | solution.py:31
  159.9 4.1 %collective-permute-start.14 = (bf16[40,2048]{1,0:T(8,128)(2,1)S(1)}, bf16[40,2048]{1,0:T(8,128)(2,1)S(1)}, u32[]{:S(2)}, u32[]{:S(2)}) collective-permute-start(bf16[40,2048]{1,0:T(8,128)(2,1)S(1)} %bitcast.64), channel_id=1, source_target_pairs={{0,4},{4,0},{1,5},{5,1},{2,6},{6,2},{3,7},{7,3},{8,12},{12,8},{9,1... | collective-permute-start | bytes 491528 | tf_op jit(solution)/shard_map/ppermute | solution.py:31
  165.0 5.8 %collective-permute-start.15 = (bf16[80,768]{1,0:T(8,128)(2,1)S(1)}, bf16[80,768]{1,0:T(8,128)(2,1)S(1)}, u32[]{:S(2)}, u32[]{:S(2)}) collective-permute-start(bf16[80,768]{1,0:T(8,128)(2,1)S(1)} %fusion.9), channel_id=1, source_target_pairs={{0,1},{1,2},{2,3},{3,0},{4,5},{5,6},{6,7},{7,4},{8,9},{9,10},{10,1... | collective-permute-start | bytes 368648 | tf_op jit(solution)/shard_map/ppermute | solution.py:31
  165.6 8.6 %collective-permute-start.16 = (bf16[80,768]{1,0:T(8,128)(2,1)S(1)}, bf16[80,768]{1,0:T(8,128)(2,1)S(1)}, u32[]{:S(2)}, u32[]{:S(2)}) collective-permute-start(bf16[80,768]{1,0:T(8,128)(2,1)S(1)} %fusion.9), channel_id=1, source_target_pairs={{0,2},{1,3},{2,0},{3,1},{4,6},{5,7},{6,4},{7,5},{8,10},{9,11},{10,... | collective-permute-start | bytes 368648 | tf_op jit(solution)/shard_map/ppermute | solution.py:31
  168.5 5.7 %collective-permute-start.17 = (bf16[80,768]{1,0:T(8,128)(2,1)S(1)}, bf16[80,768]{1,0:T(8,128)(2,1)S(1)}, u32[]{:S(2)}, u32[]{:S(2)}) collective-permute-start(bf16[80,768]{1,0:T(8,128)(2,1)S(1)} %fusion.9), channel_id=1, source_target_pairs={{0,3},{1,0},{2,1},{3,2},{4,7},{5,4},{6,5},{7,6},{8,11},{9,8},{10,9... | collective-permute-start | bytes 368648 | tf_op jit(solution)/shard_map/ppermute | solution.py:31
  176.2 3.2 %collective-permute-start.18 = (bf16[32,80,128]{2,1,0:T(8,128)(2,1)S(1)}, bf16[32,80,128]{2,1,0:T(8,128)(2,1)S(1)}, u32[]{:S(2)}, u32[]{:S(2)}) collective-permute-start(bf16[32,80,128]{2,1,0:T(8,128)(2,1)S(1)} %get-tuple-element.27), channel_id=1, source_target_pairs={{0,4},{4,0},{1,5},{5,1},{2,6},{6,2},{3,7},{7,3},{8,12},{12,8},{9,1... | collective-permute-start | bytes 1966088 | tf_op jit(solution)/shard_map/ppermute | solution.py:31
  180.5 22.9 %all-to-all-start.6 = ((bf16[32,80,128]{2,1,0:T(8,128)(2,1)}), bf16[32,80,128]{2,1,0:T(8,128)(2,1)S(1)}, u32[]{:S(2)}, u32[]{:S(2)}) async-start(bf16[32,80,128]{2,1,0:T(8,128)(2,1)} %add_convert_fusion), calls=%async_computation.6 | async-start | bytes 1310720 | tf_op jit(solution)/shard_map/all_to_all | solution.py:63

commit v3 on v1

v3 whole, which is shorter than its diff:
```python
import functools

import jax
import jax.numpy as jnp
from jax import lax
from jax.experimental import pallas as pl
from jax.experimental.pallas import tpu as pltpu
from jax.sharding import Mesh, PartitionSpec as P

D = 8192
FF = 28672
K = 80
HALF = K // 2
LIVE = 16384
F32 = jnp.float32
BF16 = jnp.bfloat16
CHUNKS = 14
BLOCK = 1024
HOLDS = 8
VMEM = pl.BlockSpec(memory_space=pltpu.VMEM)
SMEM = pl.BlockSpec(memory_space=pltpu.SMEM)
PARAMS = pltpu.CompilerParams(vmem_limit_bytes=16 << 20)


def dot(left, right, contract):
    return lax.dot_general(left, right, (contract, ((), ())), preferred_element_type=F32)


def shifted(value, axis, size, step):
    return lax.ppermute(value, axis, [(i, (i + step) % size) for i in range(size)])


def sibling(value):
    return shifted(value, "c", 2, 1)


def y_pieces(sent):
    return [sent] + [shifted(sent, "y", 4, step) for step in (1, 2, 3)]


def to_tiles(array):
    rows, cols = array.shape
    tiles = array.reshape(rows // 8, 8, cols // 128, 128).transpose(0, 2, 1, 3)
    return tiles.reshape(-1, 8, 128)


def from_tiles(tiles, rows, cols):
    split = tiles.reshape(rows // 8, cols // 128, 8, 128).transpose(0, 2, 1, 3)
    return split.reshape(rows, cols)


def exchange(pieces, axes):
    return lax.all_to_all(pieces, axes, 0, 0, tiled=True)


def spread(piece, axes, count):
    return exchange(jnp.broadcast_to(piece[None], (count,) + piece.shape), axes)


def chips_sum(part, scale):
    rows, cols = part.shape
    tiles = to_tiles(part)
    count = tiles.shape[0]
    per = -(-count // 32)
    tiles = jnp.pad(tiles, ((0, 32 * per - count), (0, 0), (0, 0)))
    pieces = tiles.reshape(32, per, 8, 128)
    mine = (exchange(pieces, ("z", "x")).astype(F32).sum(0) * scale).astype(BF16)
    whole = spread(mine, ("z", "x"), 32).reshape(32 * per, 8, 128)[:count]
    return from_tiles(whole, rows, cols)


def cost(big):
    rows, cols = big.shape
    return pl.CostEstimate(
        flops=4 * HALF * rows * cols, bytes_accessed=4 * rows * cols, transcendentals=0
    )


def in_vmem(array):
    return pltpu.with_memory_space_constraint(array, pltpu.VMEM)


def hold_kernel(given_ref, held_ref, sems):
    rows = given_ref.shape[0] // HOLDS
    copies = []
    for k in range(HOLDS):
        part = pl.ds(k * rows, rows)
        copy = pltpu.make_async_copy(given_ref.at[part], held_ref.at[part], sems.at[k])
        copy.start()
        copies.append(copy)
    for copy in copies:
        copy.wait()


def hold(given):
    given = pltpu.with_memory_space_constraint(given, pltpu.HBM)
    return pl.pallas_call(
        hold_kernel,
        out_shape=pltpu.VMEM(given.shape, given.dtype),
        in_specs=[pl.BlockSpec(memory_space=pl.ANY)],
        out_specs=VMEM,
        scratch_shapes=[pltpu.SemaphoreType.DMA((HOLDS,))],
        compiler_params=PARAMS,
        cost_estimate=pl.CostEstimate(
            flops=0, bytes_accessed=4 * given.size, transcendentals=0
        ),
        name="hold",
    )(given)


def load_kernel(
    place_ref, test_ref, grads_ref, kept_ref, sent_ref, held_ref, test_held, sems, test_sems
):
    width = grads_ref.shape[1] // CHUNKS
    copies = []
    for k in range(CHUNKS):
        cols = pl.ds(k * width, width)
        first = pltpu.make_async_copy(
            test_ref.at[:, cols], test_held.at[:, cols], test_sems.at[k]
        )
        second = pltpu.make_async_copy(
            grads_ref.at[:, cols], held_ref.at[:, cols], sems.at[k]
        )
        first.start()
        second.start()
        copies.append((first, second))
    total = None
    for k in range(CHUNKS):
        cols = pl.ds(k * width, width)
        copies[k][0].wait()
        copies[k][1].wait()
        step = dot(test_held[:, cols], held_ref[:, cols], ((1,), (1,)))
        total = step if total is None else total + step
    first = place_ref[1] == 0
    kept_ref[...] = jnp.where(first, total[:HALF], total[HALF:]).astype(BF16)
    sent_ref[...] = jnp.where(first, total[HALF:], total[:HALF]).astype(BF16)


def load_and_sketch(place, test_t, grads):
    rows, cols = grads.shape
    test_t = pltpu.with_memory_space_constraint(test_t, pltpu.HBM)
    grads = pltpu.with_memory_space_constraint(grads, pltpu.HBM)
    part = jax.ShapeDtypeStruct((HALF, rows), BF16)
    return pl.pallas_call(
        load_kernel,
        out_shape=(part, part, pltpu.VMEM((rows, cols), BF16)),
        in_specs=[SMEM] + [pl.BlockSpec(memory_space=pl.ANY)] * 2,
        out_specs=(VMEM,) * 3,
        scratch_shapes=[
            pltpu.VMEM((K, cols), BF16),
            pltpu.SemaphoreType.DMA((CHUNKS,)),
            pltpu.SemaphoreType.DMA((CHUNKS,)),
        ],
        compiler_params=PARAMS,
        cost_estimate=cost(grads),
        name="load_and_sketch",
    )(place, test_t, grads)


def summed_small(place_ref, refs, scale):
    total = refs[0][...].astype(F32)
    for ref in refs[1:]:
        total = total + ref[...].astype(F32)
    rows = total.shape[1] // 2
    slot = lax.broadcasted_iota(jnp.int32, total.shape, 1)
    own = slot < place_ref[2]
    other = (slot >= rows) & (slot < place_ref[3] + rows)
    return jnp.where(own | other, total * scale, 0.0).astype(BF16)


def token_kernel(scale, place_ref, *refs):
    own_ref, other_ref, part_ref = refs[-3:]
    small = summed_small(place_ref, refs[:-3], scale)
    rows = own_ref.shape[0]
    for k in range(own_ref.shape[1] // BLOCK):
        cols = slice(k * BLOCK, (k + 1) * BLOCK)
        out = dot(small[:, :rows], own_ref[:, cols], ((1,), (0,)))
        out = out + dot(small[:, rows:], other_ref[:, cols], ((1,), (0,)))
        part_ref[:, cols] = out.astype(BF16)


def token_part(place, pieces, own, other, scale):
    return pl.pallas_call(
        functools.partial(token_kernel, scale),
        out_shape=jax.ShapeDtypeStruct((HALF, own.shape[1]), BF16),
        in_specs=[SMEM] + [VMEM] * (len(pieces) + 2),
        out_specs=VMEM,
        compiler_params=PARAMS,
        cost_estimate=cost(own),
        name="token_part",
    )(place, *pieces, in_vmem(own), in_vmem(other))


def feature_kernel(small_ref, own_ref, other_ref, part_ref):
    rows = own_ref.shape[0]
    for at, big_ref in ((0, own_ref), (rows, other_ref)):
        total = None
        for k in range(big_ref.shape[1] // BLOCK):
            cols = slice(k * BLOCK, (k + 1) * BLOCK)
            step = dot(small_ref[:, cols], big_ref[:, cols], ((1,), (1,)))
            total = step if total is None else total + step
        part_ref[:, at : at + rows] = total.astype(BF16)


def feature_part(small, own, other):
    return pl.pallas_call(
        feature_kernel,
        out_shape=jax.ShapeDtypeStruct((HALF, 2 * own.shape[0]), BF16),
        in_specs=[VMEM] * 3,
        out_specs=VMEM,
        compiler_params=PARAMS,
        cost_estimate=cost(own),
        name="feature_part",
    )(small, in_vmem(own), in_vmem(other))


def up_kernel(place_ref, *refs):
    own_ref, other_ref, part_ref, gram_ref = refs[-4:]
    rows = own_ref.shape[0]
    pieces = [ref.at[:, : 2 * rows] for ref in refs[:-4]]
    small = summed_small(place_ref, pieces, 1.0)
    gram = None
    for ref in refs[:-4]:
        high = ref[:, 2 * rows : 2 * rows + 128].astype(F32)
        low = ref[:, 2 * rows + 128 : 2 * rows + 256].astype(F32)
        gram = high + low if gram is None else gram + (high + low)
    gram_ref[...] = gram
    width = own_ref.shape[1] // 32
    lane = lax.broadcasted_iota(jnp.int32, (HALF, 256), 1)
    high = (place_ref[2] // 32 + place_ref[3] // 32).astype(F32)
    low = (place_ref[2] % 32 + place_ref[3] % 32).astype(F32)
    digits = jnp.where(lane == width, high, jnp.where(lane == width + 1, low, 0.0))
    tail = digits.astype(BF16)[:, width:]
    for z in range(8):
        cols = slice(4 * z * width, 4 * (z + 1) * width)
        out = dot(small[:, :rows], own_ref[:, cols], ((1,), (0,)))
        out = out + dot(small[:, rows:], other_ref[:, cols], ((1,), (0,)))
        out = out.astype(BF16)
        for x in range(4):
            piece = out[:, x * width : (x + 1) * width]
            part_ref[4 * z + x] = jnp.concatenate([piece, tail], 1)


def up_part(place, pieces, own, other):
    return pl.pallas_call(
        up_kernel,
        out_shape=(
            jax.ShapeDtypeStruct((32, HALF, 256), BF16),
            jax.ShapeDtypeStruct((HALF, 128), F32),
        ),
        in_specs=[SMEM] + [VMEM] * (len(pieces) + 2),
        out_specs=(VMEM, VMEM),
        compiler_params=PARAMS,
        cost_estimate=cost(own),
        name="up_part",
    )(place, *pieces, in_vmem(own), in_vmem(other))


def split_kernel(place_ref, pieces_ref, kept_ref, sent_ref):
    owned = kept_ref.shape[1] - 16
    total = pieces_ref[0].astype(F32)
    for k in range(1, pieces_ref.shape[0]):
        total = total + pieces_ref[k].astype(F32)
    tail = total[:, 2 * owned : 2 * owned + 16]
    first = jnp.concatenate([total[:, :owned], tail], 1)
    second = total[:, owned : 2 * owned + 16]
    mine = place_ref[1] == 0
    kept_ref[...] = jnp.where(mine, first, second)
    sent_ref[...] = jnp.where(mine, second, first)


def split_up(place, pieces, owned):
    shape = jax.ShapeDtypeStruct((HALF, owned + 16), F32)
    return pl.pallas_call(
        split_kernel,
        out_shape=(shape, shape),
        in_specs=[SMEM, VMEM],
        out_specs=(VMEM, VMEM),
        compiler_params=PARAMS,
        name="split_up",
    )(place, pieces)


def finish_kernel(place_ref, kept_ref, came_ref, inverse_ref, up_ref):
    owned = up_ref.shape[1]
    kept, came = kept_ref[...], came_ref[...]
    high, low = kept[:1, owned : owned + 1], kept[:1, owned + 1 : owned + 2]
    inv_root = lax.rsqrt(32.0 * high + low)
    mine = place_ref[1] == 0
    total = jnp.concatenate([jnp.where(mine, kept, came), jnp.where(mine, came, kept)], 0)
    up = lax.dot_general(
        inverse_ref[...],
        total,
        (((1,), (0,)), ((), ())),
        precision=lax.Precision.HIGHEST,
        preferred_element_type=F32,
    )
    up_ref[...] = (inv_root * up)[:, :owned]


def finish_up(place, kept, came, inverse, owned):
    return pl.pallas_call(
        finish_kernel,
        out_shape=jax.ShapeDtypeStruct((K, owned), F32),
        in_specs=[SMEM] + [VMEM] * 3,
        out_specs=VMEM,
        compiler_params=PARAMS,
        name="finish_up",
    )(place, kept, came, inverse)


def both_halves(first, own, other):
    return jnp.where(
        first, jnp.concatenate([own, other], 0), jnp.concatenate([other, own], 0)
    )


def aligned(block):
    return jnp.pad(block, ((0, 0), (0, 128 - block.shape[1])))


def local(tokens, out_grads, test_matrix, slot_counts):
    spots = jnp.stack([lax.axis_index(("z", "x", "c")), lax.axis_index("c")])
    place = jnp.concatenate([spots, slot_counts, sibling(slot_counts)])
    scale = LIVE ** -0.5
    width = tokens.shape[1] // 64

    kept, sent, grads = load_and_sketch(spots, test_matrix.T, out_grads)
    sketch_part = jnp.concatenate([kept, sibling(sent)], 1)
    other_tokens, sketch_part = lax.optimization_barrier((sibling(tokens), sketch_part))
    sent_grads, sketch_part = lax.optimization_barrier((out_grads, sketch_part))
    other_grads = sibling(sent_grads)
    other_tokens = hold(other_tokens)

    ranged = chips_sum(
        token_part(place, y_pieces(sketch_part), tokens, other_tokens, 1.0), scale
    )
    back_part = feature_part(ranged, tokens, other_tokens)
    other_grads, back_part = lax.optimization_barrier((other_grads, back_part))
    back = y_pieces(back_part)
    other_grads = hold(other_grads)
    transposed = chips_sum(
        token_part(place, back, grads, other_grads, D ** -0.5), scale
    )
    again = y_pieces(feature_part(transposed, grads, other_grads))
    whole_range = chips_sum(
        token_part(place, again, tokens, other_tokens, FF ** -0.5), scale
    )

    other_range = sibling(whole_range)
    both = jnp.concatenate([whole_range, other_range], 0)
    gram_part = dot(whole_range, both, ((1,), (1,)))
    high = gram_part.astype(BF16)
    low = (gram_part - high.astype(F32)).astype(BF16)
    projected = feature_part(whole_range, tokens, other_tokens)
    joined = y_pieces(jnp.concatenate([projected, aligned(high), aligned(low)], 1))

    up, gram_rows = up_part(place, joined, grads, other_grads)
    up_pieces = exchange(up, ("z", "x"))
    gram_rows, place = lax.optimization_barrier((gram_rows, place))
    gram_rows = gram_rows[:, :K]
    first = place[1] == 0
    other_rows = sibling(gram_rows)
    other_rows = jnp.roll(other_rows, HALF, 1)
    gram = both_halves(first, gram_rows, other_rows)
    gram = jnp.where(first, gram, jnp.roll(gram, HALF, 1))
    lower = jnp.linalg.cholesky(gram)
    inverse = lax.linalg.triangular_solve(
        lower, jnp.eye(K, dtype=F32), left_side=True, lower=True
    )

    owned = out_grads.shape[1] // 64
    kept_up, sent_up = split_up(place, up_pieces, owned)
    adapter_up = finish_up(place, kept_up, sibling(sent_up), inverse, owned).T

    own = both_halves(first, whole_range, other_range)
    own = lax.dynamic_slice_in_dim(own, place[0] * width, width, 1).astype(F32)
    adapter_down = jnp.dot(inverse, own, precision=lax.Precision.HIGHEST).T * D ** 0.5
    return adapter_down, adapter_up


def solution(mesh):
    split = Mesh(mesh.devices.reshape(8, 4, 2, 4), ("z", "x", "c", "y"))
    dp = ("z", "x", "c")
    placed = (P(dp, "y"), P(dp, "y"), P("y", None), P(dp))
    return jax.shard_map(
        local,
        mesh=split,
        in_specs=placed,
        out_specs=(P(("y",) + dp, None), P(("y",) + dp, None)),
        check_vma=False,
    )
```

time: 242 us -> 201 us (0.83)
  Pallas kernels: 0 us -> 28.9 us
  matrix products: 26 us -> 1.34 us
  waiting for transfers between devices: 37.8 us -> 19.8 us
  blocking collectives: 114 us -> 102 us
  local copies, waits for them, and re-layouts: 10.5 us -> 2.45 us
  other arithmetic: 19.2 us -> 15.9 us
  starting transfers between devices: 29.8 us -> 27.3 us
    pallas_call x0 -> x12, Pallas kernels: none -> 28.9 us  [the longest x3 7.21 us: feature_part(): pl.pallas_call(feature_kernel, out_shape=jax.ShapeDtypeStruct((HALF, 2 *...]
    dot_general x9 -> x1, matrix products: 24.1 us -> 0.22 us  [dot(): lax.dot_general(left, right, (contract, ((), ())), preferred_element_type...]
    all_to_all x7 -> x6, blocking collectives: 114 us -> 102 us  [exchange(): return lax.all_to_all(pieces, axes, 0, 0, tiled=True)]
    ppermute x18 -> x19, waiting for transfers between devices: 27.6 us -> 16.1 us  [shifted(): lax.ppermute(value, axis, [(i, (i + step) % size) for i in range(size)])]
    all_to_all x2 -> x1, waiting for transfers between devices: 10.2 us -> 3.79 us  [exchange(): return lax.all_to_all(pieces, axes, 0, 0, tiled=True)]
    reshape x2 -> x0, local copies, waits for them, and re-layouts: 5.81 us -> none  [local(): up_part = up_part.reshape(K, 32, 2, owned).transpose(2, 1, 0, 3)]
    all_to_all x2 -> x1, starting transfers between devices: 8.83 us -> 3.91 us  [exchange(): return lax.all_to_all(pieces, axes, 0, 0, tiled=True)]
    convert_element_type x5 -> x3, other arithmetic: 3.4 us -> 0.02 us  [chips_sum(): (exchange(pieces, ('z', 'x')).astype(F32).sum(0) * scale).astype(BF16)]
  transfers between devices with their start and end apart: 20 -> 20, of which waited for: 17 -> 11; matrix products, arithmetic and copies ran while one was open for 7% -> 9% of each run, Pallas kernels for 0% -> 7%
where the time goes in v3:
time: 201 us
  blocking collectives  102 us (51%)
  Pallas kernels  28.9 us (14%)
  starting transfers between devices  27.3 us (14%)
  waiting for transfers between devices  19.8 us (10%)
  other arithmetic  15.9 us (8%)
  between operations  3.04 us (2%)
  local copies, waits for them, and re-layouts  2.45 us (1%)
    all_to_all x6, blocking collectives, exchange(): return lax.all_to_all(pieces, axes, 0, 0, tiled=True)  102 us
    ppermute x19, starting transfers between devices, shifted(): lax.ppermute(value, axis, [(i, (i + step) % size) for i in range(size)])  23.4 us
    ppermute x19, waiting for transfers between devices, shifted(): lax.ppermute(value, axis, [(i, (i + step) % size) for i in range(size)])  16.1 us
    another operation x3, other arithmetic, local(): lower = jnp.linalg.cholesky(gram)  7.98 us
    pallas_call x3, Pallas kernels, feature_part(): pl.pallas_call(feature_kernel, out_shape=jax.ShapeDtypeStruct((HALF, 2 *...  7.21 us
    another operation x2, other arithmetic, local(): lax.linalg.triangular_solve(lower, jnp.eye(K, dtype=F32), left_side=True,...  6.78 us
    pallas_call x3, Pallas kernels, token_part(): pl.pallas_call(functools.partial(token_kernel, scale), out_shape=jax.Shap...  5.89 us
    pallas_call x1, Pallas kernels, load_and_sketch(): pl.pallas_call(load_kernel, out_shape=(part, part, pltpu.VMEM((rows, cols...  4.89 us
  transfers between devices with their start and end apart: 20, of which 11 were waited for; matrix products, arithmetic and copies ran while one was open for 9% of the time, Pallas kernels for 7%

profile of v3, /device:TPU:1, one launch (start us, length us, event | category | flops | bytes accessed | tf_op | source)
XLA Modules:
  0.0 200.6 jit_solution(14031943277731712724)
XLA Ops:
  0.6 3.3 %collective-permute-start.1 = (bf16[512,2048]{1,0:T(8,128)(2,1)}, bf16[512,2048]{1,0:T(8,128)(2,1)S(1)}, u32[]{:S(2)}, u32[]{:S(2)}) collective-permute-start(bf16[512,2048]{1,0:T(8,128)(2,1)} %own_ref.3), channel_id=1, source_target_pairs={{0,4},{4,0},{1,5},{5,1},{2,6},{6,2},{3,7},{7,3},{8,12},{12,8},{9,1... | collective-permute-start | bytes 6291464 | tf_op jit(solution)/shard_map/ppermute | solution.py:30
  4.0 4.9 %load_and_sketch.1 = (bf16[40,512]{1,0:T(8,128)(2,1)S(1)}, bf16[40,512]{1,0:T(8,128)(2,1)S(1)}, bf16[512,7168]{1,0:T(8,128)(2,1)S(1)}) custom-call(s32[2]{0:T(128)S(1)} %pad_add_fusion.1.place_ref, bf16[80,7168]{1,0:T(8,128)(2,1)} %bitcast.64, bf16[512,7168]{1,0:T(8,128)(2,1)} %grads_ref.1), custom_call_target="tpu_custom_call" | custom-call | flops 587202560 | bytes 14680064 | tf_op jit(solution)/shard_map/load_and_sketch/pallas_call | solution.py:144
  15.7 1.7 hold.2.refs_5_.other_ref
  17.5 2.7 %collective-permute-done.4.refs_1_ = bf16[40,1024]{1,0:T(8,128)(2,1)S(1)} collective-permute-done((bf16[40,1024]{1,0:T(8,128)(2,1)S(1)}, bf16[40,1024]{1,0:T(8,128)(2,1)S(1)}, u32[]{:S(2)}, u32[]{:S(2)}) %collective-permute-start.4) | collective-permute-done | bytes 81952 | tf_op jit(solution)/shard_map/ppermute | solution.py:30
  21.7 20.7 %all_to_all.35 = bf16[32,3,8,128]{3,2,1,0:T(8,128)(2,1)S(1)} all-to-all(bf16[32,3,8,128]{3,2,1,0:T(8,128)(2,1)S(1)} %bitcast.66), channel_id=1, replica_groups=mesh['z'=8,'x'=4,'c'=2,'y'=4] {'z','x'}, dimensions={0} | all-to-all | bytes 393216 | tf_op jit(solution)/shard_map/all_to_all | solution.py:53
  42.5 14.3 %all_to_all.36 = bf16[32,3,8,128]{3,2,1,0:T(8,128)(2,1)S(1)} all-to-all(bf16[32,3,8,128]{3,2,1,0:T(8,128)(2,1)S(1)} %broadcast_in_dim.7), channel_id=1, replica_groups=mesh['z'=8,'x'=4,'c'=2,'y'=4] {'z','x'}, dimensions={0} | all-to-all | bytes 393216 | tf_op jit(solution)/shard_map/all_to_all | solution.py:53
  61.1 3.2 %hold.3.refs_5_.other_ref = bf16[512,7168]{1,0:T(8,128)(2,1)S(1)} custom-call(bf16[512,7168]{1,0:T(8,128)(2,1)} %copy-done.1), custom_call_target="tpu_custom_call" | custom-call | bytes 14680064 | tf_op jit(solution)/shard_map/hold/pallas_call | solution.py:97
  64.3 3.2 %token_part.4 = bf16[40,7168]{1,0:T(8,128)(2,1)S(1)} custom-call(s32[4]{0:T(128)S(1)} %pad_add_fusion.place_ref, bf16[40,1024]{1,0:T(8,128)(2,1)S(1)} %feature_part.3.refs_0_, bf16[40,1024]{1,0:T(8,128)(2,1)S(1)} %collective-permute-done.7.refs_1_, bf16[40,1024]{1,0:T(8,128)(2,1)S(1)} %collective-permute-done.8.refs_2_, ...), custom_call_target="tpu_custom_call" | custom-call | flops 587202560 | bytes 14680064 | tf_op jit(solution)/shard_map/token_part/pallas_call | solution.py:183
  67.6 17.8 %all_to_all.37 = bf16[32,9,8,128]{3,2,1,0:T(8,128)(2,1)S(1)} all-to-all(bf16[32,9,8,128]{3,2,1,0:T(8,128)(2,1)S(1)} %bitcast.62), channel_id=1, replica_groups=mesh['z'=8,'x'=4,'c'=2,'y'=4] {'z','x'}, dimensions={0} | all-to-all | bytes 1179648 | tf_op jit(solution)/shard_map/all_to_all | solution.py:53
  85.5 19.6 %all_to_all.38 = bf16[32,9,8,128]{3,2,1,0:T(8,128)(2,1)S(1)} all-to-all(bf16[32,9,8,128]{3,2,1,0:T(8,128)(2,1)S(1)} %broadcast_in_dim.8), channel_id=1, replica_groups=mesh['z'=8,'x'=4,'c'=2,'y'=4] {'z','x'}, dimensions={0} | all-to-all | bytes 1179648 | tf_op jit(solution)/shard_map/all_to_all | solution.py:53
  105.2 4.5 %feature_part.4.refs_0_ = bf16[40,1024]{1,0:T(8,128)(2,1)S(1)} custom-call(bf16[40,7168]{1,0:T(8,128)(2,1)S(1)} %bitcast.54, bf16[512,7168]{1,0:T(8,128)(2,1)S(1)} %get-tuple-element.24.refs_4_.own_ref, bf16[512,7168]{1,0:T(8,128)(2,1)S(1)} %hold.3.refs_5_.other_ref), custom_call_target="tpu_custom_call" | custom-call | flops 587202560 | bytes 14680064 | tf_op jit(solution)/shard_map/feature_part/pallas_call | solution.py:206
  110.7 1.5 collective-permute-start.11
  113.1 2.4 %collective-permute-done.11.refs_2_ = bf16[40,1024]{1,0:T(8,128)(2,1)S(1)} collective-permute-done((bf16[40,1024]{1,0:T(8,128)(2,1)S(1)}, bf16[40,1024]{1,0:T(8,128)(2,1)S(1)}, u32[]{:S(2)}, u32[]{:S(2)}) %collective-permute-start.11) | collective-permute-done | bytes 81952 | tf_op jit(solution)/shard_map/ppermute | solution.py:30
  118.1 16.3 %all_to_all.39 = bf16[32,3,8,128]{3,2,1,0:T(8,128)(2,1)S(1)} all-to-all(bf16[32,3,8,128]{3,2,1,0:T(8,128)(2,1)S(1)} %bitcast.65), channel_id=1, replica_groups=mesh['z'=8,'x'=4,'c'=2,'y'=4] {'z','x'}, dimensions={0} | all-to-all | bytes 393216 | tf_op jit(solution)/shard_map/all_to_all | solution.py:53
  134.4 13.1 %all_to_all.40 = bf16[32,3,8,128]{3,2,1,0:T(8,128)(2,1)S(1)} all-to-all(bf16[32,3,8,128]{3,2,1,0:T(8,128)(2,1)S(1)} %broadcast_in_dim.9), channel_id=1, replica_groups=mesh['z'=8,'x'=4,'c'=2,'y'=4] {'z','x'}, dimensions={0} | all-to-all | bytes 393216 | tf_op jit(solution)/shard_map/all_to_all | solution.py:53
  147.5 8.9 %collective-permute-start.13 = (bf16[40,2048]{1,0:T(8,128)(2,1)S(1)}, bf16[40,2048]{1,0:T(8,128)(2,1)S(1)}, u32[]{:S(2)}, u32[]{:S(2)}) collective-permute-start(bf16[40,2048]{1,0:T(8,128)(2,1)S(1)} %bitcast.55), channel_id=1, source_target_pairs={{0,4},{4,0},{1,5},{5,1},{2,6},{6,2},{3,7},{7,3},{8,12},{12,8},{9,1... | collective-permute-start | bytes 491528 | tf_op jit(solution)/shard_map/ppermute | solution.py:30
  159.8 2.7 %collective-permute-done.16.refs_3_ = bf16[40,1280]{1,0:T(8,128)(2,1)S(1)} collective-permute-done((bf16[40,1280]{1,0:T(8,128)(2,1)S(1)}, bf16[40,1280]{1,0:T(8,128)(2,1)S(1)}, u32[]{:S(2)}, u32[]{:S(2)}) %collective-permute-start.16) | collective-permute-done | bytes 102432 | tf_op jit(solution)/shard_map/ppermute | solution.py:30
  162.6 1.5 collective-permute-done.15.refs_2_
  164.0 2.8 %collective-permute-done.14.refs_1_ = bf16[40,1280]{1,0:T(8,128)(2,1)S(1)} collective-permute-done((bf16[40,1280]{1,0:T(8,128)(2,1)S(1)}, bf16[40,1280]{1,0:T(8,128)(2,1)S(1)}, u32[]{:S(2)}, u32[]{:S(2)}) %collective-permute-start.14) | collective-permute-done | bytes 102432 | tf_op jit(solution)/shard_map/ppermute | solution.py:30
  166.8 3.9 %up_part.1 = (bf16[32,40,256]{2,1,0:T(8,128)(2,1)}, f32[40,128]{1,0:T(8,128)S(1)}) custom-call(s32[4]{0:T(128)S(1)} %pad_add_fusion.place_ref, bf16[40,1280]{1,0:T(8,128)(2,1)S(1)} %fusion.5.refs_0_, bf16[40,1280]{1,0:T(8,128)(2,1)S(1)} %collective-permute-done.14.refs_1_, bf16[40,1280]{1,0:T(8,128)(2,1)S(1)} %collective-permute-done.15.refs_2_, ...), custom_call_target="tpu_custom_call" | custom-call | flops 587202560 | bytes 14680064 | tf_op jit(solution)/shard_map/up_part/pallas_call | solution.py:245
  172.6 3.9 %all-to-all-start.6 = ((bf16[32,40,256]{2,1,0:T(8,128)(2,1)}), bf16[32,40,256]{2,1,0:T(8,128)(2,1)S(1)}, u32[]{:S(2)}, u32[]{:S(2)}) async-start(bf16[32,40,256]{2,1,0:T(8,128)(2,1)} %get-tuple-element.29), calls=%async_computation.6 | async-start | bytes 1310720 | tf_op jit(solution)/shard_map/all_to_all | solution.py:53
  177.5 7.3 %cholesky.17 = f32[80,80]{1,0:T(8,128)S(1)} custom-call(f32[80,80]{1,0:T(8,128)S(1)} %fusion.9), custom_call_target="Cholesky" | custom-call | tf_op jit(solution)/shard_map/jit(cholesky)/cholesky | solution.py:367
  186.1 6.1 %custom-call.6 = f32[1,80,80]{1,2,0:T(8,128)S(1)} custom-call(f32[1,80,80]{2,1,0:T(8,128)S(1)} %fusion.6), custom_call_target="InvertDiagBlocksLowerTriangular" | custom-call | tf_op jit(solution)/shard_map/triangular_solve | solution.py:368
  192.5 3.8 %all-to-all-done.6.pieces_ref = bf16[32,40,256]{2,1,0:T(8,128)(2,1)S(1)} async-done(((bf16[32,40,256]{2,1,0:T(8,128)(2,1)}), bf16[32,40,256]{2,1,0:T(8,128)(2,1)S(1)}, u32[]{:S(2)}, u32[]{:S(2)}) %all-to-all-start.6) | async-done | bytes 655392 | tf_op jit(solution)/shard_map/all_to_all | solution.py:53
  (78 shorter events, 27.5 us)
Async XLA Ops:
  0.6 9.6 %collective-permute-start.1 = (bf16[512,2048]{1,0:T(8,128)(2,1)}, bf16[512,2048]{1,0:T(8,128)(2,1)S(1)}, u32[]{:S(2)}, u32[]{:S(2)}) collective-permute-start(bf16[512,2048]{1,0:T(8,128)(2,1)} %own_ref.3), channel_id=1, source_target_pairs={{0,4},{4,0},{1,5},{5,1},{2,6},{6,2},{3,7},{7,3},{8,12},{12,8},{9,1... | collective-permute-start | bytes 6291464 | tf_op jit(solution)/shard_map/ppermute | solution.py:30
  4.0 6.2 %copy-start.2 = (bf16[512,7168]{1,0:T(8,128)(2,1)S(1)}, bf16[512,7168]{1,0:T(8,128)(2,1)}, u32[]{:S(2)}) copy-start(bf16[512,7168]{1,0:T(8,128)(2,1)} %grads_ref.1) | copy-start | bytes 22020100
  8.9 1.3 collective-permute-start.2
  10.3 5.4 %copy-start.3 = (bf16[512,2048]{1,0:T(8,128)(2,1)}, bf16[512,2048]{1,0:T(8,128)(2,1)S(1)}, u32[]{:S(2)}) copy-start(bf16[512,2048]{1,0:T(8,128)(2,1)S(1)} %collective-permute-done.1.given_ref) | copy-start | bytes 6291460
  10.3 47.9 %collective-permute-start.3 = (bf16[512,7168]{1,0:T(8,128)(2,1)S(1)}, bf16[512,7168]{1,0:T(8,128)(2,1)S(1)}, u32[]{:S(2)}, u32[]{:S(2)}) collective-permute-start(bf16[512,7168]{1,0:T(8,128)(2,1)S(1)} %copy-done.2), channel_id=1, source_target_pairs={{0,4},{4,0},{1,5},{5,1},{2,6},{6,2},{3,7},{7,3},{8,12},{12,8},{9,1... | collective-permute-start | bytes 22020104 | tf_op jit(solution)/shard_map/ppermute | solution.py:30
  10.5 4.4 %collective-permute-start = (s32[1]{0:T(128)}, s32[1]{0:T(128)}, u32[]{:S(2)}, u32[]{:S(2)}) collective-permute-start(s32[1]{0:T(128)} %param.7), channel_id=1, source_target_pairs={{0,4},{4,0},{1,5},{5,1},{2,6},{6,2},{3,7},{7,3},{8,12},{12,8},{9,1... | collective-permute-start | bytes 20 | tf_op jit(solution)/shard_map/ppermute | solution.py:30
  11.6 5.9 %collective-permute-start.6 = (bf16[40,1024]{1,0:T(8,128)(2,1)S(1)}, bf16[40,1024]{1,0:T(8,128)(2,1)S(1)}, u32[]{:S(2)}, u32[]{:S(2)}) collective-permute-start(bf16[40,1024]{1,0:T(8,128)(2,1)S(1)} %pad_maximum_fusion.2.refs_0_), channel_id=1, source_target_pairs={{0,3},{1,0},{2,1},{3,2},{4,7},{5,4},{6,5},{7,6},{8,11},{9,8},{10,9... | collective-permute-start | bytes 245768 | tf_op jit(solution)/shard_map/ppermute | solution.py:30
  12.6 4.9 %collective-permute-start.5 = (bf16[40,1024]{1,0:T(8,128)(2,1)S(1)}, bf16[40,1024]{1,0:T(8,128)(2,1)S(1)}, u32[]{:S(2)}, u32[]{:S(2)}) collective-permute-start(bf16[40,1024]{1,0:T(8,128)(2,1)S(1)} %pad_maximum_fusion.2.refs_0_), channel_id=1, source_target_pairs={{0,2},{1,3},{2,0},{3,1},{4,6},{5,7},{6,4},{7,5},{8,10},{9,11},{10,... | collective-permute-start | bytes 245768 | tf_op jit(solution)/shard_map/ppermute | solution.py:30
  13.0 7.3 %collective-permute-start.4 = (bf16[40,1024]{1,0:T(8,128)(2,1)S(1)}, bf16[40,1024]{1,0:T(8,128)(2,1)S(1)}, u32[]{:S(2)}, u32[]{:S(2)}) collective-permute-start(bf16[40,1024]{1,0:T(8,128)(2,1)S(1)} %pad_maximum_fusion.2.refs_0_), channel_id=1, source_target_pairs={{0,1},{1,2},{2,3},{3,0},{4,5},{5,6},{6,7},{7,4},{8,9},{9,10},{10,1... | collective-permute-start | bytes 245768 | tf_op jit(solution)/shard_map/ppermute | solution.py:30
  15.7 4.6 %copy-start = (bf16[512,2048]{1,0:T(8,128)(2,1)S(1)}, bf16[512,2048]{1,0:T(8,128)(2,1)}, u32[]{:S(2)}) copy-start(bf16[512,2048]{1,0:T(8,128)(2,1)} %own_ref.3) | copy-start | bytes 6291460
  58.2 2.9 %copy-start.1 = (bf16[512,7168]{1,0:T(8,128)(2,1)}, bf16[512,7168]{1,0:T(8,128)(2,1)S(1)}, u32[]{:S(2)}) copy-start(bf16[512,7168]{1,0:T(8,128)(2,1)S(1)} %collective-permute-done.3.given_ref) | copy-start | bytes 22020100
  58.2 6.1 %collective-permute-start.9 = (bf16[40,1024]{1,0:T(8,128)(2,1)S(1)}, bf16[40,1024]{1,0:T(8,128)(2,1)S(1)}, u32[]{:S(2)}, u32[]{:S(2)}) collective-permute-start(bf16[40,1024]{1,0:T(8,128)(2,1)S(1)} %feature_part.3.refs_0_), channel_id=1, source_target_pairs={{0,3},{1,0},{2,1},{3,2},{4,7},{5,4},{6,5},{7,6},{8,11},{9,8},{10,9... | collective-permute-start | bytes 245768 | tf_op jit(solution)/shard_map/ppermute | solution.py:30
  58.3 6.0 %collective-permute-start.8 = (bf16[40,1024]{1,0:T(8,128)(2,1)S(1)}, bf16[40,1024]{1,0:T(8,128)(2,1)S(1)}, u32[]{:S(2)}, u32[]{:S(2)}) collective-permute-start(bf16[40,1024]{1,0:T(8,128)(2,1)S(1)} %feature_part.3.refs_0_), channel_id=1, source_target_pairs={{0,2},{1,3},{2,0},{3,1},{4,6},{5,7},{6,4},{7,5},{8,10},{9,11},{10,... | collective-permute-start | bytes 245768 | tf_op jit(solution)/shard_map/ppermute | solution.py:30
  58.4 5.9 %collective-permute-start.7 = (bf16[40,1024]{1,0:T(8,128)(2,1)S(1)}, bf16[40,1024]{1,0:T(8,128)(2,1)S(1)}, u32[]{:S(2)}, u32[]{:S(2)}) collective-permute-start(bf16[40,1024]{1,0:T(8,128)(2,1)S(1)} %feature_part.3.refs_0_), channel_id=1, source_target_pairs={{0,1},{1,2},{2,3},{3,0},{4,5},{5,6},{6,7},{7,4},{8,9},{9,10},{10,1... | collective-permute-start | bytes 245768 | tf_op jit(solution)/shard_map/ppermute | solution.py:30
  109.7 3.4 %collective-permute-start.12 = (bf16[40,1024]{1,0:T(8,128)(2,1)S(1)}, bf16[40,1024]{1,0:T(8,128)(2,1)S(1)}, u32[]{:S(2)}, u32[]{:S(2)}) collective-permute-start(bf16[40,1024]{1,0:T(8,128)(2,1)S(1)} %feature_part.4.refs_0_), channel_id=1, source_target_pairs={{0,3},{1,0},{2,1},{3,2},{4,7},{5,4},{6,5},{7,6},{8,11},{9,8},{10,9... | collective-permute-start | bytes 245768 | tf_op jit(solution)/shard_map/ppermute | solution.py:30
  110.7 4.8 %collective-permute-start.11 = (bf16[40,1024]{1,0:T(8,128)(2,1)S(1)}, bf16[40,1024]{1,0:T(8,128)(2,1)S(1)}, u32[]{:S(2)}, u32[]{:S(2)}) collective-permute-start(bf16[40,1024]{1,0:T(8,128)(2,1)S(1)} %feature_part.4.refs_0_), channel_id=1, source_target_pairs={{0,2},{1,3},{2,0},{3,1},{4,6},{5,7},{6,4},{7,5},{8,10},{9,11},{10,... | collective-permute-start | bytes 245768 | tf_op jit(solution)/shard_map/ppermute | solution.py:30
  112.2 4.5 %collective-permute-start.10 = (bf16[40,1024]{1,0:T(8,128)(2,1)S(1)}, bf16[40,1024]{1,0:T(8,128)(2,1)S(1)}, u32[]{:S(2)}, u32[]{:S(2)}) collective-permute-start(bf16[40,1024]{1,0:T(8,128)(2,1)S(1)} %feature_part.4.refs_0_), channel_id=1, source_target_pairs={{0,1},{1,2},{2,3},{3,0},{4,5},{5,6},{6,7},{7,4},{8,9},{9,10},{10,1... | collective-permute-start | bytes 245768 | tf_op jit(solution)/shard_map/ppermute | solution.py:30
  147.5 10.2 %collective-permute-start.13 = (bf16[40,2048]{1,0:T(8,128)(2,1)S(1)}, bf16[40,2048]{1,0:T(8,128)(2,1)S(1)}, u32[]{:S(2)}, u32[]{:S(2)}) collective-permute-start(bf16[40,2048]{1,0:T(8,128)(2,1)S(1)} %bitcast.55), channel_id=1, source_target_pairs={{0,4},{4,0},{1,5},{5,1},{2,6},{6,2},{3,7},{7,3},{8,12},{12,8},{9,1... | collective-permute-start | bytes 491528 | tf_op jit(solution)/shard_map/ppermute | solution.py:30
  158.0 4.6 %collective-permute-start.16 = (bf16[40,1280]{1,0:T(8,128)(2,1)S(1)}, bf16[40,1280]{1,0:T(8,128)(2,1)S(1)}, u32[]{:S(2)}, u32[]{:S(2)}) collective-permute-start(bf16[40,1280]{1,0:T(8,128)(2,1)S(1)} %fusion.5.refs_0_), channel_id=1, source_target_pairs={{0,3},{1,0},{2,1},{3,2},{4,7},{5,4},{6,5},{7,6},{8,11},{9,8},{10,9... | collective-permute-start | bytes 307208 | tf_op jit(solution)/shard_map/ppermute | solution.py:30
  158.3 5.7 %collective-permute-start.15 = (bf16[40,1280]{1,0:T(8,128)(2,1)S(1)}, bf16[40,1280]{1,0:T(8,128)(2,1)S(1)}, u32[]{:S(2)}, u32[]{:S(2)}) collective-permute-start(bf16[40,1280]{1,0:T(8,128)(2,1)S(1)} %fusion.5.refs_0_), channel_id=1, source_target_pairs={{0,2},{1,3},{2,0},{3,1},{4,6},{5,7},{6,4},{7,5},{8,10},{9,11},{10,... | collective-permute-start | bytes 307208 | tf_op jit(solution)/shard_map/ppermute | solution.py:30
  159.4 7.4 %collective-permute-start.14 = (bf16[40,1280]{1,0:T(8,128)(2,1)S(1)}, bf16[40,1280]{1,0:T(8,128)(2,1)S(1)}, u32[]{:S(2)}, u32[]{:S(2)}) collective-permute-start(bf16[40,1280]{1,0:T(8,128)(2,1)S(1)} %fusion.5.refs_0_), channel_id=1, source_target_pairs={{0,1},{1,2},{2,3},{3,0},{4,5},{5,6},{6,7},{7,4},{8,9},{9,10},{10,1... | collective-permute-start | bytes 307208 | tf_op jit(solution)/shard_map/ppermute | solution.py:30
  170.8 6.4 %collective-permute-start.17 = (f32[40,80]{0,1:T(8,128)S(1)}, f32[40,80]{0,1:T(8,128)S(1)}, u32[]{:S(2)}, u32[]{:S(2)}) collective-permute-start(f32[40,80]{0,1:T(8,128)S(1)} %slice.57), channel_id=1, source_target_pairs={{0,4},{4,0},{1,5},{5,1},{2,6},{6,2},{3,7},{7,3},{8,12},{12,8},{9,1... | collective-permute-start | bytes 38408 | tf_op jit(solution)/shard_map/ppermute | solution.py:30
  172.6 23.6 %all-to-all-start.6 = ((bf16[32,40,256]{2,1,0:T(8,128)(2,1)}), bf16[32,40,256]{2,1,0:T(8,128)(2,1)S(1)}, u32[]{:S(2)}, u32[]{:S(2)}) async-start(bf16[32,40,256]{2,1,0:T(8,128)(2,1)} %get-tuple-element.29), calls=%async_computation.6 | async-start | bytes 1310720 | tf_op jit(solution)/shard_map/all_to_all | solution.py:53
  197.1 2.1 %collective-permute-start.18 = (f32[40,128]{1,0:T(8,128)S(1)}, f32[40,128]{1,0:T(8,128)S(1)}, u32[]{:S(2)}, u32[]{:S(2)}) collective-permute-start(f32[40,128]{1,0:T(8,128)S(1)} %get-tuple-element.31), channel_id=1, source_target_pairs={{0,4},{4,0},{1,5},{5,1},{2,6},{6,2},{3,7},{7,3},{8,12},{12,8},{9,1... | collective-permute-start | bytes 61448 | tf_op jit(solution)/shard_map/ppermute | solution.py:30

commit v4 on v3

--- a/solution.py
+++ b/solution.py
@@ -35,7 +35,7 @@
 
 
 def y_pieces(sent):
-    return [sent] + [shifted(sent, "y", 4, step) for step in (1, 2, 3)]
+    return [sent] + [shifted(sent, "y", 4, step) for step in (3, 2, 1)]
 
 
 def to_tiles(array):
@@ -57,15 +57,15 @@
     return exchange(jnp.broadcast_to(piece[None], (count,) + piece.shape), axes)
 
 
-def chips_sum(part, scale):
+def chips_sum(part, scale, axes=("z", "x")):
     rows, cols = part.shape
     tiles = to_tiles(part)
     count = tiles.shape[0]
     per = -(-count // 32)
     tiles = jnp.pad(tiles, ((0, 32 * per - count), (0, 0), (0, 0)))
     pieces = tiles.reshape(32, per, 8, 128)
-    mine = (exchange(pieces, ("z", "x")).astype(F32).sum(0) * scale).astype(BF16)
-    whole = spread(mine, ("z", "x"), 32).reshape(32 * per, 8, 128)[:count]
+    mine = (exchange(pieces, axes).astype(F32).sum(0) * scale).astype(BF16)
+    whole = spread(mine, axes, 32).reshape(32 * per, 8, 128)[:count]
     return from_tiles(whole, rows, cols)
 
 
@@ -238,7 +238,7 @@
         out = out.astype(BF16)
         for x in range(4):
             piece = out[:, x * width : (x + 1) * width]
-            part_ref[4 * z + x] = jnp.concatenate([piece, tail], 1)
+            part_ref[8 * x + z] = jnp.concatenate([piece, tail], 1)
 
 
 def up_part(place, pieces, own, other):
@@ -340,7 +340,7 @@
     back = y_pieces(back_part)
     other_grads = hold(other_grads)
     transposed = chips_sum(
-        token_part(place, back, grads, other_grads, D ** -0.5), scale
+        token_part(place, back, grads, other_grads, D ** -0.5), scale, ("x", "z")
     )
     again = y_pieces(feature_part(transposed, grads, other_grads))
     whole_range = chips_sum(
@@ -356,7 +356,7 @@
     joined = y_pieces(jnp.concatenate([projected, aligned(high), aligned(low)], 1))
 
     up, gram_rows = up_part(place, joined, grads, other_grads)
-    up_pieces = exchange(up, ("z", "x"))
+    up_pieces = exchange(up, ("x", "z"))
     gram_rows, place = lax.optimization_barrier((gram_rows, place))
     gram_rows = gram_rows[:, :K]
     first = place[1] == 0

time: 201 us -> 197 us (0.980)
  starting transfers between devices: 27.3 us -> 35.4 us
  waiting for transfers between devices: 19.8 us -> 13.2 us
  blocking collectives: 102 us -> 97.7 us
    ppermute x19, starting transfers between devices: 23.4 us -> 31.5 us  [shifted(): lax.ppermute(value, axis, [(i, (i + step) % size) for i in range(size)])]
    ppermute x19, waiting for transfers between devices: 16.1 us -> 10.2 us  [shifted(): lax.ppermute(value, axis, [(i, (i + step) % size) for i in range(size)])]
    all_to_all x6, blocking collectives: 102 us -> 97.7 us  [exchange(): return lax.all_to_all(pieces, axes, 0, 0, tiled=True)]
  transfers between devices with their start and end apart: 20 -> 20, of which waited for: 11 -> 9; matrix products, arithmetic and copies ran while one was open for 9% -> 9% of each run, Pallas kernels for 7% -> 7%
where the time goes in v4:
time: 197 us
  blocking collectives  97.7 us (50%)
  starting transfers between devices  35.4 us (18%)
  Pallas kernels  28.9 us (15%)
  other arithmetic  15.9 us (8%)
  waiting for transfers between devices  13.2 us (7%)
  between operations  3.04 us (2%)
    all_to_all x6, blocking collectives, exchange(): return lax.all_to_all(pieces, axes, 0, 0, tiled=True)  97.7 us
    ppermute x19, starting transfers between devices, shifted(): lax.ppermute(value, axis, [(i, (i + step) % size) for i in range(size)])  31.5 us
    ppermute x19, waiting for transfers between devices, shifted(): lax.ppermute(value, axis, [(i, (i + step) % size) for i in range(size)])  10.2 us
    another operation x3, other arithmetic, local(): lower = jnp.linalg.cholesky(gram)  7.98 us
    pallas_call x3, Pallas kernels, feature_part(): pl.pallas_call(feature_kernel, out_shape=jax.ShapeDtypeStruct((HALF, 2 *...  7.21 us
    another operation x2, other arithmetic, local(): lax.linalg.triangular_solve(lower, jnp.eye(K, dtype=F32), left_side=True,...  6.78 us
    pallas_call x3, Pallas kernels, token_part(): pl.pallas_call(functools.partial(token_kernel, scale), out_shape=jax.Shap...  5.89 us
    pallas_call x1, Pallas kernels, load_and_sketch(): pl.pallas_call(load_kernel, out_shape=(part, part, pltpu.VMEM((rows, cols...  4.89 us
  transfers between devices with their start and end apart: 20, of which 9 were waited for; matrix products, arithmetic and copies ran while one was open for 9% of the time, Pallas kernels for 7%

profile of v4, /device:TPU:1, one launch (start us, length us, event | category | flops | bytes accessed | tf_op | source)
XLA Modules:
  0.0 196.6 jit_solution(3973988150181654289)
XLA Ops:
  0.6 3.3 %collective-permute-start.1 = (bf16[512,2048]{1,0:T(8,128)(2,1)}, bf16[512,2048]{1,0:T(8,128)(2,1)S(1)}, u32[]{:S(2)}, u32[]{:S(2)}) collective-permute-start(bf16[512,2048]{1,0:T(8,128)(2,1)} %own_ref.3), channel_id=1, source_target_pairs={{0,4},{4,0},{1,5},{5,1},{2,6},{6,2},{3,7},{7,3},{8,12},{12,8},{9,1... | collective-permute-start | bytes 6291464 | tf_op jit(solution)/shard_map/ppermute | solution.py:30
  4.0 4.9 %load_and_sketch.1 = (bf16[40,512]{1,0:T(8,128)(2,1)S(1)}, bf16[40,512]{1,0:T(8,128)(2,1)S(1)}, bf16[512,7168]{1,0:T(8,128)(2,1)S(1)}) custom-call(s32[2]{0:T(128)S(1)} %pad_add_fusion.1.place_ref, bf16[80,7168]{1,0:T(8,128)(2,1)} %bitcast.64, bf16[512,7168]{1,0:T(8,128)(2,1)} %grads_ref.1), custom_call_target="tpu_custom_call" | custom-call | flops 587202560 | bytes 14680064 | tf_op jit(solution)/shard_map/load_and_sketch/pallas_call | solution.py:144
  11.7 2.2 %collective-permute-start.5 = (bf16[40,1024]{1,0:T(8,128)(2,1)S(1)}, bf16[40,1024]{1,0:T(8,128)(2,1)S(1)}, u32[]{:S(2)}, u32[]{:S(2)}) collective-permute-start(bf16[40,1024]{1,0:T(8,128)(2,1)S(1)} %pad_maximum_fusion.2.refs_0_), channel_id=1, source_target_pairs={{0,2},{1,3},{2,0},{3,1},{4,6},{5,7},{6,4},{7,5},{8,10},{9,11},{10,... | collective-permute-start | bytes 245768 | tf_op jit(solution)/shard_map/ppermute | solution.py:30
  15.7 1.7 hold.2.refs_5_.other_ref
  20.2 20.0 %all_to_all.35 = bf16[32,3,8,128]{3,2,1,0:T(8,128)(2,1)S(1)} all-to-all(bf16[32,3,8,128]{3,2,1,0:T(8,128)(2,1)S(1)} %bitcast.66), channel_id=1, replica_groups=mesh['z'=8,'x'=4,'c'=2,'y'=4] {'z','x'}, dimensions={0} | all-to-all | bytes 393216 | tf_op jit(solution)/shard_map/all_to_all | solution.py:53
  40.2 13.9 %all_to_all.36 = bf16[32,3,8,128]{3,2,1,0:T(8,128)(2,1)S(1)} all-to-all(bf16[32,3,8,128]{3,2,1,0:T(8,128)(2,1)S(1)} %broadcast_in_dim.7), channel_id=1, replica_groups=mesh['z'=8,'x'=4,'c'=2,'y'=4] {'z','x'}, dimensions={0} | all-to-all | bytes 393216 | tf_op jit(solution)/shard_map/all_to_all | solution.py:53
  55.6 2.0 %collective-permute-start.8 = (bf16[40,1024]{1,0:T(8,128)(2,1)S(1)}, bf16[40,1024]{1,0:T(8,128)(2,1)S(1)}, u32[]{:S(2)}, u32[]{:S(2)}) collective-permute-start(bf16[40,1024]{1,0:T(8,128)(2,1)S(1)} %feature_part.3.refs_0_), channel_id=1, source_target_pairs={{0,2},{1,3},{2,0},{3,1},{4,6},{5,7},{6,4},{7,5},{8,10},{9,11},{10,... | collective-permute-start | bytes 245768 | tf_op jit(solution)/shard_map/ppermute | solution.py:30
  59.0 3.2 %hold.3.refs_5_.other_ref = bf16[512,7168]{1,0:T(8,128)(2,1)S(1)} custom-call(bf16[512,7168]{1,0:T(8,128)(2,1)} %copy-done.1), custom_call_target="tpu_custom_call" | custom-call | bytes 14680064 | tf_op jit(solution)/shard_map/hold/pallas_call | solution.py:97
  62.2 3.2 %token_part.4 = bf16[40,7168]{1,0:T(8,128)(2,1)S(1)} custom-call(s32[4]{0:T(128)S(1)} %pad_add_fusion.place_ref, bf16[40,1024]{1,0:T(8,128)(2,1)S(1)} %feature_part.3.refs_0_, bf16[40,1024]{1,0:T(8,128)(2,1)S(1)} %collective-permute-done.7.refs_1_, bf16[40,1024]{1,0:T(8,128)(2,1)S(1)} %collective-permute-done.8.refs_2_, ...), custom_call_target="tpu_custom_call" | custom-call | flops 587202560 | bytes 14680064 | tf_op jit(solution)/shard_map/token_part/pallas_call | solution.py:183
  65.4 16.4 %all_to_all.37 = bf16[32,9,8,128]{3,2,1,0:T(8,128)(2,1)S(1)} all-to-all(bf16[32,9,8,128]{3,2,1,0:T(8,128)(2,1)S(1)} %bitcast.62), channel_id=1, replica_groups=mesh['z'=8,'x'=4,'c'=2,'y'=4] {'x','z'}, dimensions={0} | all-to-all | bytes 1179648 | tf_op jit(solution)/shard_map/all_to_all | solution.py:53
  82.0 18.8 %all_to_all.38 = bf16[32,9,8,128]{3,2,1,0:T(8,128)(2,1)S(1)} all-to-all(bf16[32,9,8,128]{3,2,1,0:T(8,128)(2,1)S(1)} %broadcast_in_dim.8), channel_id=1, replica_groups=mesh['z'=8,'x'=4,'c'=2,'y'=4] {'x','z'}, dimensions={0} | all-to-all | bytes 1179648 | tf_op jit(solution)/shard_map/all_to_all | solution.py:53
  100.9 4.5 %feature_part.4.refs_0_ = bf16[40,1024]{1,0:T(8,128)(2,1)S(1)} custom-call(bf16[40,7168]{1,0:T(8,128)(2,1)S(1)} %bitcast.54, bf16[512,7168]{1,0:T(8,128)(2,1)S(1)} %get-tuple-element.24.refs_4_.own_ref, bf16[512,7168]{1,0:T(8,128)(2,1)S(1)} %hold.3.refs_5_.other_ref), custom_call_target="tpu_custom_call" | custom-call | flops 587202560 | bytes 14680064 | tf_op jit(solution)/shard_map/feature_part/pallas_call | solution.py:206
  106.0 2.6 %collective-permute-start.11 = (bf16[40,1024]{1,0:T(8,128)(2,1)S(1)}, bf16[40,1024]{1,0:T(8,128)(2,1)S(1)}, u32[]{:S(2)}, u32[]{:S(2)}) collective-permute-start(bf16[40,1024]{1,0:T(8,128)(2,1)S(1)} %feature_part.4.refs_0_), channel_id=1, source_target_pairs={{0,2},{1,3},{2,0},{3,1},{4,6},{5,7},{6,4},{7,5},{8,10},{9,11},{10,... | collective-permute-start | bytes 245768 | tf_op jit(solution)/shard_map/ppermute | solution.py:30
  113.3 15.6 %all_to_all.39 = bf16[32,3,8,128]{3,2,1,0:T(8,128)(2,1)S(1)} all-to-all(bf16[32,3,8,128]{3,2,1,0:T(8,128)(2,1)S(1)} %bitcast.65), channel_id=1, replica_groups=mesh['z'=8,'x'=4,'c'=2,'y'=4] {'z','x'}, dimensions={0} | all-to-all | bytes 393216 | tf_op jit(solution)/shard_map/all_to_all | solution.py:53
  129.0 13.1 %all_to_all.40 = bf16[32,3,8,128]{3,2,1,0:T(8,128)(2,1)S(1)} all-to-all(bf16[32,3,8,128]{3,2,1,0:T(8,128)(2,1)S(1)} %broadcast_in_dim.9), channel_id=1, replica_groups=mesh['z'=8,'x'=4,'c'=2,'y'=4] {'z','x'}, dimensions={0} | all-to-all | bytes 393216 | tf_op jit(solution)/shard_map/all_to_all | solution.py:53
  142.1 10.7 %collective-permute-start.13 = (bf16[40,2048]{1,0:T(8,128)(2,1)S(1)}, bf16[40,2048]{1,0:T(8,128)(2,1)S(1)}, u32[]{:S(2)}, u32[]{:S(2)}) collective-permute-start(bf16[40,2048]{1,0:T(8,128)(2,1)S(1)} %bitcast.55), channel_id=1, source_target_pairs={{0,4},{4,0},{1,5},{5,1},{2,6},{6,2},{3,7},{7,3},{8,12},{12,8},{9,1... | collective-permute-start | bytes 491528 | tf_op jit(solution)/shard_map/ppermute | solution.py:30
  155.2 2.7 %collective-permute-start.15 = (bf16[40,1280]{1,0:T(8,128)(2,1)S(1)}, bf16[40,1280]{1,0:T(8,128)(2,1)S(1)}, u32[]{:S(2)}, u32[]{:S(2)}) collective-permute-start(bf16[40,1280]{1,0:T(8,128)(2,1)S(1)} %fusion.5.refs_0_), channel_id=1, source_target_pairs={{0,2},{1,3},{2,0},{3,1},{4,6},{5,7},{6,4},{7,5},{8,10},{9,11},{10,... | collective-permute-start | bytes 307208 | tf_op jit(solution)/shard_map/ppermute | solution.py:30
  157.9 2.3 %collective-permute-done.16.refs_3_ = bf16[40,1280]{1,0:T(8,128)(2,1)S(1)} collective-permute-done((bf16[40,1280]{1,0:T(8,128)(2,1)S(1)}, bf16[40,1280]{1,0:T(8,128)(2,1)S(1)}, u32[]{:S(2)}, u32[]{:S(2)}) %collective-permute-start.16) | collective-permute-done | bytes 102432 | tf_op jit(solution)/shard_map/ppermute | solution.py:30
  160.2 2.9 %collective-permute-done.15.refs_2_ = bf16[40,1280]{1,0:T(8,128)(2,1)S(1)} collective-permute-done((bf16[40,1280]{1,0:T(8,128)(2,1)S(1)}, bf16[40,1280]{1,0:T(8,128)(2,1)S(1)}, u32[]{:S(2)}, u32[]{:S(2)}) %collective-permute-start.15) | collective-permute-done | bytes 102432 | tf_op jit(solution)/shard_map/ppermute | solution.py:30
  163.1 3.9 %up_part.1 = (bf16[32,40,256]{2,1,0:T(8,128)(2,1)}, f32[40,128]{1,0:T(8,128)S(1)}) custom-call(s32[4]{0:T(128)S(1)} %pad_add_fusion.place_ref, bf16[40,1280]{1,0:T(8,128)(2,1)S(1)} %fusion.5.refs_0_, bf16[40,1280]{1,0:T(8,128)(2,1)S(1)} %collective-permute-done.14.refs_1_, bf16[40,1280]{1,0:T(8,128)(2,1)S(1)} %collective-permute-done.15.refs_2_, ...), custom_call_target="tpu_custom_call" | custom-call | flops 587202560 | bytes 14680064 | tf_op jit(solution)/shard_map/up_part/pallas_call | solution.py:245
  169.2 3.9 %all-to-all-start.6 = ((bf16[32,40,256]{2,1,0:T(8,128)(2,1)}), bf16[32,40,256]{2,1,0:T(8,128)(2,1)S(1)}, u32[]{:S(2)}, u32[]{:S(2)}) async-start(bf16[32,40,256]{2,1,0:T(8,128)(2,1)} %get-tuple-element.29), calls=%async_computation.6 | async-start | bytes 1310720 | tf_op jit(solution)/shard_map/all_to_all | solution.py:53
  174.0 7.3 %cholesky.17 = f32[80,80]{1,0:T(8,128)S(1)} custom-call(f32[80,80]{1,0:T(8,128)S(1)} %fusion.9), custom_call_target="Cholesky" | custom-call | tf_op jit(solution)/shard_map/jit(cholesky)/cholesky | solution.py:367
  182.7 6.1 %custom-call.6 = f32[1,80,80]{1,2,0:T(8,128)S(1)} custom-call(f32[1,80,80]{2,1,0:T(8,128)S(1)} %fusion.6), custom_call_target="InvertDiagBlocksLowerTriangular" | custom-call | tf_op jit(solution)/shard_map/triangular_solve | solution.py:368
  189.1 3.0 %all-to-all-done.6.pieces_ref = bf16[32,40,256]{2,1,0:T(8,128)(2,1)S(1)} async-done(((bf16[32,40,256]{2,1,0:T(8,128)(2,1)}), bf16[32,40,256]{2,1,0:T(8,128)(2,1)S(1)}, u32[]{:S(2)}, u32[]{:S(2)}) %all-to-all-start.6) | async-done | bytes 655392 | tf_op jit(solution)/shard_map/all_to_all | solution.py:53
  (78 shorter events, 25.5 us)
Async XLA Ops:
  0.6 9.6 %collective-permute-start.1 = (bf16[512,2048]{1,0:T(8,128)(2,1)}, bf16[512,2048]{1,0:T(8,128)(2,1)S(1)}, u32[]{:S(2)}, u32[]{:S(2)}) collective-permute-start(bf16[512,2048]{1,0:T(8,128)(2,1)} %own_ref.3), channel_id=1, source_target_pairs={{0,4},{4,0},{1,5},{5,1},{2,6},{6,2},{3,7},{7,3},{8,12},{12,8},{9,1... | collective-permute-start | bytes 6291464 | tf_op jit(solution)/shard_map/ppermute | solution.py:30
  4.0 6.2 %copy-start.2 = (bf16[512,7168]{1,0:T(8,128)(2,1)S(1)}, bf16[512,7168]{1,0:T(8,128)(2,1)}, u32[]{:S(2)}) copy-start(bf16[512,7168]{1,0:T(8,128)(2,1)} %grads_ref.1) | copy-start | bytes 22020100
  8.9 1.3 collective-permute-start.2
  10.3 5.4 %copy-start.3 = (bf16[512,2048]{1,0:T(8,128)(2,1)}, bf16[512,2048]{1,0:T(8,128)(2,1)S(1)}, u32[]{:S(2)}) copy-start(bf16[512,2048]{1,0:T(8,128)(2,1)S(1)} %collective-permute-done.1.given_ref) | copy-start | bytes 6291460
  10.3 45.2 %collective-permute-start.3 = (bf16[512,7168]{1,0:T(8,128)(2,1)S(1)}, bf16[512,7168]{1,0:T(8,128)(2,1)S(1)}, u32[]{:S(2)}, u32[]{:S(2)}) collective-permute-start(bf16[512,7168]{1,0:T(8,128)(2,1)S(1)} %copy-done.2), channel_id=1, source_target_pairs={{0,4},{4,0},{1,5},{5,1},{2,6},{6,2},{3,7},{7,3},{8,12},{12,8},{9,1... | collective-permute-start | bytes 22020104 | tf_op jit(solution)/shard_map/ppermute | solution.py:30
  10.5 4.4 %collective-permute-start = (s32[1]{0:T(128)}, s32[1]{0:T(128)}, u32[]{:S(2)}, u32[]{:S(2)}) collective-permute-start(s32[1]{0:T(128)} %param.7), channel_id=1, source_target_pairs={{0,4},{4,0},{1,5},{5,1},{2,6},{6,2},{3,7},{7,3},{8,12},{12,8},{9,1... | collective-permute-start | bytes 20 | tf_op jit(solution)/shard_map/ppermute | solution.py:30
  11.6 5.9 %collective-permute-start.6 = (bf16[40,1024]{1,0:T(8,128)(2,1)S(1)}, bf16[40,1024]{1,0:T(8,128)(2,1)S(1)}, u32[]{:S(2)}, u32[]{:S(2)}) collective-permute-start(bf16[40,1024]{1,0:T(8,128)(2,1)S(1)} %pad_maximum_fusion.2.refs_0_), channel_id=1, source_target_pairs={{0,1},{1,2},{2,3},{3,0},{4,5},{5,6},{6,7},{7,4},{8,9},{9,10},{10,1... | collective-permute-start | bytes 245768 | tf_op jit(solution)/shard_map/ppermute | solution.py:30
  11.7 6.4 %collective-permute-start.5 = (bf16[40,1024]{1,0:T(8,128)(2,1)S(1)}, bf16[40,1024]{1,0:T(8,128)(2,1)S(1)}, u32[]{:S(2)}, u32[]{:S(2)}) collective-permute-start(bf16[40,1024]{1,0:T(8,128)(2,1)S(1)} %pad_maximum_fusion.2.refs_0_), channel_id=1, source_target_pairs={{0,2},{1,3},{2,0},{3,1},{4,6},{5,7},{6,4},{7,5},{8,10},{9,11},{10,... | collective-permute-start | bytes 245768 | tf_op jit(solution)/shard_map/ppermute | solution.py:30
  13.8 4.9 %collective-permute-start.4 = (bf16[40,1024]{1,0:T(8,128)(2,1)S(1)}, bf16[40,1024]{1,0:T(8,128)(2,1)S(1)}, u32[]{:S(2)}, u32[]{:S(2)}) collective-permute-start(bf16[40,1024]{1,0:T(8,128)(2,1)S(1)} %pad_maximum_fusion.2.refs_0_), channel_id=1, source_target_pairs={{0,3},{1,0},{2,1},{3,2},{4,7},{5,4},{6,5},{7,6},{8,11},{9,8},{10,9... | collective-permute-start | bytes 245768 | tf_op jit(solution)/shard_map/ppermute | solution.py:30
  15.7 3.1 %copy-start = (bf16[512,2048]{1,0:T(8,128)(2,1)S(1)}, bf16[512,2048]{1,0:T(8,128)(2,1)}, u32[]{:S(2)}) copy-start(bf16[512,2048]{1,0:T(8,128)(2,1)} %own_ref.3) | copy-start | bytes 6291460
  55.5 3.5 %copy-start.1 = (bf16[512,7168]{1,0:T(8,128)(2,1)}, bf16[512,7168]{1,0:T(8,128)(2,1)S(1)}, u32[]{:S(2)}) copy-start(bf16[512,7168]{1,0:T(8,128)(2,1)S(1)} %collective-permute-done.3.given_ref) | copy-start | bytes 22020100
  55.5 6.6 %collective-permute-start.9 = (bf16[40,1024]{1,0:T(8,128)(2,1)S(1)}, bf16[40,1024]{1,0:T(8,128)(2,1)S(1)}, u32[]{:S(2)}, u32[]{:S(2)}) collective-permute-start(bf16[40,1024]{1,0:T(8,128)(2,1)S(1)} %feature_part.3.refs_0_), channel_id=1, source_target_pairs={{0,1},{1,2},{2,3},{3,0},{4,5},{5,6},{6,7},{7,4},{8,9},{9,10},{10,1... | collective-permute-start | bytes 245768 | tf_op jit(solution)/shard_map/ppermute | solution.py:30
  55.6 6.6 %collective-permute-start.8 = (bf16[40,1024]{1,0:T(8,128)(2,1)S(1)}, bf16[40,1024]{1,0:T(8,128)(2,1)S(1)}, u32[]{:S(2)}, u32[]{:S(2)}) collective-permute-start(bf16[40,1024]{1,0:T(8,128)(2,1)S(1)} %feature_part.3.refs_0_), channel_id=1, source_target_pairs={{0,2},{1,3},{2,0},{3,1},{4,6},{5,7},{6,4},{7,5},{8,10},{9,11},{10,... | collective-permute-start | bytes 245768 | tf_op jit(solution)/shard_map/ppermute | solution.py:30
  57.6 4.6 %collective-permute-start.7 = (bf16[40,1024]{1,0:T(8,128)(2,1)S(1)}, bf16[40,1024]{1,0:T(8,128)(2,1)S(1)}, u32[]{:S(2)}, u32[]{:S(2)}) collective-permute-start(bf16[40,1024]{1,0:T(8,128)(2,1)S(1)} %feature_part.3.refs_0_), channel_id=1, source_target_pairs={{0,3},{1,0},{2,1},{3,2},{4,7},{5,4},{6,5},{7,6},{8,11},{9,8},{10,9... | collective-permute-start | bytes 245768 | tf_op jit(solution)/shard_map/ppermute | solution.py:30
  105.4 4.6 %collective-permute-start.12 = (bf16[40,1024]{1,0:T(8,128)(2,1)S(1)}, bf16[40,1024]{1,0:T(8,128)(2,1)S(1)}, u32[]{:S(2)}, u32[]{:S(2)}) collective-permute-start(bf16[40,1024]{1,0:T(8,128)(2,1)S(1)} %feature_part.4.refs_0_), channel_id=1, source_target_pairs={{0,1},{1,2},{2,3},{3,0},{4,5},{5,6},{6,7},{7,4},{8,9},{9,10},{10,1... | collective-permute-start | bytes 245768 | tf_op jit(solution)/shard_map/ppermute | solution.py:30
  106.0 5.4 %collective-permute-start.11 = (bf16[40,1024]{1,0:T(8,128)(2,1)S(1)}, bf16[40,1024]{1,0:T(8,128)(2,1)S(1)}, u32[]{:S(2)}, u32[]{:S(2)}) collective-permute-start(bf16[40,1024]{1,0:T(8,128)(2,1)S(1)} %feature_part.4.refs_0_), channel_id=1, source_target_pairs={{0,2},{1,3},{2,0},{3,1},{4,6},{5,7},{6,4},{7,5},{8,10},{9,11},{10,... | collective-permute-start | bytes 245768 | tf_op jit(solution)/shard_map/ppermute | solution.py:30
  108.6 3.3 %collective-permute-start.10 = (bf16[40,1024]{1,0:T(8,128)(2,1)S(1)}, bf16[40,1024]{1,0:T(8,128)(2,1)S(1)}, u32[]{:S(2)}, u32[]{:S(2)}) collective-permute-start(bf16[40,1024]{1,0:T(8,128)(2,1)S(1)} %feature_part.4.refs_0_), channel_id=1, source_target_pairs={{0,3},{1,0},{2,1},{3,2},{4,7},{5,4},{6,5},{7,6},{8,11},{9,8},{10,9... | collective-permute-start | bytes 245768 | tf_op jit(solution)/shard_map/ppermute | solution.py:30
  142.1 12.0 %collective-permute-start.13 = (bf16[40,2048]{1,0:T(8,128)(2,1)S(1)}, bf16[40,2048]{1,0:T(8,128)(2,1)S(1)}, u32[]{:S(2)}, u32[]{:S(2)}) collective-permute-start(bf16[40,2048]{1,0:T(8,128)(2,1)S(1)} %bitcast.55), channel_id=1, source_target_pairs={{0,4},{4,0},{1,5},{5,1},{2,6},{6,2},{3,7},{7,3},{8,12},{12,8},{9,1... | collective-permute-start | bytes 491528 | tf_op jit(solution)/shard_map/ppermute | solution.py:30
  154.4 5.8 %collective-permute-start.16 = (bf16[40,1280]{1,0:T(8,128)(2,1)S(1)}, bf16[40,1280]{1,0:T(8,128)(2,1)S(1)}, u32[]{:S(2)}, u32[]{:S(2)}) collective-permute-start(bf16[40,1280]{1,0:T(8,128)(2,1)S(1)} %fusion.5.refs_0_), channel_id=1, source_target_pairs={{0,1},{1,2},{2,3},{3,0},{4,5},{5,6},{6,7},{7,4},{8,9},{9,10},{10,1... | collective-permute-start | bytes 307208 | tf_op jit(solution)/shard_map/ppermute | solution.py:30
  155.2 7.9 %collective-permute-start.15 = (bf16[40,1280]{1,0:T(8,128)(2,1)S(1)}, bf16[40,1280]{1,0:T(8,128)(2,1)S(1)}, u32[]{:S(2)}, u32[]{:S(2)}) collective-permute-start(bf16[40,1280]{1,0:T(8,128)(2,1)S(1)} %fusion.5.refs_0_), channel_id=1, source_target_pairs={{0,2},{1,3},{2,0},{3,1},{4,6},{5,7},{6,4},{7,5},{8,10},{9,11},{10,... | collective-permute-start | bytes 307208 | tf_op jit(solution)/shard_map/ppermute | solution.py:30
  157.9 5.2 %collective-permute-start.14 = (bf16[40,1280]{1,0:T(8,128)(2,1)S(1)}, bf16[40,1280]{1,0:T(8,128)(2,1)S(1)}, u32[]{:S(2)}, u32[]{:S(2)}) collective-permute-start(bf16[40,1280]{1,0:T(8,128)(2,1)S(1)} %fusion.5.refs_0_), channel_id=1, source_target_pairs={{0,3},{1,0},{2,1},{3,2},{4,7},{5,4},{6,5},{7,6},{8,11},{9,8},{10,9... | collective-permute-start | bytes 307208 | tf_op jit(solution)/shard_map/ppermute | solution.py:30
  167.1 6.7 %collective-permute-start.17 = (f32[40,80]{0,1:T(8,128)S(1)}, f32[40,80]{0,1:T(8,128)S(1)}, u32[]{:S(2)}, u32[]{:S(2)}) collective-permute-start(f32[40,80]{0,1:T(8,128)S(1)} %slice.57), channel_id=1, source_target_pairs={{0,4},{4,0},{1,5},{5,1},{2,6},{6,2},{3,7},{7,3},{8,12},{12,8},{9,1... | collective-permute-start | bytes 38408 | tf_op jit(solution)/shard_map/ppermute | solution.py:30
  169.2 22.8 %all-to-all-start.6 = ((bf16[32,40,256]{2,1,0:T(8,128)(2,1)}), bf16[32,40,256]{2,1,0:T(8,128)(2,1)S(1)}, u32[]{:S(2)}, u32[]{:S(2)}) async-start(bf16[32,40,256]{2,1,0:T(8,128)(2,1)} %get-tuple-element.29), calls=%async_computation.6 | async-start | bytes 1310720 | tf_op jit(solution)/shard_map/all_to_all | solution.py:53
  192.9 2.4 %collective-permute-start.18 = (f32[40,128]{1,0:T(8,128)S(1)}, f32[40,128]{1,0:T(8,128)S(1)}, u32[]{:S(2)}, u32[]{:S(2)}) collective-permute-start(f32[40,128]{1,0:T(8,128)S(1)} %get-tuple-element.31), channel_id=1, source_target_pairs={{0,4},{4,0},{1,5},{5,1},{2,6},{6,2},{3,7},{7,3},{8,12},{12,8},{9,1... | collective-permute-start | bytes 61448 | tf_op jit(solution)/shard_map/ppermute | solution.py:30

commit v5 on v4

--- a/solution.py
+++ b/solution.py
@@ -349,7 +349,8 @@
 
     other_range = sibling(whole_range)
     both = jnp.concatenate([whole_range, other_range], 0)
-    gram_part = dot(whole_range, both, ((1,), (1,)))
+    gram_part = dot(both, both, ((1,), (1,)))
+    gram_part = jnp.concatenate([gram_part[:HALF], gram_part[HALF:, HALF:]], 1)
     high = gram_part.astype(BF16)
     low = (gram_part - high.astype(F32)).astype(BF16)
     projected = feature_part(whole_range, tokens, other_tokens)
@@ -358,12 +359,11 @@
     up, gram_rows = up_part(place, joined, grads, other_grads)
     up_pieces = exchange(up, ("x", "z"))
     gram_rows, place = lax.optimization_barrier((gram_rows, place))
-    gram_rows = gram_rows[:, :K]
+    own_rows, corner = gram_rows[:, :K], gram_rows[:, K : K + HALF]
+    other_rows = jnp.concatenate([own_rows[:, HALF:].T, corner], 1)
+    gram = jnp.concatenate([own_rows, other_rows], 0)
     first = place[1] == 0
-    other_rows = sibling(gram_rows)
-    other_rows = jnp.roll(other_rows, HALF, 1)
-    gram = both_halves(first, gram_rows, other_rows)
-    gram = jnp.where(first, gram, jnp.roll(gram, HALF, 1))
+    gram = jnp.where(first, gram, jnp.roll(gram, (HALF, HALF), (0, 1)))
     lower = jnp.linalg.cholesky(gram)
     inverse = lax.linalg.triangular_solve(
         lower, jnp.eye(K, dtype=F32), left_side=True, lower=True

time: 197 us -> 196 us (level)
  waiting for transfers between devices: 13.2 us -> 10.3 us
    all_to_all x1, waiting for transfers between devices: 2.98 us -> 0.01 us  [exchange(): return lax.all_to_all(pieces, axes, 0, 0, tiled=True)]
    ppermute x19 -> x18, starting transfers between devices: 31.5 us -> 33.1 us  [shifted(): lax.ppermute(value, axis, [(i, (i + step) % size) for i in range(size)])]
    ppermute x19 -> x18, waiting for transfers between devices: 10.2 us -> 10.2 us  [shifted(): lax.ppermute(value, axis, [(i, (i + step) % size) for i in range(size)])]
  transfers between devices with their start and end apart: 20 -> 19, of which waited for: 9 -> 8; matrix products, arithmetic and copies ran while one was open for 9% -> 9% of each run, Pallas kernels for 7% -> 7%
where the time goes in v5:
time: 196 us
  blocking collectives  97.7 us (50%)
  starting transfers between devices  37 us (19%)
  Pallas kernels  28.9 us (15%)
  other arithmetic  16.1 us (8%)
  waiting for transfers between devices  10.3 us (5%)
  between operations  3.03 us (2%)
    all_to_all x6, blocking collectives, exchange(): return lax.all_to_all(pieces, axes, 0, 0, tiled=True)  97.7 us
    ppermute x18, starting transfers between devices, shifted(): lax.ppermute(value, axis, [(i, (i + step) % size) for i in range(size)])  33.1 us
    ppermute x18, waiting for transfers between devices, shifted(): lax.ppermute(value, axis, [(i, (i + step) % size) for i in range(size)])  10.2 us
    another operation x3, other arithmetic, local(): lower = jnp.linalg.cholesky(gram)  7.98 us
    pallas_call x3, Pallas kernels, feature_part(): pl.pallas_call(feature_kernel, out_shape=jax.ShapeDtypeStruct((HALF, 2 *...  7.21 us
    another operation x2, other arithmetic, local(): lax.linalg.triangular_solve(lower, jnp.eye(K, dtype=F32), left_side=True,...  6.78 us
    pallas_call x3, Pallas kernels, token_part(): pl.pallas_call(functools.partial(token_kernel, scale), out_shape=jax.Shap...  5.89 us
    pallas_call x1, Pallas kernels, load_and_sketch(): pl.pallas_call(load_kernel, out_shape=(part, part, pltpu.VMEM((rows, cols...  4.89 us
  transfers between devices with their start and end apart: 19, of which 8 were waited for; matrix products, arithmetic and copies ran while one was open for 9% of the time, Pallas kernels for 7%

profile of v5, /device:TPU:1, one launch (start us, length us, event | category | flops | bytes accessed | tf_op | source)
XLA Modules:
  0.0 195.6 jit_solution(263421889848252595)
XLA Ops:
  0.6 3.3 %collective-permute-start.1 = (bf16[512,2048]{1,0:T(8,128)(2,1)}, bf16[512,2048]{1,0:T(8,128)(2,1)S(1)}, u32[]{:S(2)}, u32[]{:S(2)}) collective-permute-start(bf16[512,2048]{1,0:T(8,128)(2,1)} %own_ref.3), channel_id=1, source_target_pairs={{0,4},{4,0},{1,5},{5,1},{2,6},{6,2},{3,7},{7,3},{8,12},{12,8},{9,1... | collective-permute-start | bytes 6291464 | tf_op jit(solution)/shard_map/ppermute | solution.py:30
  4.0 4.9 %load_and_sketch.1 = (bf16[40,512]{1,0:T(8,128)(2,1)S(1)}, bf16[40,512]{1,0:T(8,128)(2,1)S(1)}, bf16[512,7168]{1,0:T(8,128)(2,1)S(1)}) custom-call(s32[2]{0:T(128)S(1)} %pad_add_fusion.1.place_ref, bf16[80,7168]{1,0:T(8,128)(2,1)} %bitcast.65, bf16[512,7168]{1,0:T(8,128)(2,1)} %grads_ref.1), custom_call_target="tpu_custom_call" | custom-call | flops 587202560 | bytes 14680064 | tf_op jit(solution)/shard_map/load_and_sketch/pallas_call | solution.py:144
  11.7 2.2 %collective-permute-start.5 = (bf16[40,1024]{1,0:T(8,128)(2,1)S(1)}, bf16[40,1024]{1,0:T(8,128)(2,1)S(1)}, u32[]{:S(2)}, u32[]{:S(2)}) collective-permute-start(bf16[40,1024]{1,0:T(8,128)(2,1)S(1)} %pad_maximum_fusion.2.refs_0_), channel_id=1, source_target_pairs={{0,2},{1,3},{2,0},{3,1},{4,6},{5,7},{6,4},{7,5},{8,10},{9,11},{10,... | collective-permute-start | bytes 245768 | tf_op jit(solution)/shard_map/ppermute | solution.py:30
  15.6 1.7 hold.2.refs_5_.other_ref
  20.2 20.0 %all_to_all.35 = bf16[32,3,8,128]{3,2,1,0:T(8,128)(2,1)S(1)} all-to-all(bf16[32,3,8,128]{3,2,1,0:T(8,128)(2,1)S(1)} %bitcast.67), channel_id=1, replica_groups=mesh['z'=8,'x'=4,'c'=2,'y'=4] {'z','x'}, dimensions={0} | all-to-all | bytes 393216 | tf_op jit(solution)/shard_map/all_to_all | solution.py:53
  40.2 13.9 %all_to_all.36 = bf16[32,3,8,128]{3,2,1,0:T(8,128)(2,1)S(1)} all-to-all(bf16[32,3,8,128]{3,2,1,0:T(8,128)(2,1)S(1)} %broadcast_in_dim.7), channel_id=1, replica_groups=mesh['z'=8,'x'=4,'c'=2,'y'=4] {'z','x'}, dimensions={0} | all-to-all | bytes 393216 | tf_op jit(solution)/shard_map/all_to_all | solution.py:53
  55.6 2.0 %collective-permute-start.8 = (bf16[40,1024]{1,0:T(8,128)(2,1)S(1)}, bf16[40,1024]{1,0:T(8,128)(2,1)S(1)}, u32[]{:S(2)}, u32[]{:S(2)}) collective-permute-start(bf16[40,1024]{1,0:T(8,128)(2,1)S(1)} %feature_part.3.refs_0_), channel_id=1, source_target_pairs={{0,2},{1,3},{2,0},{3,1},{4,6},{5,7},{6,4},{7,5},{8,10},{9,11},{10,... | collective-permute-start | bytes 245768 | tf_op jit(solution)/shard_map/ppermute | solution.py:30
  59.0 3.2 %hold.3.refs_5_.other_ref = bf16[512,7168]{1,0:T(8,128)(2,1)S(1)} custom-call(bf16[512,7168]{1,0:T(8,128)(2,1)} %copy-done.1), custom_call_target="tpu_custom_call" | custom-call | bytes 14680064 | tf_op jit(solution)/shard_map/hold/pallas_call | solution.py:97
  62.2 3.2 %token_part.4 = bf16[40,7168]{1,0:T(8,128)(2,1)S(1)} custom-call(s32[4]{0:T(128)S(1)} %pad_add_fusion.place_ref, bf16[40,1024]{1,0:T(8,128)(2,1)S(1)} %feature_part.3.refs_0_, bf16[40,1024]{1,0:T(8,128)(2,1)S(1)} %collective-permute-done.7.refs_1_, bf16[40,1024]{1,0:T(8,128)(2,1)S(1)} %collective-permute-done.8.refs_2_, ...), custom_call_target="tpu_custom_call" | custom-call | flops 587202560 | bytes 14680064 | tf_op jit(solution)/shard_map/token_part/pallas_call | solution.py:183
  65.4 16.4 %all_to_all.37 = bf16[32,9,8,128]{3,2,1,0:T(8,128)(2,1)S(1)} all-to-all(bf16[32,9,8,128]{3,2,1,0:T(8,128)(2,1)S(1)} %bitcast.63), channel_id=1, replica_groups=mesh['z'=8,'x'=4,'c'=2,'y'=4] {'x','z'}, dimensions={0} | all-to-all | bytes 1179648 | tf_op jit(solution)/shard_map/all_to_all | solution.py:53
  82.0 18.8 %all_to_all.38 = bf16[32,9,8,128]{3,2,1,0:T(8,128)(2,1)S(1)} all-to-all(bf16[32,9,8,128]{3,2,1,0:T(8,128)(2,1)S(1)} %broadcast_in_dim.8), channel_id=1, replica_groups=mesh['z'=8,'x'=4,'c'=2,'y'=4] {'x','z'}, dimensions={0} | all-to-all | bytes 1179648 | tf_op jit(solution)/shard_map/all_to_all | solution.py:53
  100.9 4.5 %feature_part.4.refs_0_ = bf16[40,1024]{1,0:T(8,128)(2,1)S(1)} custom-call(bf16[40,7168]{1,0:T(8,128)(2,1)S(1)} %bitcast.55, bf16[512,7168]{1,0:T(8,128)(2,1)S(1)} %get-tuple-element.24.refs_4_.own_ref, bf16[512,7168]{1,0:T(8,128)(2,1)S(1)} %hold.3.refs_5_.other_ref), custom_call_target="tpu_custom_call" | custom-call | flops 587202560 | bytes 14680064 | tf_op jit(solution)/shard_map/feature_part/pallas_call | solution.py:206
  106.0 2.6 %collective-permute-start.11 = (bf16[40,1024]{1,0:T(8,128)(2,1)S(1)}, bf16[40,1024]{1,0:T(8,128)(2,1)S(1)}, u32[]{:S(2)}, u32[]{:S(2)}) collective-permute-start(bf16[40,1024]{1,0:T(8,128)(2,1)S(1)} %feature_part.4.refs_0_), channel_id=1, source_target_pairs={{0,2},{1,3},{2,0},{3,1},{4,6},{5,7},{6,4},{7,5},{8,10},{9,11},{10,... | collective-permute-start | bytes 245768 | tf_op jit(solution)/shard_map/ppermute | solution.py:30
  113.3 15.6 %all_to_all.39 = bf16[32,3,8,128]{3,2,1,0:T(8,128)(2,1)S(1)} all-to-all(bf16[32,3,8,128]{3,2,1,0:T(8,128)(2,1)S(1)} %bitcast.66), channel_id=1, replica_groups=mesh['z'=8,'x'=4,'c'=2,'y'=4] {'z','x'}, dimensions={0} | all-to-all | bytes 393216 | tf_op jit(solution)/shard_map/all_to_all | solution.py:53
  129.0 13.1 %all_to_all.40 = bf16[32,3,8,128]{3,2,1,0:T(8,128)(2,1)S(1)} all-to-all(bf16[32,3,8,128]{3,2,1,0:T(8,128)(2,1)S(1)} %broadcast_in_dim.9), channel_id=1, replica_groups=mesh['z'=8,'x'=4,'c'=2,'y'=4] {'z','x'}, dimensions={0} | all-to-all | bytes 393216 | tf_op jit(solution)/shard_map/all_to_all | solution.py:53
  142.1 10.7 %collective-permute-start.13 = (bf16[40,2048]{1,0:T(8,128)(2,1)S(1)}, bf16[40,2048]{1,0:T(8,128)(2,1)S(1)}, u32[]{:S(2)}, u32[]{:S(2)}) collective-permute-start(bf16[40,2048]{1,0:T(8,128)(2,1)S(1)} %bitcast.56), channel_id=1, source_target_pairs={{0,4},{4,0},{1,5},{5,1},{2,6},{6,2},{3,7},{7,3},{8,12},{12,8},{9,1... | collective-permute-start | bytes 491528 | tf_op jit(solution)/shard_map/ppermute | solution.py:30
  155.4 2.7 %collective-permute-start.15 = (bf16[40,1280]{1,0:T(8,128)(2,1)S(1)}, bf16[40,1280]{1,0:T(8,128)(2,1)S(1)}, u32[]{:S(2)}, u32[]{:S(2)}) collective-permute-start(bf16[40,1280]{1,0:T(8,128)(2,1)S(1)} %fusion.5.refs_0_), channel_id=1, source_target_pairs={{0,2},{1,3},{2,0},{3,1},{4,6},{5,7},{6,4},{7,5},{8,10},{9,11},{10,... | collective-permute-start | bytes 307208 | tf_op jit(solution)/shard_map/ppermute | solution.py:30
  158.1 2.3 %collective-permute-done.16.refs_3_ = bf16[40,1280]{1,0:T(8,128)(2,1)S(1)} collective-permute-done((bf16[40,1280]{1,0:T(8,128)(2,1)S(1)}, bf16[40,1280]{1,0:T(8,128)(2,1)S(1)}, u32[]{:S(2)}, u32[]{:S(2)}) %collective-permute-start.16) | collective-permute-done | bytes 102432 | tf_op jit(solution)/shard_map/ppermute | solution.py:30
  160.4 2.9 %collective-permute-done.15.refs_2_ = bf16[40,1280]{1,0:T(8,128)(2,1)S(1)} collective-permute-done((bf16[40,1280]{1,0:T(8,128)(2,1)S(1)}, bf16[40,1280]{1,0:T(8,128)(2,1)S(1)}, u32[]{:S(2)}, u32[]{:S(2)}) %collective-permute-start.15) | collective-permute-done | bytes 102432 | tf_op jit(solution)/shard_map/ppermute | solution.py:30
  163.4 3.9 %up_part.1 = (bf16[32,40,256]{2,1,0:T(8,128)(2,1)}, f32[40,128]{1,0:T(8,128)S(1)}) custom-call(s32[4]{0:T(128)S(1)} %pad_add_fusion.place_ref, bf16[40,1280]{1,0:T(8,128)(2,1)S(1)} %fusion.5.refs_0_, bf16[40,1280]{1,0:T(8,128)(2,1)S(1)} %collective-permute-done.14.refs_1_, bf16[40,1280]{1,0:T(8,128)(2,1)S(1)} %collective-permute-done.15.refs_2_, ...), custom_call_target="tpu_custom_call" | custom-call | flops 587202560 | bytes 14680064 | tf_op jit(solution)/shard_map/up_part/pallas_call | solution.py:245
  167.4 3.9 %all-to-all-start.6 = ((bf16[32,40,256]{2,1,0:T(8,128)(2,1)}), bf16[32,40,256]{2,1,0:T(8,128)(2,1)S(1)}, u32[]{:S(2)}, u32[]{:S(2)}) async-start(bf16[32,40,256]{2,1,0:T(8,128)(2,1)} %get-tuple-element.29), calls=%async_computation.6 | async-start | bytes 1310720 | tf_op jit(solution)/shard_map/all_to_all | solution.py:53
  173.5 7.3 %cholesky.17 = f32[80,80]{1,0:T(8,128)S(1)} custom-call(f32[80,80]{1,0:T(8,128)S(1)} %fusion.9), custom_call_target="Cholesky" | custom-call | tf_op jit(solution)/shard_map/jit(cholesky)/cholesky | solution.py:367
  182.2 6.1 %custom-call.6 = f32[1,80,80]{1,2,0:T(8,128)S(1)} custom-call(f32[1,80,80]{2,1,0:T(8,128)S(1)} %fusion.6), custom_call_target="InvertDiagBlocksLowerTriangular" | custom-call | tf_op jit(solution)/shard_map/triangular_solve | solution.py:368
  189.4 3.9 %collective-permute-start.17 = (f32[40,128]{1,0:T(8,128)S(1)}, f32[40,128]{1,0:T(8,128)S(1)}, u32[]{:S(2)}, u32[]{:S(2)}) collective-permute-start(f32[40,128]{1,0:T(8,128)S(1)} %get-tuple-element.31), channel_id=1, source_target_pairs={{0,4},{4,0},{1,5},{5,1},{2,6},{6,2},{3,7},{7,3},{8,12},{12,8},{9,1... | collective-permute-start | bytes 61448 | tf_op jit(solution)/shard_map/ppermute | solution.py:30
  (81 shorter events, 23.5 us)
Async XLA Ops:
  0.6 9.6 %collective-permute-start.1 = (bf16[512,2048]{1,0:T(8,128)(2,1)}, bf16[512,2048]{1,0:T(8,128)(2,1)S(1)}, u32[]{:S(2)}, u32[]{:S(2)}) collective-permute-start(bf16[512,2048]{1,0:T(8,128)(2,1)} %own_ref.3), channel_id=1, source_target_pairs={{0,4},{4,0},{1,5},{5,1},{2,6},{6,2},{3,7},{7,3},{8,12},{12,8},{9,1... | collective-permute-start | bytes 6291464 | tf_op jit(solution)/shard_map/ppermute | solution.py:30
  4.0 6.2 %copy-start.2 = (bf16[512,7168]{1,0:T(8,128)(2,1)S(1)}, bf16[512,7168]{1,0:T(8,128)(2,1)}, u32[]{:S(2)}) copy-start(bf16[512,7168]{1,0:T(8,128)(2,1)} %grads_ref.1) | copy-start | bytes 22020100
  8.9 1.3 collective-permute-start.2
  10.3 5.4 %copy-start.3 = (bf16[512,2048]{1,0:T(8,128)(2,1)}, bf16[512,2048]{1,0:T(8,128)(2,1)S(1)}, u32[]{:S(2)}) copy-start(bf16[512,2048]{1,0:T(8,128)(2,1)S(1)} %collective-permute-done.1.given_ref) | copy-start | bytes 6291460
  10.3 45.2 %collective-permute-start.3 = (bf16[512,7168]{1,0:T(8,128)(2,1)S(1)}, bf16[512,7168]{1,0:T(8,128)(2,1)S(1)}, u32[]{:S(2)}, u32[]{:S(2)}) collective-permute-start(bf16[512,7168]{1,0:T(8,128)(2,1)S(1)} %copy-done.2), channel_id=1, source_target_pairs={{0,4},{4,0},{1,5},{5,1},{2,6},{6,2},{3,7},{7,3},{8,12},{12,8},{9,1... | collective-permute-start | bytes 22020104 | tf_op jit(solution)/shard_map/ppermute | solution.py:30
  10.5 4.4 %collective-permute-start = (s32[1]{0:T(128)}, s32[1]{0:T(128)}, u32[]{:S(2)}, u32[]{:S(2)}) collective-permute-start(s32[1]{0:T(128)} %param.7), channel_id=1, source_target_pairs={{0,4},{4,0},{1,5},{5,1},{2,6},{6,2},{3,7},{7,3},{8,12},{12,8},{9,1... | collective-permute-start | bytes 20 | tf_op jit(solution)/shard_map/ppermute | solution.py:30
  11.6 5.8 %collective-permute-start.6 = (bf16[40,1024]{1,0:T(8,128)(2,1)S(1)}, bf16[40,1024]{1,0:T(8,128)(2,1)S(1)}, u32[]{:S(2)}, u32[]{:S(2)}) collective-permute-start(bf16[40,1024]{1,0:T(8,128)(2,1)S(1)} %pad_maximum_fusion.2.refs_0_), channel_id=1, source_target_pairs={{0,1},{1,2},{2,3},{3,0},{4,5},{5,6},{6,7},{7,4},{8,9},{9,10},{10,1... | collective-permute-start | bytes 245768 | tf_op jit(solution)/shard_map/ppermute | solution.py:30
  11.7 6.4 %collective-permute-start.5 = (bf16[40,1024]{1,0:T(8,128)(2,1)S(1)}, bf16[40,1024]{1,0:T(8,128)(2,1)S(1)}, u32[]{:S(2)}, u32[]{:S(2)}) collective-permute-start(bf16[40,1024]{1,0:T(8,128)(2,1)S(1)} %pad_maximum_fusion.2.refs_0_), channel_id=1, source_target_pairs={{0,2},{1,3},{2,0},{3,1},{4,6},{5,7},{6,4},{7,5},{8,10},{9,11},{10,... | collective-permute-start | bytes 245768 | tf_op jit(solution)/shard_map/ppermute | solution.py:30
  13.8 4.9 %collective-permute-start.4 = (bf16[40,1024]{1,0:T(8,128)(2,1)S(1)}, bf16[40,1024]{1,0:T(8,128)(2,1)S(1)}, u32[]{:S(2)}, u32[]{:S(2)}) collective-permute-start(bf16[40,1024]{1,0:T(8,128)(2,1)S(1)} %pad_maximum_fusion.2.refs_0_), channel_id=1, source_target_pairs={{0,3},{1,0},{2,1},{3,2},{4,7},{5,4},{6,5},{7,6},{8,11},{9,8},{10,9... | collective-permute-start | bytes 245768 | tf_op jit(solution)/shard_map/ppermute | solution.py:30
  15.6 3.1 %copy-start = (bf16[512,2048]{1,0:T(8,128)(2,1)S(1)}, bf16[512,2048]{1,0:T(8,128)(2,1)}, u32[]{:S(2)}) copy-start(bf16[512,2048]{1,0:T(8,128)(2,1)} %own_ref.3) | copy-start | bytes 6291460
  55.5 3.5 %copy-start.1 = (bf16[512,7168]{1,0:T(8,128)(2,1)}, bf16[512,7168]{1,0:T(8,128)(2,1)S(1)}, u32[]{:S(2)}) copy-start(bf16[512,7168]{1,0:T(8,128)(2,1)S(1)} %collective-permute-done.3.given_ref) | copy-start | bytes 22020100
  55.5 6.6 %collective-permute-start.9 = (bf16[40,1024]{1,0:T(8,128)(2,1)S(1)}, bf16[40,1024]{1,0:T(8,128)(2,1)S(1)}, u32[]{:S(2)}, u32[]{:S(2)}) collective-permute-start(bf16[40,1024]{1,0:T(8,128)(2,1)S(1)} %feature_part.3.refs_0_), channel_id=1, source_target_pairs={{0,1},{1,2},{2,3},{3,0},{4,5},{5,6},{6,7},{7,4},{8,9},{9,10},{10,1... | collective-permute-start | bytes 245768 | tf_op jit(solution)/shard_map/ppermute | solution.py:30
  55.6 6.6 %collective-permute-start.8 = (bf16[40,1024]{1,0:T(8,128)(2,1)S(1)}, bf16[40,1024]{1,0:T(8,128)(2,1)S(1)}, u32[]{:S(2)}, u32[]{:S(2)}) collective-permute-start(bf16[40,1024]{1,0:T(8,128)(2,1)S(1)} %feature_part.3.refs_0_), channel_id=1, source_target_pairs={{0,2},{1,3},{2,0},{3,1},{4,6},{5,7},{6,4},{7,5},{8,10},{9,11},{10,... | collective-permute-start | bytes 245768 | tf_op jit(solution)/shard_map/ppermute | solution.py:30
  57.6 4.6 %collective-permute-start.7 = (bf16[40,1024]{1,0:T(8,128)(2,1)S(1)}, bf16[40,1024]{1,0:T(8,128)(2,1)S(1)}, u32[]{:S(2)}, u32[]{:S(2)}) collective-permute-start(bf16[40,1024]{1,0:T(8,128)(2,1)S(1)} %feature_part.3.refs_0_), channel_id=1, source_target_pairs={{0,3},{1,0},{2,1},{3,2},{4,7},{5,4},{6,5},{7,6},{8,11},{9,8},{10,9... | collective-permute-start | bytes 245768 | tf_op jit(solution)/shard_map/ppermute | solution.py:30
  105.4 4.6 %collective-permute-start.12 = (bf16[40,1024]{1,0:T(8,128)(2,1)S(1)}, bf16[40,1024]{1,0:T(8,128)(2,1)S(1)}, u32[]{:S(2)}, u32[]{:S(2)}) collective-permute-start(bf16[40,1024]{1,0:T(8,128)(2,1)S(1)} %feature_part.4.refs_0_), channel_id=1, source_target_pairs={{0,1},{1,2},{2,3},{3,0},{4,5},{5,6},{6,7},{7,4},{8,9},{9,10},{10,1... | collective-permute-start | bytes 245768 | tf_op jit(solution)/shard_map/ppermute | solution.py:30
  106.0 5.4 %collective-permute-start.11 = (bf16[40,1024]{1,0:T(8,128)(2,1)S(1)}, bf16[40,1024]{1,0:T(8,128)(2,1)S(1)}, u32[]{:S(2)}, u32[]{:S(2)}) collective-permute-start(bf16[40,1024]{1,0:T(8,128)(2,1)S(1)} %feature_part.4.refs_0_), channel_id=1, source_target_pairs={{0,2},{1,3},{2,0},{3,1},{4,6},{5,7},{6,4},{7,5},{8,10},{9,11},{10,... | collective-permute-start | bytes 245768 | tf_op jit(solution)/shard_map/ppermute | solution.py:30
  108.6 3.3 %collective-permute-start.10 = (bf16[40,1024]{1,0:T(8,128)(2,1)S(1)}, bf16[40,1024]{1,0:T(8,128)(2,1)S(1)}, u32[]{:S(2)}, u32[]{:S(2)}) collective-permute-start(bf16[40,1024]{1,0:T(8,128)(2,1)S(1)} %feature_part.4.refs_0_), channel_id=1, source_target_pairs={{0,3},{1,0},{2,1},{3,2},{4,7},{5,4},{6,5},{7,6},{8,11},{9,8},{10,9... | collective-permute-start | bytes 245768 | tf_op jit(solution)/shard_map/ppermute | solution.py:30
  142.1 12.0 %collective-permute-start.13 = (bf16[40,2048]{1,0:T(8,128)(2,1)S(1)}, bf16[40,2048]{1,0:T(8,128)(2,1)S(1)}, u32[]{:S(2)}, u32[]{:S(2)}) collective-permute-start(bf16[40,2048]{1,0:T(8,128)(2,1)S(1)} %bitcast.56), channel_id=1, source_target_pairs={{0,4},{4,0},{1,5},{5,1},{2,6},{6,2},{3,7},{7,3},{8,12},{12,8},{9,1... | collective-permute-start | bytes 491528 | tf_op jit(solution)/shard_map/ppermute | solution.py:30
  154.6 5.8 %collective-permute-start.16 = (bf16[40,1280]{1,0:T(8,128)(2,1)S(1)}, bf16[40,1280]{1,0:T(8,128)(2,1)S(1)}, u32[]{:S(2)}, u32[]{:S(2)}) collective-permute-start(bf16[40,1280]{1,0:T(8,128)(2,1)S(1)} %fusion.5.refs_0_), channel_id=1, source_target_pairs={{0,1},{1,2},{2,3},{3,0},{4,5},{5,6},{6,7},{7,4},{8,9},{9,10},{10,1... | collective-permute-start | bytes 307208 | tf_op jit(solution)/shard_map/ppermute | solution.py:30
  155.4 7.9 %collective-permute-start.15 = (bf16[40,1280]{1,0:T(8,128)(2,1)S(1)}, bf16[40,1280]{1,0:T(8,128)(2,1)S(1)}, u32[]{:S(2)}, u32[]{:S(2)}) collective-permute-start(bf16[40,1280]{1,0:T(8,128)(2,1)S(1)} %fusion.5.refs_0_), channel_id=1, source_target_pairs={{0,2},{1,3},{2,0},{3,1},{4,6},{5,7},{6,4},{7,5},{8,10},{9,11},{10,... | collective-permute-start | bytes 307208 | tf_op jit(solution)/shard_map/ppermute | solution.py:30
  158.1 5.2 %collective-permute-start.14 = (bf16[40,1280]{1,0:T(8,128)(2,1)S(1)}, bf16[40,1280]{1,0:T(8,128)(2,1)S(1)}, u32[]{:S(2)}, u32[]{:S(2)}) collective-permute-start(bf16[40,1280]{1,0:T(8,128)(2,1)S(1)} %fusion.5.refs_0_), channel_id=1, source_target_pairs={{0,3},{1,0},{2,1},{3,2},{4,7},{5,4},{6,5},{7,6},{8,11},{9,8},{10,9... | collective-permute-start | bytes 307208 | tf_op jit(solution)/shard_map/ppermute | solution.py:30
  167.4 21.1 %all-to-all-start.6 = ((bf16[32,40,256]{2,1,0:T(8,128)(2,1)}), bf16[32,40,256]{2,1,0:T(8,128)(2,1)S(1)}, u32[]{:S(2)}, u32[]{:S(2)}) async-start(bf16[32,40,256]{2,1,0:T(8,128)(2,1)} %get-tuple-element.29), calls=%async_computation.6 | async-start | bytes 1310720 | tf_op jit(solution)/shard_map/all_to_all | solution.py:53
  189.4 4.8 %collective-permute-start.17 = (f32[40,128]{1,0:T(8,128)S(1)}, f32[40,128]{1,0:T(8,128)S(1)}, u32[]{:S(2)}, u32[]{:S(2)}) collective-permute-start(f32[40,128]{1,0:T(8,128)S(1)} %get-tuple-element.31), channel_id=1, source_target_pairs={{0,4},{4,0},{1,5},{5,1},{2,6},{6,2},{3,7},{7,3},{8,12},{12,8},{9,1... | collective-permute-start | bytes 61448 | tf_op jit(solution)/shard_map/ppermute | solution.py:30

commit v6 on v5

--- a/solution.py
+++ b/solution.py
@@ -226,26 +226,32 @@
         gram = high + low if gram is None else gram + (high + low)
     gram_ref[...] = gram
     width = own_ref.shape[1] // 32
-    lane = lax.broadcasted_iota(jnp.int32, (HALF, 256), 1)
+    over = width - 128
+    lane = lax.broadcasted_iota(jnp.int32, (8, 128 - over), 1)
     high = (place_ref[2] // 32 + place_ref[3] // 32).astype(F32)
     low = (place_ref[2] % 32 + place_ref[3] % 32).astype(F32)
-    digits = jnp.where(lane == width, high, jnp.where(lane == width + 1, low, 0.0))
-    tail = digits.astype(BF16)[:, width:]
+    digits = jnp.where(lane == 0, high, jnp.where(lane == 1, low, 0.0))
     for z in range(8):
         cols = slice(4 * z * width, 4 * (z + 1) * width)
         out = dot(small[:, :rows], own_ref[:, cols], ((1,), (0,)))
         out = out + dot(small[:, rows:], other_ref[:, cols], ((1,), (0,)))
-        out = out.astype(BF16)
         for x in range(4):
             piece = out[:, x * width : (x + 1) * width]
-            part_ref[8 * x + z] = jnp.concatenate([piece, tail], 1)
+            rest = piece[:, 128:]
+            last = rest[32:]
+            beside = [last[:, 32 * i : 32 * i + 32] for i in range(3)] + [digits]
+            for i in range(5):
+                part_ref[8 * x + z, i] = piece[8 * i : 8 * i + 8, :128].astype(BF16)
+            for i in range(4):
+                tile = jnp.concatenate([rest[8 * i : 8 * i + 8], beside[i]], 1)
+                part_ref[8 * x + z, 5 + i] = tile.astype(BF16)
 
 
 def up_part(place, pieces, own, other):
     return pl.pallas_call(
         up_kernel,
         out_shape=(
-            jax.ShapeDtypeStruct((32, HALF, 256), BF16),
+            jax.ShapeDtypeStruct((32, 9, 8, 128), BF16),
             jax.ShapeDtypeStruct((HALF, 128), F32),
         ),
         in_specs=[SMEM] + [VMEM] * (len(pieces) + 2),
@@ -261,9 +267,14 @@
     total = pieces_ref[0].astype(F32)
     for k in range(1, pieces_ref.shape[0]):
         total = total + pieces_ref[k].astype(F32)
-    tail = total[:, 2 * owned : 2 * owned + 16]
-    first = jnp.concatenate([total[:, :owned], tail], 1)
-    second = total[:, owned : 2 * owned + 16]
+    over = 2 * owned - 128
+    last = jnp.concatenate([total[5 + i][:, over:] for i in range(3)], 1)
+    wide = jnp.concatenate([total[i] for i in range(5)], 0)
+    rest = jnp.concatenate([total[5 + i][:, :over] for i in range(4)] + [last], 0)
+    tail = jnp.concatenate([total[8][:, over : over + 16]] * 5, 0)
+    both = jnp.concatenate([wide, rest], 1)
+    first = jnp.concatenate([both[:, :owned], tail], 1)
+    second = jnp.concatenate([both[:, owned:], tail], 1)
     mine = place_ref[1] == 0
     kept_ref[...] = jnp.where(mine, first, second)
     sent_ref[...] = jnp.where(mine, second, first)

time: 196 us -> 195 us (level)
  no operation moved by 1% of the time
where the time goes in v6:
time: 195 us; the launch traced here: 194 us
  blocking collectives  97.7 us (50%)
  starting transfers between devices  36 us (18%)
  Pallas kernels  28.8 us (15%)
  other arithmetic  16.1 us (8%)
  waiting for transfers between devices  10.3 us (5%)
  between operations  3.03 us (2%)
    all_to_all x6, blocking collectives, exchange(): return lax.all_to_all(pieces, axes, 0, 0, tiled=True)  97.7 us
    ppermute x18, starting transfers between devices, shifted(): lax.ppermute(value, axis, [(i, (i + step) % size) for i in range(size)])  32.1 us
    ppermute x18, waiting for transfers between devices, shifted(): lax.ppermute(value, axis, [(i, (i + step) % size) for i in range(size)])  10.2 us
    another operation x3, other arithmetic, local(): lower = jnp.linalg.cholesky(gram)  7.98 us
    pallas_call x3, Pallas kernels, feature_part(): pl.pallas_call(feature_kernel, out_shape=jax.ShapeDtypeStruct((HALF, 2 *...  7.21 us
    another operation x2, other arithmetic, local(): lax.linalg.triangular_solve(lower, jnp.eye(K, dtype=F32), left_side=True,...  6.78 us
    pallas_call x3, Pallas kernels, token_part(): pl.pallas_call(functools.partial(token_kernel, scale), out_shape=jax.Shap...  5.89 us
    pallas_call x1, Pallas kernels, load_and_sketch(): pl.pallas_call(load_kernel, out_shape=(part, part, pltpu.VMEM((rows, cols...  4.89 us
  transfers between devices with their start and end apart: 19, of which 8 were waited for; matrix products, arithmetic and copies ran while one was open for 9% of the time, Pallas kernels for 7%

profile of v6, /device:TPU:1, one launch (start us, length us, event | category | flops | bytes accessed | tf_op | source)
XLA Modules:
  0.0 194.5 jit_solution(12745480798225686696)
XLA Ops:
  0.6 3.3 %collective-permute-start.1 = (bf16[512,2048]{1,0:T(8,128)(2,1)}, bf16[512,2048]{1,0:T(8,128)(2,1)S(1)}, u32[]{:S(2)}, u32[]{:S(2)}) collective-permute-start(bf16[512,2048]{1,0:T(8,128)(2,1)} %own_ref.3), channel_id=1, source_target_pairs={{0,4},{4,0},{1,5},{5,1},{2,6},{6,2},{3,7},{7,3},{8,12},{12,8},{9,1... | collective-permute-start | bytes 6291464 | tf_op jit(solution)/shard_map/ppermute | solution.py:30
  4.0 4.9 %load_and_sketch.1 = (bf16[40,512]{1,0:T(8,128)(2,1)S(1)}, bf16[40,512]{1,0:T(8,128)(2,1)S(1)}, bf16[512,7168]{1,0:T(8,128)(2,1)S(1)}) custom-call(s32[2]{0:T(128)S(1)} %pad_add_fusion.1.place_ref, bf16[80,7168]{1,0:T(8,128)(2,1)} %bitcast.65, bf16[512,7168]{1,0:T(8,128)(2,1)} %grads_ref.1), custom_call_target="tpu_custom_call" | custom-call | flops 587202560 | bytes 14680064 | tf_op jit(solution)/shard_map/load_and_sketch/pallas_call | solution.py:144
  11.7 2.2 %collective-permute-start.5 = (bf16[40,1024]{1,0:T(8,128)(2,1)S(1)}, bf16[40,1024]{1,0:T(8,128)(2,1)S(1)}, u32[]{:S(2)}, u32[]{:S(2)}) collective-permute-start(bf16[40,1024]{1,0:T(8,128)(2,1)S(1)} %pad_maximum_fusion.2.refs_0_), channel_id=1, source_target_pairs={{0,2},{1,3},{2,0},{3,1},{4,6},{5,7},{6,4},{7,5},{8,10},{9,11},{10,... | collective-permute-start | bytes 245768 | tf_op jit(solution)/shard_map/ppermute | solution.py:30
  15.6 1.7 hold.2.refs_5_.other_ref
  20.2 20.0 %all_to_all.35 = bf16[32,3,8,128]{3,2,1,0:T(8,128)(2,1)S(1)} all-to-all(bf16[32,3,8,128]{3,2,1,0:T(8,128)(2,1)S(1)} %bitcast.67), channel_id=1, replica_groups=mesh['z'=8,'x'=4,'c'=2,'y'=4] {'z','x'}, dimensions={0} | all-to-all | bytes 393216 | tf_op jit(solution)/shard_map/all_to_all | solution.py:53
  40.2 13.9 %all_to_all.36 = bf16[32,3,8,128]{3,2,1,0:T(8,128)(2,1)S(1)} all-to-all(bf16[32,3,8,128]{3,2,1,0:T(8,128)(2,1)S(1)} %broadcast_in_dim.7), channel_id=1, replica_groups=mesh['z'=8,'x'=4,'c'=2,'y'=4] {'z','x'}, dimensions={0} | all-to-all | bytes 393216 | tf_op jit(solution)/shard_map/all_to_all | solution.py:53
  55.6 2.0 %collective-permute-start.8 = (bf16[40,1024]{1,0:T(8,128)(2,1)S(1)}, bf16[40,1024]{1,0:T(8,128)(2,1)S(1)}, u32[]{:S(2)}, u32[]{:S(2)}) collective-permute-start(bf16[40,1024]{1,0:T(8,128)(2,1)S(1)} %feature_part.3.refs_0_), channel_id=1, source_target_pairs={{0,2},{1,3},{2,0},{3,1},{4,6},{5,7},{6,4},{7,5},{8,10},{9,11},{10,... | collective-permute-start | bytes 245768 | tf_op jit(solution)/shard_map/ppermute | solution.py:30
  59.0 3.2 %hold.3.refs_5_.other_ref = bf16[512,7168]{1,0:T(8,128)(2,1)S(1)} custom-call(bf16[512,7168]{1,0:T(8,128)(2,1)} %copy-done.1), custom_call_target="tpu_custom_call" | custom-call | bytes 14680064 | tf_op jit(solution)/shard_map/hold/pallas_call | solution.py:97
  62.2 3.2 %token_part.4 = bf16[40,7168]{1,0:T(8,128)(2,1)S(1)} custom-call(s32[4]{0:T(128)S(1)} %pad_add_fusion.place_ref, bf16[40,1024]{1,0:T(8,128)(2,1)S(1)} %feature_part.3.refs_0_, bf16[40,1024]{1,0:T(8,128)(2,1)S(1)} %collective-permute-done.7.refs_1_, bf16[40,1024]{1,0:T(8,128)(2,1)S(1)} %collective-permute-done.8.refs_2_, ...), custom_call_target="tpu_custom_call" | custom-call | flops 587202560 | bytes 14680064 | tf_op jit(solution)/shard_map/token_part/pallas_call | solution.py:183
  65.4 16.4 %all_to_all.37 = bf16[32,9,8,128]{3,2,1,0:T(8,128)(2,1)S(1)} all-to-all(bf16[32,9,8,128]{3,2,1,0:T(8,128)(2,1)S(1)} %bitcast.63), channel_id=1, replica_groups=mesh['z'=8,'x'=4,'c'=2,'y'=4] {'x','z'}, dimensions={0} | all-to-all | bytes 1179648 | tf_op jit(solution)/shard_map/all_to_all | solution.py:53
  82.0 18.8 %all_to_all.38 = bf16[32,9,8,128]{3,2,1,0:T(8,128)(2,1)S(1)} all-to-all(bf16[32,9,8,128]{3,2,1,0:T(8,128)(2,1)S(1)} %broadcast_in_dim.8), channel_id=1, replica_groups=mesh['z'=8,'x'=4,'c'=2,'y'=4] {'x','z'}, dimensions={0} | all-to-all | bytes 1179648 | tf_op jit(solution)/shard_map/all_to_all | solution.py:53
  100.9 4.5 %feature_part.4.refs_0_ = bf16[40,1024]{1,0:T(8,128)(2,1)S(1)} custom-call(bf16[40,7168]{1,0:T(8,128)(2,1)S(1)} %bitcast.55, bf16[512,7168]{1,0:T(8,128)(2,1)S(1)} %get-tuple-element.24.refs_4_.own_ref, bf16[512,7168]{1,0:T(8,128)(2,1)S(1)} %hold.3.refs_5_.other_ref), custom_call_target="tpu_custom_call" | custom-call | flops 587202560 | bytes 14680064 | tf_op jit(solution)/shard_map/feature_part/pallas_call | solution.py:206
  106.0 2.6 %collective-permute-start.11 = (bf16[40,1024]{1,0:T(8,128)(2,1)S(1)}, bf16[40,1024]{1,0:T(8,128)(2,1)S(1)}, u32[]{:S(2)}, u32[]{:S(2)}) collective-permute-start(bf16[40,1024]{1,0:T(8,128)(2,1)S(1)} %feature_part.4.refs_0_), channel_id=1, source_target_pairs={{0,2},{1,3},{2,0},{3,1},{4,6},{5,7},{6,4},{7,5},{8,10},{9,11},{10,... | collective-permute-start | bytes 245768 | tf_op jit(solution)/shard_map/ppermute | solution.py:30
  113.3 15.6 %all_to_all.39 = bf16[32,3,8,128]{3,2,1,0:T(8,128)(2,1)S(1)} all-to-all(bf16[32,3,8,128]{3,2,1,0:T(8,128)(2,1)S(1)} %bitcast.66), channel_id=1, replica_groups=mesh['z'=8,'x'=4,'c'=2,'y'=4] {'z','x'}, dimensions={0} | all-to-all | bytes 393216 | tf_op jit(solution)/shard_map/all_to_all | solution.py:53
  129.0 13.1 %all_to_all.40 = bf16[32,3,8,128]{3,2,1,0:T(8,128)(2,1)S(1)} all-to-all(bf16[32,3,8,128]{3,2,1,0:T(8,128)(2,1)S(1)} %broadcast_in_dim.9), channel_id=1, replica_groups=mesh['z'=8,'x'=4,'c'=2,'y'=4] {'z','x'}, dimensions={0} | all-to-all | bytes 393216 | tf_op jit(solution)/shard_map/all_to_all | solution.py:53
  142.1 10.7 %collective-permute-start.13 = (bf16[40,2048]{1,0:T(8,128)(2,1)S(1)}, bf16[40,2048]{1,0:T(8,128)(2,1)S(1)}, u32[]{:S(2)}, u32[]{:S(2)}) collective-permute-start(bf16[40,2048]{1,0:T(8,128)(2,1)S(1)} %bitcast.56), channel_id=1, source_target_pairs={{0,4},{4,0},{1,5},{5,1},{2,6},{6,2},{3,7},{7,3},{8,12},{12,8},{9,1... | collective-permute-start | bytes 491528 | tf_op jit(solution)/shard_map/ppermute | solution.py:30
  155.4 2.7 %collective-permute-start.15 = (bf16[40,1280]{1,0:T(8,128)(2,1)S(1)}, bf16[40,1280]{1,0:T(8,128)(2,1)S(1)}, u32[]{:S(2)}, u32[]{:S(2)}) collective-permute-start(bf16[40,1280]{1,0:T(8,128)(2,1)S(1)} %fusion.5.refs_0_), channel_id=1, source_target_pairs={{0,2},{1,3},{2,0},{3,1},{4,6},{5,7},{6,4},{7,5},{8,10},{9,11},{10,... | collective-permute-start | bytes 307208 | tf_op jit(solution)/shard_map/ppermute | solution.py:30
  158.1 2.3 %collective-permute-done.16.refs_3_ = bf16[40,1280]{1,0:T(8,128)(2,1)S(1)} collective-permute-done((bf16[40,1280]{1,0:T(8,128)(2,1)S(1)}, bf16[40,1280]{1,0:T(8,128)(2,1)S(1)}, u32[]{:S(2)}, u32[]{:S(2)}) %collective-permute-start.16) | collective-permute-done | bytes 102432 | tf_op jit(solution)/shard_map/ppermute | solution.py:30
  160.4 2.9 %collective-permute-done.15.refs_2_ = bf16[40,1280]{1,0:T(8,128)(2,1)S(1)} collective-permute-done((bf16[40,1280]{1,0:T(8,128)(2,1)S(1)}, bf16[40,1280]{1,0:T(8,128)(2,1)S(1)}, u32[]{:S(2)}, u32[]{:S(2)}) %collective-permute-start.15) | collective-permute-done | bytes 102432 | tf_op jit(solution)/shard_map/ppermute | solution.py:30
  163.4 3.9 %up_part.1 = (bf16[32,9,8,128]{3,2,1,0:T(8,128)(2,1)}, f32[40,128]{1,0:T(8,128)S(1)}) custom-call(s32[4]{0:T(128)S(1)} %pad_add_fusion.place_ref, bf16[40,1280]{1,0:T(8,128)(2,1)S(1)} %fusion.5.refs_0_, bf16[40,1280]{1,0:T(8,128)(2,1)S(1)} %collective-permute-done.14.refs_1_, bf16[40,1280]{1,0:T(8,128)(2,1)S(1)} %collective-permute-done.15.refs_2_, ...), custom_call_target="tpu_custom_call" | custom-call | flops 587202560 | bytes 14680064 | tf_op jit(solution)/shard_map/up_part/pallas_call | solution.py:251
  168.7 3.9 %all-to-all-start.6 = ((bf16[32,9,8,128]{3,2,1,0:T(8,128)(2,1)}), bf16[32,9,8,128]{3,2,1,0:T(8,128)(2,1)S(1)}, u32[]{:S(2)}, u32[]{:S(2)}) async-start(bf16[32,9,8,128]{3,2,1,0:T(8,128)(2,1)} %get-tuple-element.29), calls=%async_computation.6 | async-start | bytes 1179648 | tf_op jit(solution)/shard_map/all_to_all | solution.py:53
  173.5 7.3 %cholesky.17 = f32[80,80]{1,0:T(8,128)S(1)} custom-call(f32[80,80]{1,0:T(8,128)S(1)} %fusion.9), custom_call_target="Cholesky" | custom-call | tf_op jit(solution)/shard_map/jit(cholesky)/cholesky | solution.py:378
  182.2 6.1 %custom-call.6 = f32[1,80,80]{1,2,0:T(8,128)S(1)} custom-call(f32[1,80,80]{2,1,0:T(8,128)S(1)} %fusion.6), custom_call_target="InvertDiagBlocksLowerTriangular" | custom-call | tf_op jit(solution)/shard_map/triangular_solve | solution.py:379
  189.3 3.0 %collective-permute-start.17 = (f32[40,128]{1,0:T(8,128)S(1)}, f32[40,128]{1,0:T(8,128)S(1)}, u32[]{:S(2)}, u32[]{:S(2)}) collective-permute-start(f32[40,128]{1,0:T(8,128)S(1)} %get-tuple-element.31), channel_id=1, source_target_pairs={{0,4},{4,0},{1,5},{5,1},{2,6},{6,2},{3,7},{7,3},{8,12},{12,8},{9,1... | collective-permute-start | bytes 61448 | tf_op jit(solution)/shard_map/ppermute | solution.py:30
  (81 shorter events, 23.4 us)
Async XLA Ops:
  0.6 9.6 %collective-permute-start.1 = (bf16[512,2048]{1,0:T(8,128)(2,1)}, bf16[512,2048]{1,0:T(8,128)(2,1)S(1)}, u32[]{:S(2)}, u32[]{:S(2)}) collective-permute-start(bf16[512,2048]{1,0:T(8,128)(2,1)} %own_ref.3), channel_id=1, source_target_pairs={{0,4},{4,0},{1,5},{5,1},{2,6},{6,2},{3,7},{7,3},{8,12},{12,8},{9,1... | collective-permute-start | bytes 6291464 | tf_op jit(solution)/shard_map/ppermute | solution.py:30
  4.0 6.2 %copy-start.2 = (bf16[512,7168]{1,0:T(8,128)(2,1)S(1)}, bf16[512,7168]{1,0:T(8,128)(2,1)}, u32[]{:S(2)}) copy-start(bf16[512,7168]{1,0:T(8,128)(2,1)} %grads_ref.1) | copy-start | bytes 22020100
  8.9 1.3 collective-permute-start.2
  10.3 5.4 %copy-start.3 = (bf16[512,2048]{1,0:T(8,128)(2,1)}, bf16[512,2048]{1,0:T(8,128)(2,1)S(1)}, u32[]{:S(2)}) copy-start(bf16[512,2048]{1,0:T(8,128)(2,1)S(1)} %collective-permute-done.1.given_ref) | copy-start | bytes 6291460
  10.3 45.2 %collective-permute-start.3 = (bf16[512,7168]{1,0:T(8,128)(2,1)S(1)}, bf16[512,7168]{1,0:T(8,128)(2,1)S(1)}, u32[]{:S(2)}, u32[]{:S(2)}) collective-permute-start(bf16[512,7168]{1,0:T(8,128)(2,1)S(1)} %copy-done.2), channel_id=1, source_target_pairs={{0,4},{4,0},{1,5},{5,1},{2,6},{6,2},{3,7},{7,3},{8,12},{12,8},{9,1... | collective-permute-start | bytes 22020104 | tf_op jit(solution)/shard_map/ppermute | solution.py:30
  10.5 4.4 %collective-permute-start = (s32[1]{0:T(128)}, s32[1]{0:T(128)}, u32[]{:S(2)}, u32[]{:S(2)}) collective-permute-start(s32[1]{0:T(128)} %param.7), channel_id=1, source_target_pairs={{0,4},{4,0},{1,5},{5,1},{2,6},{6,2},{3,7},{7,3},{8,12},{12,8},{9,1... | collective-permute-start | bytes 20 | tf_op jit(solution)/shard_map/ppermute | solution.py:30
  11.6 5.8 %collective-permute-start.6 = (bf16[40,1024]{1,0:T(8,128)(2,1)S(1)}, bf16[40,1024]{1,0:T(8,128)(2,1)S(1)}, u32[]{:S(2)}, u32[]{:S(2)}) collective-permute-start(bf16[40,1024]{1,0:T(8,128)(2,1)S(1)} %pad_maximum_fusion.2.refs_0_), channel_id=1, source_target_pairs={{0,1},{1,2},{2,3},{3,0},{4,5},{5,6},{6,7},{7,4},{8,9},{9,10},{10,1... | collective-permute-start | bytes 245768 | tf_op jit(solution)/shard_map/ppermute | solution.py:30
  11.7 6.4 %collective-permute-start.5 = (bf16[40,1024]{1,0:T(8,128)(2,1)S(1)}, bf16[40,1024]{1,0:T(8,128)(2,1)S(1)}, u32[]{:S(2)}, u32[]{:S(2)}) collective-permute-start(bf16[40,1024]{1,0:T(8,128)(2,1)S(1)} %pad_maximum_fusion.2.refs_0_), channel_id=1, source_target_pairs={{0,2},{1,3},{2,0},{3,1},{4,6},{5,7},{6,4},{7,5},{8,10},{9,11},{10,... | collective-permute-start | bytes 245768 | tf_op jit(solution)/shard_map/ppermute | solution.py:30
  13.8 4.9 %collective-permute-start.4 = (bf16[40,1024]{1,0:T(8,128)(2,1)S(1)}, bf16[40,1024]{1,0:T(8,128)(2,1)S(1)}, u32[]{:S(2)}, u32[]{:S(2)}) collective-permute-start(bf16[40,1024]{1,0:T(8,128)(2,1)S(1)} %pad_maximum_fusion.2.refs_0_), channel_id=1, source_target_pairs={{0,3},{1,0},{2,1},{3,2},{4,7},{5,4},{6,5},{7,6},{8,11},{9,8},{10,9... | collective-permute-start | bytes 245768 | tf_op jit(solution)/shard_map/ppermute | solution.py:30
  15.6 3.1 %copy-start = (bf16[512,2048]{1,0:T(8,128)(2,1)S(1)}, bf16[512,2048]{1,0:T(8,128)(2,1)}, u32[]{:S(2)}) copy-start(bf16[512,2048]{1,0:T(8,128)(2,1)} %own_ref.3) | copy-start | bytes 6291460
  55.5 3.5 %copy-start.1 = (bf16[512,7168]{1,0:T(8,128)(2,1)}, bf16[512,7168]{1,0:T(8,128)(2,1)S(1)}, u32[]{:S(2)}) copy-start(bf16[512,7168]{1,0:T(8,128)(2,1)S(1)} %collective-permute-done.3.given_ref) | copy-start | bytes 22020100
  55.5 6.6 %collective-permute-start.9 = (bf16[40,1024]{1,0:T(8,128)(2,1)S(1)}, bf16[40,1024]{1,0:T(8,128)(2,1)S(1)}, u32[]{:S(2)}, u32[]{:S(2)}) collective-permute-start(bf16[40,1024]{1,0:T(8,128)(2,1)S(1)} %feature_part.3.refs_0_), channel_id=1, source_target_pairs={{0,1},{1,2},{2,3},{3,0},{4,5},{5,6},{6,7},{7,4},{8,9},{9,10},{10,1... | collective-permute-start | bytes 245768 | tf_op jit(solution)/shard_map/ppermute | solution.py:30
  55.6 6.6 %collective-permute-start.8 = (bf16[40,1024]{1,0:T(8,128)(2,1)S(1)}, bf16[40,1024]{1,0:T(8,128)(2,1)S(1)}, u32[]{:S(2)}, u32[]{:S(2)}) collective-permute-start(bf16[40,1024]{1,0:T(8,128)(2,1)S(1)} %feature_part.3.refs_0_), channel_id=1, source_target_pairs={{0,2},{1,3},{2,0},{3,1},{4,6},{5,7},{6,4},{7,5},{8,10},{9,11},{10,... | collective-permute-start | bytes 245768 | tf_op jit(solution)/shard_map/ppermute | solution.py:30
  57.6 4.6 %collective-permute-start.7 = (bf16[40,1024]{1,0:T(8,128)(2,1)S(1)}, bf16[40,1024]{1,0:T(8,128)(2,1)S(1)}, u32[]{:S(2)}, u32[]{:S(2)}) collective-permute-start(bf16[40,1024]{1,0:T(8,128)(2,1)S(1)} %feature_part.3.refs_0_), channel_id=1, source_target_pairs={{0,3},{1,0},{2,1},{3,2},{4,7},{5,4},{6,5},{7,6},{8,11},{9,8},{10,9... | collective-permute-start | bytes 245768 | tf_op jit(solution)/shard_map/ppermute | solution.py:30
  105.4 4.6 %collective-permute-start.12 = (bf16[40,1024]{1,0:T(8,128)(2,1)S(1)}, bf16[40,1024]{1,0:T(8,128)(2,1)S(1)}, u32[]{:S(2)}, u32[]{:S(2)}) collective-permute-start(bf16[40,1024]{1,0:T(8,128)(2,1)S(1)} %feature_part.4.refs_0_), channel_id=1, source_target_pairs={{0,1},{1,2},{2,3},{3,0},{4,5},{5,6},{6,7},{7,4},{8,9},{9,10},{10,1... | collective-permute-start | bytes 245768 | tf_op jit(solution)/shard_map/ppermute | solution.py:30
  106.0 5.4 %collective-permute-start.11 = (bf16[40,1024]{1,0:T(8,128)(2,1)S(1)}, bf16[40,1024]{1,0:T(8,128)(2,1)S(1)}, u32[]{:S(2)}, u32[]{:S(2)}) collective-permute-start(bf16[40,1024]{1,0:T(8,128)(2,1)S(1)} %feature_part.4.refs_0_), channel_id=1, source_target_pairs={{0,2},{1,3},{2,0},{3,1},{4,6},{5,7},{6,4},{7,5},{8,10},{9,11},{10,... | collective-permute-start | bytes 245768 | tf_op jit(solution)/shard_map/ppermute | solution.py:30
  108.6 3.3 %collective-permute-start.10 = (bf16[40,1024]{1,0:T(8,128)(2,1)S(1)}, bf16[40,1024]{1,0:T(8,128)(2,1)S(1)}, u32[]{:S(2)}, u32[]{:S(2)}) collective-permute-start(bf16[40,1024]{1,0:T(8,128)(2,1)S(1)} %feature_part.4.refs_0_), channel_id=1, source_target_pairs={{0,3},{1,0},{2,1},{3,2},{4,7},{5,4},{6,5},{7,6},{8,11},{9,8},{10,9... | collective-permute-start | bytes 245768 | tf_op jit(solution)/shard_map/ppermute | solution.py:30
  142.1 12.0 %collective-permute-start.13 = (bf16[40,2048]{1,0:T(8,128)(2,1)S(1)}, bf16[40,2048]{1,0:T(8,128)(2,1)S(1)}, u32[]{:S(2)}, u32[]{:S(2)}) collective-permute-start(bf16[40,2048]{1,0:T(8,128)(2,1)S(1)} %bitcast.56), channel_id=1, source_target_pairs={{0,4},{4,0},{1,5},{5,1},{2,6},{6,2},{3,7},{7,3},{8,12},{12,8},{9,1... | collective-permute-start | bytes 491528 | tf_op jit(solution)/shard_map/ppermute | solution.py:30
  154.6 5.8 %collective-permute-start.16 = (bf16[40,1280]{1,0:T(8,128)(2,1)S(1)}, bf16[40,1280]{1,0:T(8,128)(2,1)S(1)}, u32[]{:S(2)}, u32[]{:S(2)}) collective-permute-start(bf16[40,1280]{1,0:T(8,128)(2,1)S(1)} %fusion.5.refs_0_), channel_id=1, source_target_pairs={{0,1},{1,2},{2,3},{3,0},{4,5},{5,6},{6,7},{7,4},{8,9},{9,10},{10,1... | collective-permute-start | bytes 307208 | tf_op jit(solution)/shard_map/ppermute | solution.py:30
  155.4 7.9 %collective-permute-start.15 = (bf16[40,1280]{1,0:T(8,128)(2,1)S(1)}, bf16[40,1280]{1,0:T(8,128)(2,1)S(1)}, u32[]{:S(2)}, u32[]{:S(2)}) collective-permute-start(bf16[40,1280]{1,0:T(8,128)(2,1)S(1)} %fusion.5.refs_0_), channel_id=1, source_target_pairs={{0,2},{1,3},{2,0},{3,1},{4,6},{5,7},{6,4},{7,5},{8,10},{9,11},{10,... | collective-permute-start | bytes 307208 | tf_op jit(solution)/shard_map/ppermute | solution.py:30
  158.1 5.2 %collective-permute-start.14 = (bf16[40,1280]{1,0:T(8,128)(2,1)S(1)}, bf16[40,1280]{1,0:T(8,128)(2,1)S(1)}, u32[]{:S(2)}, u32[]{:S(2)}) collective-permute-start(bf16[40,1280]{1,0:T(8,128)(2,1)S(1)} %fusion.5.refs_0_), channel_id=1, source_target_pairs={{0,3},{1,0},{2,1},{3,2},{4,7},{5,4},{6,5},{7,6},{8,11},{9,8},{10,9... | collective-permute-start | bytes 307208 | tf_op jit(solution)/shard_map/ppermute | solution.py:30
  168.7 19.9 %all-to-all-start.6 = ((bf16[32,9,8,128]{3,2,1,0:T(8,128)(2,1)}), bf16[32,9,8,128]{3,2,1,0:T(8,128)(2,1)S(1)}, u32[]{:S(2)}, u32[]{:S(2)}) async-start(bf16[32,9,8,128]{3,2,1,0:T(8,128)(2,1)} %get-tuple-element.29), calls=%async_computation.6 | async-start | bytes 1179648 | tf_op jit(solution)/shard_map/all_to_all | solution.py:53
  189.3 3.9 %collective-permute-start.17 = (f32[40,128]{1,0:T(8,128)S(1)}, f32[40,128]{1,0:T(8,128)S(1)}, u32[]{:S(2)}, u32[]{:S(2)}) collective-permute-start(f32[40,128]{1,0:T(8,128)S(1)} %get-tuple-element.31), channel_id=1, source_target_pairs={{0,4},{4,0},{1,5},{5,1},{2,6},{6,2},{3,7},{7,3},{8,12},{12,8},{9,1... | collective-permute-start | bytes 61448 | tf_op jit(solution)/shard_map/ppermute | solution.py:30

commit v7 on v6

--- a/solution.py
+++ b/solution.py
@@ -224,7 +224,8 @@
         high = ref[:, 2 * rows : 2 * rows + 128].astype(F32)
         low = ref[:, 2 * rows + 128 : 2 * rows + 256].astype(F32)
         gram = high + low if gram is None else gram + (high + low)
-    gram_ref[...] = gram
+    spot = lax.broadcasted_iota(jnp.int32, gram.shape, 1)
+    gram_ref[...] = jnp.where(spot == K + HALF, place_ref[1].astype(F32), gram)
     width = own_ref.shape[1] // 32
     over = width - 128
     lane = lax.broadcasted_iota(jnp.int32, (8, 128 - over), 1)
@@ -369,11 +370,10 @@
 
     up, gram_rows = up_part(place, joined, grads, other_grads)
     up_pieces = exchange(up, ("x", "z"))
-    gram_rows, place = lax.optimization_barrier((gram_rows, place))
     own_rows, corner = gram_rows[:, :K], gram_rows[:, K : K + HALF]
     other_rows = jnp.concatenate([own_rows[:, HALF:].T, corner], 1)
     gram = jnp.concatenate([own_rows, other_rows], 0)
-    first = place[1] == 0
+    first = gram_rows[:1, K + HALF : K + HALF + 1] == 0.0
     gram = jnp.where(first, gram, jnp.roll(gram, (HALF, HALF), (0, 1)))
     lower = jnp.linalg.cholesky(gram)
     inverse = lax.linalg.triangular_solve(
@@ -384,8 +384,9 @@
     kept_up, sent_up = split_up(place, up_pieces, owned)
     adapter_up = finish_up(place, kept_up, sibling(sent_up), inverse, owned).T
 
+    inverse, spots = lax.optimization_barrier((inverse, place))
     own = both_halves(first, whole_range, other_range)
-    own = lax.dynamic_slice_in_dim(own, place[0] * width, width, 1).astype(F32)
+    own = lax.dynamic_slice_in_dim(own, spots[0] * width, width, 1).astype(F32)
     adapter_down = jnp.dot(inverse, own, precision=lax.Precision.HIGHEST).T * D ** 0.5
     return adapter_down, adapter_up
 

time: 195 us -> 194 us (level)
  transfers between devices with their start and end apart: 19 -> 19, of which waited for: 8 -> 9; matrix products, arithmetic and copies ran while one was open for 9% -> 9% of each run, Pallas kernels for 7% -> 7%
where the time goes in v7:
time: 194 us
  blocking collectives  97.7 us (50%)
  starting transfers between devices  36 us (19%)
  Pallas kernels  28.8 us (15%)
  other arithmetic  16.1 us (8%)
  waiting for transfers between devices  10.2 us (5%)
  between operations  2.41 us (1%)
    all_to_all x6, blocking collectives, exchange(): return lax.all_to_all(pieces, axes, 0, 0, tiled=True)  97.7 us
    ppermute x18, starting transfers between devices, shifted(): lax.ppermute(value, axis, [(i, (i + step) % size) for i in range(size)])  32.1 us
    ppermute x18, waiting for transfers between devices, shifted(): lax.ppermute(value, axis, [(i, (i + step) % size) for i in range(size)])  10.2 us
    another operation x3, other arithmetic, local(): lower = jnp.linalg.cholesky(gram)  7.98 us
    pallas_call x3, Pallas kernels, feature_part(): pl.pallas_call(feature_kernel, out_shape=jax.ShapeDtypeStruct((HALF, 2 *...  7.21 us
    another operation x2, other arithmetic, local(): lax.linalg.triangular_solve(lower, jnp.eye(K, dtype=F32), left_side=True,...  6.78 us
    pallas_call x3, Pallas kernels, token_part(): pl.pallas_call(functools.partial(token_kernel, scale), out_shape=jax.Shap...  5.89 us
    pallas_call x1, Pallas kernels, load_and_sketch(): pl.pallas_call(load_kernel, out_shape=(part, part, pltpu.VMEM((rows, cols...  4.89 us
  transfers between devices with their start and end apart: 19, of which 9 were waited for; matrix products, arithmetic and copies ran while one was open for 9% of the time, Pallas kernels for 7%

profile of v7, /device:TPU:1, one launch (start us, length us, event | category | flops | bytes accessed | tf_op | source)
XLA Modules:
  0.0 193.8 jit_solution(18440883531972999405)
XLA Ops:
  0.6 3.3 %collective-permute-start.1 = (bf16[512,2048]{1,0:T(8,128)(2,1)}, bf16[512,2048]{1,0:T(8,128)(2,1)S(1)}, u32[]{:S(2)}, u32[]{:S(2)}) collective-permute-start(bf16[512,2048]{1,0:T(8,128)(2,1)} %own_ref.3), channel_id=1, source_target_pairs={{0,4},{4,0},{1,5},{5,1},{2,6},{6,2},{3,7},{7,3},{8,12},{12,8},{9,1... | collective-permute-start | bytes 6291464 | tf_op jit(solution)/shard_map/ppermute | solution.py:30
  4.0 4.9 %load_and_sketch.1 = (bf16[40,512]{1,0:T(8,128)(2,1)S(1)}, bf16[40,512]{1,0:T(8,128)(2,1)S(1)}, bf16[512,7168]{1,0:T(8,128)(2,1)S(1)}) custom-call(s32[2]{0:T(128)S(1)} %pad_add_fusion.1.place_ref, bf16[80,7168]{1,0:T(8,128)(2,1)} %bitcast.67, bf16[512,7168]{1,0:T(8,128)(2,1)} %grads_ref.1), custom_call_target="tpu_custom_call" | custom-call | flops 587202560 | bytes 14680064 | tf_op jit(solution)/shard_map/load_and_sketch/pallas_call | solution.py:144
  11.7 2.2 %collective-permute-start.5 = (bf16[40,1024]{1,0:T(8,128)(2,1)S(1)}, bf16[40,1024]{1,0:T(8,128)(2,1)S(1)}, u32[]{:S(2)}, u32[]{:S(2)}) collective-permute-start(bf16[40,1024]{1,0:T(8,128)(2,1)S(1)} %pad_maximum_fusion.2.refs_0_), channel_id=1, source_target_pairs={{0,2},{1,3},{2,0},{3,1},{4,6},{5,7},{6,4},{7,5},{8,10},{9,11},{10,... | collective-permute-start | bytes 245768 | tf_op jit(solution)/shard_map/ppermute | solution.py:30
  15.8 1.7 hold.2.refs_5_.other_ref
  20.2 20.0 %all_to_all.35 = bf16[32,3,8,128]{3,2,1,0:T(8,128)(2,1)S(1)} all-to-all(bf16[32,3,8,128]{3,2,1,0:T(8,128)(2,1)S(1)} %bitcast.69), channel_id=1, replica_groups=mesh['z'=8,'x'=4,'c'=2,'y'=4] {'z','x'}, dimensions={0} | all-to-all | bytes 393216 | tf_op jit(solution)/shard_map/all_to_all | solution.py:53
  40.2 13.9 %all_to_all.36 = bf16[32,3,8,128]{3,2,1,0:T(8,128)(2,1)S(1)} all-to-all(bf16[32,3,8,128]{3,2,1,0:T(8,128)(2,1)S(1)} %broadcast_in_dim.38), channel_id=1, replica_groups=mesh['z'=8,'x'=4,'c'=2,'y'=4] {'z','x'}, dimensions={0} | all-to-all | bytes 393216 | tf_op jit(solution)/shard_map/all_to_all | solution.py:53
  55.6 2.0 %collective-permute-start.8 = (bf16[40,1024]{1,0:T(8,128)(2,1)S(1)}, bf16[40,1024]{1,0:T(8,128)(2,1)S(1)}, u32[]{:S(2)}, u32[]{:S(2)}) collective-permute-start(bf16[40,1024]{1,0:T(8,128)(2,1)S(1)} %feature_part.3.refs_0_), channel_id=1, source_target_pairs={{0,2},{1,3},{2,0},{3,1},{4,6},{5,7},{6,4},{7,5},{8,10},{9,11},{10,... | collective-permute-start | bytes 245768 | tf_op jit(solution)/shard_map/ppermute | solution.py:30
  59.0 3.2 %hold.3.refs_5_.other_ref = bf16[512,7168]{1,0:T(8,128)(2,1)S(1)} custom-call(bf16[512,7168]{1,0:T(8,128)(2,1)} %copy-done.1), custom_call_target="tpu_custom_call" | custom-call | bytes 14680064 | tf_op jit(solution)/shard_map/hold/pallas_call | solution.py:97
  62.2 3.2 %token_part.4 = bf16[40,7168]{1,0:T(8,128)(2,1)S(1)} custom-call(s32[4]{0:T(128)S(1)} %pad_add_fusion.place_ref, bf16[40,1024]{1,0:T(8,128)(2,1)S(1)} %feature_part.3.refs_0_, bf16[40,1024]{1,0:T(8,128)(2,1)S(1)} %collective-permute-done.7.refs_1_, bf16[40,1024]{1,0:T(8,128)(2,1)S(1)} %collective-permute-done.8.refs_2_, ...), custom_call_target="tpu_custom_call" | custom-call | flops 587202560 | bytes 14680064 | tf_op jit(solution)/shard_map/token_part/pallas_call | solution.py:183
  65.4 16.4 %all_to_all.37 = bf16[32,9,8,128]{3,2,1,0:T(8,128)(2,1)S(1)} all-to-all(bf16[32,9,8,128]{3,2,1,0:T(8,128)(2,1)S(1)} %bitcast.65), channel_id=1, replica_groups=mesh['z'=8,'x'=4,'c'=2,'y'=4] {'x','z'}, dimensions={0} | all-to-all | bytes 1179648 | tf_op jit(solution)/shard_map/all_to_all | solution.py:53
  82.0 18.8 %all_to_all.38 = bf16[32,9,8,128]{3,2,1,0:T(8,128)(2,1)S(1)} all-to-all(bf16[32,9,8,128]{3,2,1,0:T(8,128)(2,1)S(1)} %broadcast_in_dim.39), channel_id=1, replica_groups=mesh['z'=8,'x'=4,'c'=2,'y'=4] {'x','z'}, dimensions={0} | all-to-all | bytes 1179648 | tf_op jit(solution)/shard_map/all_to_all | solution.py:53
  100.9 4.5 %feature_part.4.refs_0_ = bf16[40,1024]{1,0:T(8,128)(2,1)S(1)} custom-call(bf16[40,7168]{1,0:T(8,128)(2,1)S(1)} %bitcast.56, bf16[512,7168]{1,0:T(8,128)(2,1)S(1)} %get-tuple-element.24.refs_4_.own_ref, bf16[512,7168]{1,0:T(8,128)(2,1)S(1)} %hold.3.refs_5_.other_ref), custom_call_target="tpu_custom_call" | custom-call | flops 587202560 | bytes 14680064 | tf_op jit(solution)/shard_map/feature_part/pallas_call | solution.py:206
  106.0 2.6 %collective-permute-start.11 = (bf16[40,1024]{1,0:T(8,128)(2,1)S(1)}, bf16[40,1024]{1,0:T(8,128)(2,1)S(1)}, u32[]{:S(2)}, u32[]{:S(2)}) collective-permute-start(bf16[40,1024]{1,0:T(8,128)(2,1)S(1)} %feature_part.4.refs_0_), channel_id=1, source_target_pairs={{0,2},{1,3},{2,0},{3,1},{4,6},{5,7},{6,4},{7,5},{8,10},{9,11},{10,... | collective-permute-start | bytes 245768 | tf_op jit(solution)/shard_map/ppermute | solution.py:30
  113.3 15.6 %all_to_all.39 = bf16[32,3,8,128]{3,2,1,0:T(8,128)(2,1)S(1)} all-to-all(bf16[32,3,8,128]{3,2,1,0:T(8,128)(2,1)S(1)} %bitcast.68), channel_id=1, replica_groups=mesh['z'=8,'x'=4,'c'=2,'y'=4] {'z','x'}, dimensions={0} | all-to-all | bytes 393216 | tf_op jit(solution)/shard_map/all_to_all | solution.py:53
  129.0 13.1 %all_to_all.40 = bf16[32,3,8,128]{3,2,1,0:T(8,128)(2,1)S(1)} all-to-all(bf16[32,3,8,128]{3,2,1,0:T(8,128)(2,1)S(1)} %broadcast_in_dim.40), channel_id=1, replica_groups=mesh['z'=8,'x'=4,'c'=2,'y'=4] {'z','x'}, dimensions={0} | all-to-all | bytes 393216 | tf_op jit(solution)/shard_map/all_to_all | solution.py:53
  142.1 10.7 %collective-permute-start.13 = (bf16[40,2048]{1,0:T(8,128)(2,1)S(1)}, bf16[40,2048]{1,0:T(8,128)(2,1)S(1)}, u32[]{:S(2)}, u32[]{:S(2)}) collective-permute-start(bf16[40,2048]{1,0:T(8,128)(2,1)S(1)} %bitcast.57), channel_id=1, source_target_pairs={{0,4},{4,0},{1,5},{5,1},{2,6},{6,2},{3,7},{7,3},{8,12},{12,8},{9,1... | collective-permute-start | bytes 491528 | tf_op jit(solution)/shard_map/ppermute | solution.py:30
  155.4 2.7 %collective-permute-start.15 = (bf16[40,1280]{1,0:T(8,128)(2,1)S(1)}, bf16[40,1280]{1,0:T(8,128)(2,1)S(1)}, u32[]{:S(2)}, u32[]{:S(2)}) collective-permute-start(bf16[40,1280]{1,0:T(8,128)(2,1)S(1)} %fusion.5.refs_0_), channel_id=1, source_target_pairs={{0,2},{1,3},{2,0},{3,1},{4,6},{5,7},{6,4},{7,5},{8,10},{9,11},{10,... | collective-permute-start | bytes 307208 | tf_op jit(solution)/shard_map/ppermute | solution.py:30
  158.1 2.3 %collective-permute-done.16.refs_3_ = bf16[40,1280]{1,0:T(8,128)(2,1)S(1)} collective-permute-done((bf16[40,1280]{1,0:T(8,128)(2,1)S(1)}, bf16[40,1280]{1,0:T(8,128)(2,1)S(1)}, u32[]{:S(2)}, u32[]{:S(2)}) %collective-permute-start.16) | collective-permute-done | bytes 102432 | tf_op jit(solution)/shard_map/ppermute | solution.py:30
  160.4 2.9 %collective-permute-done.15.refs_2_ = bf16[40,1280]{1,0:T(8,128)(2,1)S(1)} collective-permute-done((bf16[40,1280]{1,0:T(8,128)(2,1)S(1)}, bf16[40,1280]{1,0:T(8,128)(2,1)S(1)}, u32[]{:S(2)}, u32[]{:S(2)}) %collective-permute-start.15) | collective-permute-done | bytes 102432 | tf_op jit(solution)/shard_map/ppermute | solution.py:30
  163.4 3.9 %up_part.1 = (bf16[32,9,8,128]{3,2,1,0:T(8,128)(2,1)}, f32[40,128]{1,0:T(8,128)S(1)}) custom-call(s32[4]{0:T(128)S(1)} %pad_add_fusion.place_ref, bf16[40,1280]{1,0:T(8,128)(2,1)S(1)} %fusion.5.refs_0_, bf16[40,1280]{1,0:T(8,128)(2,1)S(1)} %collective-permute-done.14.refs_1_, bf16[40,1280]{1,0:T(8,128)(2,1)S(1)} %collective-permute-done.15.refs_2_, ...), custom_call_target="tpu_custom_call" | custom-call | flops 587202560 | bytes 14680064 | tf_op jit(solution)/shard_map/up_part/pallas_call | solution.py:252
  168.0 3.9 %all-to-all-start.6 = ((bf16[32,9,8,128]{3,2,1,0:T(8,128)(2,1)}), bf16[32,9,8,128]{3,2,1,0:T(8,128)(2,1)S(1)}, u32[]{:S(2)}, u32[]{:S(2)}) async-start(bf16[32,9,8,128]{3,2,1,0:T(8,128)(2,1)} %get-tuple-element.29), calls=%async_computation.6 | async-start | bytes 1179648 | tf_op jit(solution)/shard_map/all_to_all | solution.py:53
  172.9 7.3 %cholesky.17 = f32[80,80]{1,0:T(8,128)S(1)} custom-call(f32[80,80]{1,0:T(8,128)S(1)} %fusion.9), custom_call_target="Cholesky" | custom-call | tf_op jit(solution)/shard_map/jit(cholesky)/cholesky | solution.py:378
  181.5 6.1 %custom-call.6 = f32[1,80,80]{1,2,0:T(8,128)S(1)} custom-call(f32[1,80,80]{2,1,0:T(8,128)S(1)} %fusion.6), custom_call_target="InvertDiagBlocksLowerTriangular" | custom-call | tf_op jit(solution)/shard_map/triangular_solve | solution.py:379
  188.7 2.9 %collective-permute-start.17 = (f32[40,128]{1,0:T(8,128)S(1)}, f32[40,128]{1,0:T(8,128)S(1)}, u32[]{:S(2)}, u32[]{:S(2)}) collective-permute-start(f32[40,128]{1,0:T(8,128)S(1)} %get-tuple-element.31), channel_id=1, source_target_pairs={{0,4},{4,0},{1,5},{5,1},{2,6},{6,2},{3,7},{7,3},{8,12},{12,8},{9,1... | collective-permute-start | bytes 61448 | tf_op jit(solution)/shard_map/ppermute | solution.py:30
  (81 shorter events, 23.4 us)
Async XLA Ops:
  0.6 9.6 %collective-permute-start.1 = (bf16[512,2048]{1,0:T(8,128)(2,1)}, bf16[512,2048]{1,0:T(8,128)(2,1)S(1)}, u32[]{:S(2)}, u32[]{:S(2)}) collective-permute-start(bf16[512,2048]{1,0:T(8,128)(2,1)} %own_ref.3), channel_id=1, source_target_pairs={{0,4},{4,0},{1,5},{5,1},{2,6},{6,2},{3,7},{7,3},{8,12},{12,8},{9,1... | collective-permute-start | bytes 6291464 | tf_op jit(solution)/shard_map/ppermute | solution.py:30
  4.0 6.2 %copy-start.2 = (bf16[512,7168]{1,0:T(8,128)(2,1)S(1)}, bf16[512,7168]{1,0:T(8,128)(2,1)}, u32[]{:S(2)}) copy-start(bf16[512,7168]{1,0:T(8,128)(2,1)} %grads_ref.1) | copy-start | bytes 22020100
  8.9 1.3 collective-permute-start.2
  10.3 5.5 %copy-start.3 = (bf16[512,2048]{1,0:T(8,128)(2,1)}, bf16[512,2048]{1,0:T(8,128)(2,1)S(1)}, u32[]{:S(2)}) copy-start(bf16[512,2048]{1,0:T(8,128)(2,1)S(1)} %collective-permute-done.1.given_ref) | copy-start | bytes 6291460
  10.3 45.2 %collective-permute-start.3 = (bf16[512,7168]{1,0:T(8,128)(2,1)S(1)}, bf16[512,7168]{1,0:T(8,128)(2,1)S(1)}, u32[]{:S(2)}, u32[]{:S(2)}) collective-permute-start(bf16[512,7168]{1,0:T(8,128)(2,1)S(1)} %copy-done.2), channel_id=1, source_target_pairs={{0,4},{4,0},{1,5},{5,1},{2,6},{6,2},{3,7},{7,3},{8,12},{12,8},{9,1... | collective-permute-start | bytes 22020104 | tf_op jit(solution)/shard_map/ppermute | solution.py:30
  10.5 4.5 %collective-permute-start = (s32[1]{0:T(128)}, s32[1]{0:T(128)}, u32[]{:S(2)}, u32[]{:S(2)}) collective-permute-start(s32[1]{0:T(128)} %param.7), channel_id=1, source_target_pairs={{0,4},{4,0},{1,5},{5,1},{2,6},{6,2},{3,7},{7,3},{8,12},{12,8},{9,1... | collective-permute-start | bytes 20 | tf_op jit(solution)/shard_map/ppermute | solution.py:30
  11.6 5.9 %collective-permute-start.6 = (bf16[40,1024]{1,0:T(8,128)(2,1)S(1)}, bf16[40,1024]{1,0:T(8,128)(2,1)S(1)}, u32[]{:S(2)}, u32[]{:S(2)}) collective-permute-start(bf16[40,1024]{1,0:T(8,128)(2,1)S(1)} %pad_maximum_fusion.2.refs_0_), channel_id=1, source_target_pairs={{0,1},{1,2},{2,3},{3,0},{4,5},{5,6},{6,7},{7,4},{8,9},{9,10},{10,1... | collective-permute-start | bytes 245768 | tf_op jit(solution)/shard_map/ppermute | solution.py:30
  11.7 6.4 %collective-permute-start.5 = (bf16[40,1024]{1,0:T(8,128)(2,1)S(1)}, bf16[40,1024]{1,0:T(8,128)(2,1)S(1)}, u32[]{:S(2)}, u32[]{:S(2)}) collective-permute-start(bf16[40,1024]{1,0:T(8,128)(2,1)S(1)} %pad_maximum_fusion.2.refs_0_), channel_id=1, source_target_pairs={{0,2},{1,3},{2,0},{3,1},{4,6},{5,7},{6,4},{7,5},{8,10},{9,11},{10,... | collective-permute-start | bytes 245768 | tf_op jit(solution)/shard_map/ppermute | solution.py:30
  13.8 4.9 %collective-permute-start.4 = (bf16[40,1024]{1,0:T(8,128)(2,1)S(1)}, bf16[40,1024]{1,0:T(8,128)(2,1)S(1)}, u32[]{:S(2)}, u32[]{:S(2)}) collective-permute-start(bf16[40,1024]{1,0:T(8,128)(2,1)S(1)} %pad_maximum_fusion.2.refs_0_), channel_id=1, source_target_pairs={{0,3},{1,0},{2,1},{3,2},{4,7},{5,4},{6,5},{7,6},{8,11},{9,8},{10,9... | collective-permute-start | bytes 245768 | tf_op jit(solution)/shard_map/ppermute | solution.py:30
  15.8 3.0 %copy-start = (bf16[512,2048]{1,0:T(8,128)(2,1)S(1)}, bf16[512,2048]{1,0:T(8,128)(2,1)}, u32[]{:S(2)}) copy-start(bf16[512,2048]{1,0:T(8,128)(2,1)} %own_ref.3) | copy-start | bytes 6291460
  55.5 3.5 %copy-start.1 = (bf16[512,7168]{1,0:T(8,128)(2,1)}, bf16[512,7168]{1,0:T(8,128)(2,1)S(1)}, u32[]{:S(2)}) copy-start(bf16[512,7168]{1,0:T(8,128)(2,1)S(1)} %collective-permute-done.3.given_ref) | copy-start | bytes 22020100
  55.5 6.6 %collective-permute-start.9 = (bf16[40,1024]{1,0:T(8,128)(2,1)S(1)}, bf16[40,1024]{1,0:T(8,128)(2,1)S(1)}, u32[]{:S(2)}, u32[]{:S(2)}) collective-permute-start(bf16[40,1024]{1,0:T(8,128)(2,1)S(1)} %feature_part.3.refs_0_), channel_id=1, source_target_pairs={{0,1},{1,2},{2,3},{3,0},{4,5},{5,6},{6,7},{7,4},{8,9},{9,10},{10,1... | collective-permute-start | bytes 245768 | tf_op jit(solution)/shard_map/ppermute | solution.py:30
  55.6 6.6 %collective-permute-start.8 = (bf16[40,1024]{1,0:T(8,128)(2,1)S(1)}, bf16[40,1024]{1,0:T(8,128)(2,1)S(1)}, u32[]{:S(2)}, u32[]{:S(2)}) collective-permute-start(bf16[40,1024]{1,0:T(8,128)(2,1)S(1)} %feature_part.3.refs_0_), channel_id=1, source_target_pairs={{0,2},{1,3},{2,0},{3,1},{4,6},{5,7},{6,4},{7,5},{8,10},{9,11},{10,... | collective-permute-start | bytes 245768 | tf_op jit(solution)/shard_map/ppermute | solution.py:30
  57.6 4.6 %collective-permute-start.7 = (bf16[40,1024]{1,0:T(8,128)(2,1)S(1)}, bf16[40,1024]{1,0:T(8,128)(2,1)S(1)}, u32[]{:S(2)}, u32[]{:S(2)}) collective-permute-start(bf16[40,1024]{1,0:T(8,128)(2,1)S(1)} %feature_part.3.refs_0_), channel_id=1, source_target_pairs={{0,3},{1,0},{2,1},{3,2},{4,7},{5,4},{6,5},{7,6},{8,11},{9,8},{10,9... | collective-permute-start | bytes 245768 | tf_op jit(solution)/shard_map/ppermute | solution.py:30
  105.4 4.6 %collective-permute-start.12 = (bf16[40,1024]{1,0:T(8,128)(2,1)S(1)}, bf16[40,1024]{1,0:T(8,128)(2,1)S(1)}, u32[]{:S(2)}, u32[]{:S(2)}) collective-permute-start(bf16[40,1024]{1,0:T(8,128)(2,1)S(1)} %feature_part.4.refs_0_), channel_id=1, source_target_pairs={{0,1},{1,2},{2,3},{3,0},{4,5},{5,6},{6,7},{7,4},{8,9},{9,10},{10,1... | collective-permute-start | bytes 245768 | tf_op jit(solution)/shard_map/ppermute | solution.py:30
  106.0 5.4 %collective-permute-start.11 = (bf16[40,1024]{1,0:T(8,128)(2,1)S(1)}, bf16[40,1024]{1,0:T(8,128)(2,1)S(1)}, u32[]{:S(2)}, u32[]{:S(2)}) collective-permute-start(bf16[40,1024]{1,0:T(8,128)(2,1)S(1)} %feature_part.4.refs_0_), channel_id=1, source_target_pairs={{0,2},{1,3},{2,0},{3,1},{4,6},{5,7},{6,4},{7,5},{8,10},{9,11},{10,... | collective-permute-start | bytes 245768 | tf_op jit(solution)/shard_map/ppermute | solution.py:30
  108.6 3.3 %collective-permute-start.10 = (bf16[40,1024]{1,0:T(8,128)(2,1)S(1)}, bf16[40,1024]{1,0:T(8,128)(2,1)S(1)}, u32[]{:S(2)}, u32[]{:S(2)}) collective-permute-start(bf16[40,1024]{1,0:T(8,128)(2,1)S(1)} %feature_part.4.refs_0_), channel_id=1, source_target_pairs={{0,3},{1,0},{2,1},{3,2},{4,7},{5,4},{6,5},{7,6},{8,11},{9,8},{10,9... | collective-permute-start | bytes 245768 | tf_op jit(solution)/shard_map/ppermute | solution.py:30
  142.1 12.0 %collective-permute-start.13 = (bf16[40,2048]{1,0:T(8,128)(2,1)S(1)}, bf16[40,2048]{1,0:T(8,128)(2,1)S(1)}, u32[]{:S(2)}, u32[]{:S(2)}) collective-permute-start(bf16[40,2048]{1,0:T(8,128)(2,1)S(1)} %bitcast.57), channel_id=1, source_target_pairs={{0,4},{4,0},{1,5},{5,1},{2,6},{6,2},{3,7},{7,3},{8,12},{12,8},{9,1... | collective-permute-start | bytes 491528 | tf_op jit(solution)/shard_map/ppermute | solution.py:30
  154.6 5.8 %collective-permute-start.16 = (bf16[40,1280]{1,0:T(8,128)(2,1)S(1)}, bf16[40,1280]{1,0:T(8,128)(2,1)S(1)}, u32[]{:S(2)}, u32[]{:S(2)}) collective-permute-start(bf16[40,1280]{1,0:T(8,128)(2,1)S(1)} %fusion.5.refs_0_), channel_id=1, source_target_pairs={{0,1},{1,2},{2,3},{3,0},{4,5},{5,6},{6,7},{7,4},{8,9},{9,10},{10,1... | collective-permute-start | bytes 307208 | tf_op jit(solution)/shard_map/ppermute | solution.py:30
  155.4 7.9 %collective-permute-start.15 = (bf16[40,1280]{1,0:T(8,128)(2,1)S(1)}, bf16[40,1280]{1,0:T(8,128)(2,1)S(1)}, u32[]{:S(2)}, u32[]{:S(2)}) collective-permute-start(bf16[40,1280]{1,0:T(8,128)(2,1)S(1)} %fusion.5.refs_0_), channel_id=1, source_target_pairs={{0,2},{1,3},{2,0},{3,1},{4,6},{5,7},{6,4},{7,5},{8,10},{9,11},{10,... | collective-permute-start | bytes 307208 | tf_op jit(solution)/shard_map/ppermute | solution.py:30
  158.1 5.2 %collective-permute-start.14 = (bf16[40,1280]{1,0:T(8,128)(2,1)S(1)}, bf16[40,1280]{1,0:T(8,128)(2,1)S(1)}, u32[]{:S(2)}, u32[]{:S(2)}) collective-permute-start(bf16[40,1280]{1,0:T(8,128)(2,1)S(1)} %fusion.5.refs_0_), channel_id=1, source_target_pairs={{0,3},{1,0},{2,1},{3,2},{4,7},{5,4},{6,5},{7,6},{8,11},{9,8},{10,9... | collective-permute-start | bytes 307208 | tf_op jit(solution)/shard_map/ppermute | solution.py:30
  168.0 19.9 %all-to-all-start.6 = ((bf16[32,9,8,128]{3,2,1,0:T(8,128)(2,1)}), bf16[32,9,8,128]{3,2,1,0:T(8,128)(2,1)S(1)}, u32[]{:S(2)}, u32[]{:S(2)}) async-start(bf16[32,9,8,128]{3,2,1,0:T(8,128)(2,1)} %get-tuple-element.29), calls=%async_computation.6 | async-start | bytes 1179648 | tf_op jit(solution)/shard_map/all_to_all | solution.py:53
  188.7 3.8 %collective-permute-start.17 = (f32[40,128]{1,0:T(8,128)S(1)}, f32[40,128]{1,0:T(8,128)S(1)}, u32[]{:S(2)}, u32[]{:S(2)}) collective-permute-start(f32[40,128]{1,0:T(8,128)S(1)} %get-tuple-element.31), channel_id=1, source_target_pairs={{0,4},{4,0},{1,5},{5,1},{2,6},{6,2},{3,7},{7,3},{8,12},{12,8},{9,1... | collective-permute-start | bytes 61448 | tf_op jit(solution)/shard_map/ppermute | solution.py:30
